TPU v7x, 512 devices: a whole 4x8x8 slice. The times are simulated.
512 devices in a mesh: dp: 16 (over z, core), mp: 32 (over x, y).
Axes of the slice: x: 4, y: 8, z: 8, core: 2. Of those that a mesh axis runs over, the one named last changes fastest.
Arguments:
- tokens: bfloat16 [4096, 2560], P('dp', 'mp'), may hold values from -6 to 6
- cotangent: bfloat16 [4096, 2560], P('dp', 'mp'), may hold values from -6 to 6
- in_blocks: bfloat16 [1024, 128, 128], P('mp'), may hold values from -0.25 to 0.25
- in_lists: int32 [1024, 2], P('mp'), may hold values from -1 to 19, as said below
- out_blocks: bfloat16 [1024, 128, 128], P('mp'), may hold values from -0.1875 to 0.1875
- out_lists: int32 [1024, 2], P('mp'), may hold values from -1 to 19, as said below
Outputs:
- layer_output: bfloat16 [4096, 2560], P('dp', 'mp')
- token_grad: bfloat16 [4096, 2560], P('dp', 'mp')
- in_grad: bfloat16 [1024, 128, 128], P('mp', 'dp')
- out_grad: bfloat16 [1024, 128, 128], P('mp', 'dp')
Inputs may be any that keep to these rules, and one draw needn't show every extreme that they name: `in_lists`: each owner's 32 slots list distinct blocks of its 5 block rows (row within the owner, column) in ascending order first, then (-1, -1); in each projection some owner fills all 32 slots. `out_lists`: as for in_lists, drawn independently.
All inputs are finite; a program needn't handle non-finite values.
Results may differ from a plain program's by a relative error of at most 0.023.
Values may be sent and summed in bfloat16 or wider, within the bound.
No kernel may reach another device: no remote copies, remote signals or barrier semaphores. Data moves between devices by JAX's collectives and lax.ppermute only.
A program may use at most 64 MiB of HBM per device.

v0:
```python
import math

import jax
import jax.numpy as jnp
from jax import lax
from jax.sharding import PartitionSpec as P

FF = 20480


root_coeff = math.sqrt(2.0 / math.pi)
cubic_coeff = 0.044715


def gelu_pair(pre_values):
    tanh_val = jnp.tanh(
        root_coeff * (pre_values + cubic_coeff * pre_values * pre_values * pre_values)
    )
    values = 0.5 * pre_values * (1.0 + tanh_val)
    slopes = 0.5 * (1.0 + tanh_val) + 0.5 * pre_values * (
        1.0 - tanh_val * tanh_val
    ) * root_coeff * (1.0 + 3.0 * cubic_coeff * pre_values * pre_values)
    return (values, slopes)


def tables(lists, row_count, col_count):
    row_ids = lists[:, 0]
    col_ids = lists[:, 1]
    live_mask = (row_ids >= 0).astype(jnp.float32)
    row_hot = (row_ids[:, None] == jnp.arange(row_count, dtype=jnp.int32)[None, :]).astype(
        jnp.float32
    )
    col_hot = (col_ids[:, None] == jnp.arange(col_count, dtype=jnp.int32)[None, :]).astype(
        jnp.float32
    )
    return (jnp.maximum(row_ids, 0), jnp.maximum(col_ids, 0), live_mask, row_hot, col_hot)


def body(tokens, cotangent, in_blocks, in_lists, out_blocks, out_lists):
    highest = lax.Precision.HIGHEST
    group_rows = tokens.shape[0]
    block_size = in_blocks.shape[1]
    full_width = tokens.shape[1] * lax.axis_size("mp")
    col_count = full_width // block_size
    row_count = FF // (block_size * lax.axis_size("mp"))
    grad_scale = float(group_rows * lax.axis_size("dp")) ** (-0.5)
    in_rows, in_cols, in_live, in_rhot, in_chot = tables(in_lists, row_count, col_count)
    out_rows, out_cols, out_live, out_rhot, out_chot = tables(out_lists, row_count, col_count)
    gathered = lax.all_gather(tokens, "mp", axis=1, tiled=True).reshape(
        group_rows, col_count, block_size
    )
    x_cols = jnp.take(gathered, in_cols, axis=1)
    pre_terms = jnp.einsum("tsk,sjk->tsj", x_cols, in_blocks, preferred_element_type=jnp.float32)
    hidden = jnp.einsum("tsj,sr->trj", pre_terms, in_rhot, precision=highest)
    activation, slopes = gelu_pair(hidden)
    activation = activation.astype(jnp.bfloat16)
    a_rows = jnp.take(activation, out_rows, axis=1)
    y_terms = jnp.einsum("tsj,sjk->tsk", a_rows, out_blocks, preferred_element_type=jnp.float32)
    y_part = jnp.einsum("tsk,sd->tdk", y_terms, out_chot, precision=highest).reshape(
        group_rows, full_width
    )
    layer_output = lax.psum_scatter(
        y_part.astype(jnp.bfloat16), "mp", scatter_dimension=1, tiled=True
    )
    cot_whole = lax.all_gather(cotangent, "mp", axis=1, tiled=True).reshape(
        group_rows, col_count, block_size
    )
    g_cols = jnp.take(cot_whole, out_cols, axis=1)
    back_terms = jnp.einsum("tsk,sjk->tsj", g_cols, out_blocks, preferred_element_type=jnp.float32)
    d_act = jnp.einsum("tsj,sr->trj", back_terms, out_rhot, precision=highest)
    d_hidden = (d_act * slopes).astype(jnp.bfloat16)
    out_terms = (
        jnp.einsum("tsj,tsk->sjk", a_rows, g_cols, preferred_element_type=jnp.float32)
        * out_live[:, None, None]
    )
    h_rows = jnp.take(d_hidden, in_rows, axis=1)
    dx_terms = jnp.einsum("tsj,sjk->tsk", h_rows, in_blocks, preferred_element_type=jnp.float32)
    dx_part = jnp.einsum("tsk,sd->tdk", dx_terms, in_chot, precision=highest).reshape(
        group_rows, full_width
    )
    in_terms = (
        jnp.einsum("tsj,tsk->sjk", h_rows, x_cols, preferred_element_type=jnp.float32)
        * in_live[:, None, None]
    )
    out_summed, in_summed = (
        lax.psum_scatter(
            out_terms.astype(jnp.bfloat16), "dp", scatter_dimension=1, tiled=True
        ).astype(jnp.float32),
        lax.psum_scatter(
            in_terms.astype(jnp.bfloat16), "dp", scatter_dimension=1, tiled=True
        ).astype(jnp.float32),
    )
    out_grad = (out_summed * grad_scale).astype(jnp.bfloat16)
    in_grad = (in_summed * grad_scale).astype(jnp.bfloat16)
    token_grad = lax.psum_scatter(
        dx_part.astype(jnp.bfloat16), "mp", scatter_dimension=1, tiled=True
    )
    return (layer_output, token_grad, in_grad, out_grad)


def solution(mesh):
    return jax.shard_map(
        body,
        mesh=mesh,
        in_specs=(
            P("dp", "mp"),
            P("dp", "mp"),
            P("mp", None, None),
            P("mp", None),
            P("mp", None, None),
            P("mp", None),
        ),
        out_specs=(P("dp", "mp"), P("dp", "mp"), P("mp", "dp", None), P("mp", "dp", None)),
        check_vma=False,
    )
```

profile of v0, /device:TPU:1, one launch (start us, length us, event | category | flops | bytes accessed | tf_op | source)
XLA Modules:
  0.0 779.9 jit_solution(12360293334919574698)
XLA Ops:
  13.3 80.9 %all-gather.3.cloned.1.call-done = bf16[256,2560]{0,1:T(8,128)(2,1)} async-done(((bf16[256,80]{0,1:T(8,128)(2,1)}), bf16[256,2560]{0,1:T(8,128)(2,1)}) %all-gather.3.cloned.1.call-update) | async-done | bytes 1310736 | tf_op jit(solution)/shard_map/all_gather | solution.py:49
  94.2 1.8 copy.44
  96.0 81.3 %all-gather.5.cloned.1.call-done = bf16[256,2560]{0,1:T(8,128)(2,1)} async-done(((bf16[256,80]{0,1:T(8,128)(2,1)}), bf16[256,2560]{0,1:T(8,128)(2,1)}) %all-gather.5.cloned.1.call-update) | async-done | bytes 1310736 | tf_op jit(solution)/shard_map/all_gather | solution.py:65
  177.3 2.4 copy.49
  179.7 3.5 gather_fusion.2
  183.2 2.1 gather_fusion
  185.4 2.3 convolution_bitcast_fusion.3
  187.7 3.9 fusion.6
  192.4 3.9 fusion.2
  196.8 2.1 gather_fusion.3
  198.9 3.2 multiply_convert_fusion.1
  203.0 1.4 copy.92
  204.5 2.1 gather_fusion.1
  206.7 2.6 multiply_convert_fusion
  210.0 1.4 copy.91
  212.7 5.5 fusion.35
  218.1 2.9 copy.48
  221.4 2.0 convolution_bitcast_fusion
  223.3 4.3 fusion.32
  227.6 1.7 copy.53
  229.4 35.4 %reduce-scatter.13.cloned.1.call-done = bf16[8,4096]{1,0:T(8,128)(2,1)} async-done(((bf16[128,4096]{1,0:T(8,128)(2,1)}), bf16[8,4096]{1,0:T(8,128)(2,1)}) %reduce-scatter.13.cloned.1.call-update) | async-done | bytes 65552
  265.7 60.7 %reduce-scatter.15.cloned.1.call-done = bf16[8,4096]{1,0:T(8,128)(2,1)} async-done(((bf16[128,4096]{1,0:T(8,128)(2,1)}), bf16[8,4096]{1,0:T(8,128)(2,1)}) %reduce-scatter.15.cloned.1.call-update) | async-done | bytes 65552
  328.6 219.7 %reduce-scatter.9.cloned.1.call-done = bf16[256,80]{0,1:T(8,128)(2,1)} async-done(((bf16[256,2560]{0,1:T(8,128)(2,1)}), bf16[256,80]{0,1:T(8,128)(2,1)}) %reduce-scatter.9.cloned.1.call-update) | async-done | bytes 40976 | tf_op jit(solution)/shard_map/reduce_scatter | solution.py:62
  548.3 224.8 %reduce-scatter.11.cloned.1.call-done = bf16[256,80]{0,1:T(8,128)(2,1)} async-done(((bf16[256,2560]{0,1:T(8,128)(2,1)}), bf16[256,80]{0,1:T(8,128)(2,1)}) %reduce-scatter.11.cloned.1.call-update) | async-done | bytes 40976 | tf_op jit(solution)/shard_map/reduce_scatter | solution.py:95
  (41 shorter events, 13.6 us)
Async XLA Ops:
  7.2 184.4 %copy-start = (bf16[32,128,128]{2,1,0:T(8,128)(2,1)S(1)}, bf16[32,128,128]{2,1,0:T(8,128)(2,1)}, u32[]{:S(2)}) copy-start(bf16[32,128,128]{2,1,0:T(8,128)(2,1)} %param.14) | copy-start | bytes 3145732
  7.2 87.0 %all-gather.3.cloned.1.call-start = ((), (), s32[]{:S(2)}) async-start(), calls=%async_computation.4 | async-start | bytes 1351680 | tf_op jit(solution)/shard_map/all_gather | solution.py:49
  7.9 169.4 %all-gather.5.cloned.1.call-start = ((), (), s32[]{:S(2)}) async-start(), calls=%async_computation.6 | async-start | bytes 1351680 | tf_op jit(solution)/shard_map/all_gather | solution.py:65
  8.7 256.2 %reduce-scatter.13.cloned.1.call-start = ((), (), s32[]{:S(2)}) async-start(), calls=%async_computation.8 | async-start | bytes 1114112
  183.2 2.1 copy-start.5
  187.7 3.9 copy-start.2
  204.4 122.0 %reduce-scatter.15.cloned.1.call-start = ((), (), s32[]{:S(2)}) async-start(), calls=%async_computation.9 | async-start | bytes 1114112
  204.5 2.2 copy-start.3
  210.0 2.0 copy-start.4
  211.4 336.9 %reduce-scatter.9.cloned.1.call-start = ((), (), s32[]{:S(2)}) async-start(), calls=%async_computation.5 | async-start | bytes 1351680 | tf_op jit(solution)/shard_map/reduce_scatter | solution.py:62
  218.1 3.2 copy-start.1
  221.1 552.0 %reduce-scatter.11.cloned.1.call-start = ((), (), s32[]{:S(2)}) async-start(), calls=%async_computation.7 | async-start | bytes 1351680 | tf_op jit(solution)/shard_map/reduce_scatter | solution.py:95
Sparse Core Ops, SparseCore 0:
  11.2 82.9 all-gather.2
  97.4 79.8 all-gather.4
  204.6 60.2 reduce-scatter.12
  267.7 58.6 reduce-scatter.14
  331.2 216.9 reduce-scatter.8
  553.1 219.9 reduce-scatter.10
where the time goes:
time: 784 us; the launch traced here: 780 us
  waiting for transfers between devices  704 us (90%)
  matrix products  29.1 us (4%)
  local copies, waits for them, and re-layouts  26.9 us (3%)
  between operations  14.3 us (2%)
    reduce_scatter x1, waiting for transfers between devices, body(): lax.psum_scatter(dx_part.astype(jnp.bfloat16), 'mp', scatter_dimension=1,...  225 us
    reduce_scatter x1, waiting for transfers between devices, body(): lax.psum_scatter(y_part.astype(jnp.bfloat16), 'mp', scatter_dimension=1,...  220 us
    unnamed x8, waiting for transfers between devices  97.6 us
    all_gather x1, waiting for transfers between devices, body(): lax.all_gather(cotangent, 'mp', axis=1, tiled=True)  81.3 us
    all_gather x1, waiting for transfers between devices, body(): lax.all_gather(tokens, 'mp', axis=1, tiled=True)  80.9 us
  transfers between devices with their start and end apart: 6, of which 6 were waited for; matrix products, arithmetic and copies ran while one was open for 4% of the time, Pallas kernels for 0%

commit v1 on v0

v1 whole, which is shorter than its diff:
```python
import functools
import math

import jax
import jax.numpy as jnp
from jax import lax
from jax.experimental import pallas as pl
from jax.experimental.pallas import tpu as pltpu
from jax.sharding import Mesh
from jax.sharding import PartitionSpec as P

Z, C, X, Y = 8, 2, 4, 8
BLK = 128
CAP = 32
ROWS = 5
COLS = 20
T = 256
FEAT = COLS * BLK
OWN = FEAT // (X * Y)
SUB = BLK // (Z * C)

ROOT_COEFF = math.sqrt(2.0 / math.pi)
CUBIC_COEFF = 0.044715


def gelu_pair(pre):
    tanh_val = jnp.tanh(ROOT_COEFF * (pre + CUBIC_COEFF * pre * pre * pre))
    values = 0.5 * pre * (1.0 + tanh_val)
    slopes = 0.5 * (1.0 + tanh_val) + 0.5 * pre * (1.0 - tanh_val * tanh_val) * ROOT_COEFF * (
        1.0 + 3.0 * CUBIC_COEFF * pre * pre
    )
    return values, slopes


def dot(a, b, dims):
    return lax.dot_general(a, b, (dims, ((), ())), preferred_element_type=jnp.float32)


def place(lists, s):
    row, col = lists[2 * s], lists[2 * s + 1]
    live = jnp.where(row >= 0, 1.0, 0.0).astype(jnp.float32)
    row = jnp.maximum(row, 0)
    return row, pl.multiple_of(jnp.maximum(col, 0) * BLK, BLK), live


def units_kernel(core, in_l, out_l, xg, w_in, w_out, keep, send, act, dh, hidden, d_act):
    hidden[...] = jnp.zeros_like(hidden)
    d_act[...] = jnp.zeros_like(d_act)

    def product(s, carry):
        row, col, live = place(in_l, s)
        hidden[row] += dot(w_in[s], xg[pl.ds(col, BLK), :T], ((1,), (0,))) * live
        row, col, live = place(out_l, s)
        d_act[row] += dot(w_out[s], xg[pl.ds(col, BLK), T:], ((1,), (0,))) * live
        return carry

    lax.fori_loop(0, CAP, product, 0, unroll=8)
    for row in range(ROWS):
        values, slopes = gelu_pair(hidden[row])
        act[row] = values.astype(act.dtype)
        dh[row] = (d_act[row] * slopes).astype(dh.dtype)

    first = core[0] == 0
    scale = float(T * Z * C) ** -0.5

    def pair(p, carry):
        for which, (lists, units, lo) in enumerate(((out_l, act, T), (in_l, dh, 0))):
            parts = []
            for i in range(2):
                row, col, live = place(lists, 2 * p + i)
                part = dot(units[row], xg[pl.ds(col, BLK), lo : lo + T], ((1,), (1,)))
                parts.append((part * (live * scale)).reshape(Z, C, SUB, BLK))
            both = jnp.stack(parts, axis=2).reshape(Z, C, 2 * SUB, BLK)
            at = pl.multiple_of((which * CAP + 2 * p) * SUB, 2 * SUB)
            keep[:, pl.ds(at, 2 * SUB), :] = jnp.where(first, both[:, 0], both[:, 1]).astype(
                keep.dtype
            )
            send[:, pl.ds(at, 2 * SUB), :] = jnp.where(first, both[:, 1], both[:, 0]).astype(
                send.dtype
            )
        return carry

    lax.fori_loop(0, CAP // 2, pair, 0, unroll=4)


def partials_kernel(in_l, out_l, act, dh, w_in, w_out, out, total):
    total[...] = jnp.zeros_like(total)

    def product(s, carry):
        row, col, live = place(out_l, s)
        total[pl.ds(col, BLK), :T] += dot(w_out[s], act[row], ((0,), (0,))) * live
        row, col, live = place(in_l, s)
        total[pl.ds(col, BLK), T:] += dot(w_in[s], dh[row], ((0,), (0,))) * live
        return carry

    lax.fori_loop(0, CAP, product, 0, unroll=8)
    out[...] = total[...].astype(out.dtype)


SMEM = pl.BlockSpec(memory_space=pltpu.SMEM)
VMEM = pl.BlockSpec(memory_space=pltpu.VMEM)
LIMIT = pltpu.CompilerParams(vmem_limit_bytes=48 * 1024 * 1024)


def units_call(core, in_l, out_l, xg, w_in, w_out, interpret=False):
    bf = jnp.bfloat16
    half = jax.ShapeDtypeStruct((Z, 2 * CAP * SUB, BLK), bf)
    rows = jax.ShapeDtypeStruct((ROWS, BLK, T), bf)
    return pl.pallas_call(
        units_kernel,
        out_shape=(half, half, rows, rows),
        in_specs=[SMEM] * 3 + [VMEM] * 3,
        out_specs=[VMEM] * 4,
        scratch_shapes=[pltpu.VMEM((ROWS, BLK, T), jnp.float32)] * 2,
        compiler_params=LIMIT,
        interpret=interpret,
    )(core, in_l, out_l, xg, w_in, w_out)


def partials_call(in_l, out_l, act, dh, w_in, w_out, interpret=False):
    return pl.pallas_call(
        partials_kernel,
        out_shape=jax.ShapeDtypeStruct((FEAT, 2 * T), jnp.bfloat16),
        in_specs=[SMEM] * 2 + [VMEM] * 4,
        out_specs=VMEM,
        scratch_shapes=[pltpu.VMEM((FEAT, 2 * T), jnp.float32)],
        compiler_params=LIMIT,
        interpret=interpret,
    )(in_l, out_l, act, dh, w_in, w_out)


def exchange(x, axis):
    return lax.all_to_all(x, axis, split_axis=0, concat_axis=0)


def spread(x, axis, size):
    return exchange(jnp.broadcast_to(x[None], (size,) + x.shape), axis)


def body(tokens, cotangent, in_blocks, in_lists, out_blocks, out_lists):
    bf, f32 = jnp.bfloat16, jnp.float32
    in_l, out_l = in_lists.reshape(-1), out_lists.reshape(-1)
    own = jnp.concatenate([tokens.T, cotangent.T], axis=1)
    along_y = spread(own, "y", Y).reshape(Y * OWN, 2 * T)
    xg = spread(along_y, "x", X).reshape(FEAT, 2 * T)
    core = lax.axis_index("c").astype(jnp.int32).reshape(1)
    keep, send, act, dh = units_call(core, in_l, out_l, xg, in_blocks, out_blocks)
    got = lax.ppermute(send, "c", [(0, 1), (1, 0)])
    parts = partials_call(in_l, out_l, act, dh, in_blocks, out_blocks)
    grads = (keep.astype(f32) + got.astype(f32)).astype(bf)
    grads, parts = lax.optimization_barrier((grads, parts))
    grads = lax.psum_scatter(grads, "z", scatter_dimension=0)
    parts = exchange(parts.reshape(X, Y * OWN, 2 * T), "x")
    parts = jnp.sum(parts.astype(f32), axis=0).astype(bf)
    parts = exchange(parts.reshape(Y, OWN, 2 * T), "y")
    sums = jnp.sum(parts.astype(f32), axis=0).astype(bf)
    grads = grads.reshape(2, CAP, SUB, BLK)
    return sums[:, :T].T, sums[:, T:].T, grads[1], grads[0]


def solution(mesh):
    fine = Mesh(mesh.devices.reshape(Z, C, X, Y), ("z", "c", "x", "y"))
    dp, mp = ("z", "c"), ("x", "y")
    blocks, lists = P(mp, None, None), P(mp, None)
    return jax.shard_map(
        body,
        mesh=fine,
        in_specs=(P(dp, mp), P(dp, mp), blocks, lists, blocks, lists),
        out_specs=(P(dp, mp), P(dp, mp), P(mp, dp, None), P(mp, dp, None)),
        check_vma=False,
    )
```

time: 784 us -> 157 us (0.20)
  waiting for transfers between devices: 704 us -> 80.8 us
  matrix products: 29.1 us -> 0 us
  blocking collectives: 0 us -> 25.3 us
  local copies, waits for them, and re-layouts: 26.9 us -> 4.32 us
  starting transfers between devices: 0.46 us -> 17.8 us
  Pallas kernels: 0 us -> 10.4 us
    reduce_scatter x2 -> x1, waiting for transfers between devices: 445 us -> 5.1 us  [body(): grads = lax.psum_scatter(grads, 'z', scatter_dimension=0)]
    all_gather x2 -> x0, waiting for transfers between devices: 162 us -> none  [the longest x1 81.3 us: body(): lax.all_gather(cotangent, 'mp', axis=1, tiled=True)]
    unnamed x8 -> x1, waiting for transfers between devices: 97.6 us -> 0.68 us
    all_to_all x0 -> x3, waiting for transfers between devices: none -> 75.1 us  [exchange(): return lax.all_to_all(x, axis, split_axis=0, concat_axis=0)]
    dot_general x10 -> x0, matrix products: 29.1 us -> none  [the longest x1 5.45 us: body(): jnp.einsum('tsk,sd->tdk', y_terms, out_chot, precision=highest)]
    all_to_all x0 -> x1, blocking collectives: none -> 25.3 us  [exchange(): return lax.all_to_all(x, axis, split_axis=0, concat_axis=0)]
    all_to_all x0 -> x3, starting transfers between devices: none -> 12.6 us  [exchange(): return lax.all_to_all(x, axis, split_axis=0, concat_axis=0)]
    pallas_call x0 -> x2, Pallas kernels: none -> 10.4 us  [the longest x1 5.8 us: units_call(): pl.pallas_call(units_kernel, out_shape=(half, half, rows, rows), in_specs...]
  transfers between devices with their start and end apart: 6 -> 5, of which waited for: 6 -> 4; matrix products, arithmetic and copies ran while one was open for 4% -> 2% of each run, Pallas kernels for 0% -> 3%
where the time goes in v1:
time: 157 us; the launch traced here: 156 us
  waiting for transfers between devices  80.8 us (51%)
  blocking collectives  25.3 us (16%)
  starting transfers between devices  17.8 us (11%)
  between operations  14.1 us (9%)
  Pallas kernels  10.4 us (7%)
  local copies, waits for them, and re-layouts  4.32 us (3%)
  other arithmetic  3.56 us (2%)
    all_to_all x3, waiting for transfers between devices, exchange(): return lax.all_to_all(x, axis, split_axis=0, concat_axis=0)  75.1 us
    all_to_all x1, blocking collectives, exchange(): return lax.all_to_all(x, axis, split_axis=0, concat_axis=0)  25.3 us
    all_to_all x3, starting transfers between devices, exchange(): return lax.all_to_all(x, axis, split_axis=0, concat_axis=0)  12.6 us
    pallas_call x1, Pallas kernels, units_call(): pl.pallas_call(units_kernel, out_shape=(half, half, rows, rows), in_specs...  5.8 us
    ppermute x1, starting transfers between devices, body(): got = lax.ppermute(send, 'c', [(0, 1), (1, 0)])  5.14 us
    reduce_scatter x1, waiting for transfers between devices, body(): grads = lax.psum_scatter(grads, 'z', scatter_dimension=0)  5.1 us
    pallas_call x1, Pallas kernels, partials_call(): pl.pallas_call(partials_kernel, out_shape=jax.ShapeDtypeStruct((FEAT, 2 *...  4.56 us
  transfers between devices with their start and end apart: 5, of which 4 were waited for; matrix products, arithmetic and copies ran while one was open for 2% of the time, Pallas kernels for 3%

profile of v1, /device:TPU:1, one launch (start us, length us, event | category | flops | bytes accessed | tf_op | source)
XLA Modules:
  0.0 156.3 jit_solution(8005582788771870734)
XLA Ops:
  7.2 0.8 pad_maximum_fusion
  8.0 25.3 %all_to_all.20 = bf16[8,80,512]{2,1,0:T(8,128)(2,1)S(1)} all-to-all(bf16[8,80,512]{2,1,0:T(8,128)(2,1)S(1)} %broadcast_in_dim.6), channel_id=1, replica_groups=mesh['z'=8,'c'=2,'x'=4,'y'=8] {'y'}, dimensions={0} | all-to-all | bytes 1310720 | tf_op jit(solution)/shard_map/all_to_all | solution.py:133
  33.4 1.7 %broadcast_in_dim.15 = bf16[4,640,512]{2,1,0:T(8,128)(2,1)} broadcast(bf16[640,512]{1,0:T(8,128)(2,1)S(1)} %bitcast.15), dimensions={1,2} | broadcast | bytes 3276800 | tf_op jit(solution)/shard_map/broadcast_in_dim | solution.py:137
  35.1 5.4 %all-to-all-start.1 = ((bf16[4,640,512]{2,1,0:T(8,128)(2,1)}), bf16[4,640,512]{2,1,0:T(8,128)(2,1)}, u32[]{:S(2)}, u32[]{:S(2)}) async-start(bf16[4,640,512]{2,1,0:T(8,128)(2,1)} %broadcast_in_dim.15), calls=%async_computation.1 | async-start | bytes 5242880 | tf_op jit(solution)/shard_map/all_to_all | solution.py:133
  40.5 0.1 copy.14
  40.6 0.1 reshape.33.in_l
  40.7 0.1 copy.15
  40.8 0.1 reshape.34.out_l
  40.9 29.7 %all-to-all-done.1 = bf16[4,640,512]{2,1,0:T(8,128)(2,1)} async-done(((bf16[4,640,512]{2,1,0:T(8,128)(2,1)}), bf16[4,640,512]{2,1,0:T(8,128)(2,1)}, u32[]{:S(2)}, u32[]{:S(2)}) %all-to-all-start.1) | async-done | bytes 2621472 | tf_op jit(solution)/shard_map/all_to_all | solution.py:133
  70.6 5.8 %shard_map.93 = (bf16[8,512,128]{2,1,0:T(8,128)(2,1)S(1)}, bf16[8,512,128]{2,1,0:T(8,128)(2,1)S(1)}, bf16[5,128,256]{2,1,0:T(8,128)(2,1)S(1)}, bf16[5,128,256]{2,1,0:T(8,128)(2,1)S(1)}) custom-call(s32[1]{0:T(128)} %bitcast.core, s32[64]{0:T(128)S(1)} %reshape.33.in_l, s32[64]{0:T(128)S(1)} %reshape.34.out_l, bf16[2560,512]{1,0:T(8,128)(2,1)} %bitcast.4.xg, ...), custom_call_target="tpu_custom_call" | custom-call | tf_op jit(solution)/shard_map/pallas_call | solution.py:109
  76.4 5.1 %collective-permute-start = (bf16[8,512,128]{2,1,0:T(8,128)(2,1)S(1)}, bf16[8,512,128]{2,1,0:T(8,128)(2,1)S(1)}, u32[]{:S(2)}, u32[]{:S(2)}) collective-permute-start(bf16[8,512,128]{2,1,0:T(8,128)(2,1)S(1)} %get-tuple-element.11), channel_id=1, source_target_pairs={{0,32},{32,0},{1,33},{33,1},{2,34},{34,2},{3,35},{35,3},{4,36},{36... | collective-permute-start | bytes 3145736 | tf_op jit(solution)/shard_map/ppermute | solution.py:148
  81.5 4.6 %shard_map.94 = bf16[2560,512]{1,0:T(8,128)(2,1)} custom-call(s32[64]{0:T(128)S(1)} %reshape.33.in_l, s32[64]{0:T(128)S(1)} %reshape.34.out_l, bf16[5,128,256]{2,1,0:T(8,128)(2,1)S(1)} %get-tuple-element.12.act, bf16[5,128,256]{2,1,0:T(8,128)(2,1)S(1)} %get-tuple-element.13.dh, bf16[32,128,128]{2,1,0:T(8,128)(2,1)S(1)} %copy-done, ...), custom_call_target="tpu_custom_call" | custom-call | tf_op jit(solution)/shard_map/pallas_call | solution.py:121
  86.1 1.2 add_convert_fusion
  87.3 3.7 %all-to-all-start.2 = ((bf16[4,640,512]{2,1,0:T(8,128)(2,1)}), bf16[4,640,512]{2,1,0:T(8,128)(2,1)S(1)}, u32[]{:S(2)}, u32[]{:S(2)}) async-start(bf16[4,640,512]{2,1,0:T(8,128)(2,1)} %bitcast.5), calls=%async_computation.2 | async-start | bytes 5242880 | tf_op jit(solution)/shard_map/all_to_all | solution.py:133
  91.0 0.0 reduce-scatter.2.cloned.1.call-start
  91.1 0.7 reduce-scatter.2.cloned.1.call-update
  91.7 31.3 %all-to-all-done.2 = bf16[4,640,512]{2,1,0:T(8,128)(2,1)S(1)} async-done(((bf16[4,640,512]{2,1,0:T(8,128)(2,1)}), bf16[4,640,512]{2,1,0:T(8,128)(2,1)S(1)}, u32[]{:S(2)}, u32[]{:S(2)}) %all-to-all-start.2) | async-done | bytes 2621472 | tf_op jit(solution)/shard_map/all_to_all | solution.py:133
  123.1 1.4 reduce_sum.24
  124.5 3.5 %all-to-all-start.3 = ((bf16[8,80,512]{2,1,0:T(8,128)(2,1)}), bf16[8,80,512]{2,1,0:T(8,128)(2,1)S(1)}, u32[]{:S(2)}, u32[]{:S(2)}) async-start(bf16[8,80,512]{2,1,0:T(8,128)(2,1)} %bitcast.6), calls=%async_computation.3 | async-start | bytes 1310720 | tf_op jit(solution)/shard_map/all_to_all | solution.py:133
  128.0 5.1 %reduce-scatter.2.cloned.1.call-done = bf16[1,512,128]{2,1,0:T(8,128)(2,1)} async-done(((bf16[8,512,128]{2,1,0:T(8,128)(2,1)}), bf16[1,512,128]{2,1,0:T(8,128)(2,1)}) %reduce-scatter.2.cloned.1.call-update) | async-done | bytes 131088 | tf_op jit(solution)/shard_map/reduce_scatter | solution.py:152
  133.1 1.5 slice_bitcast_fusion
  134.7 14.0 %all-to-all-done.3 = bf16[8,80,512]{2,1,0:T(8,128)(2,1)S(1)} async-done(((bf16[8,80,512]{2,1,0:T(8,128)(2,1)}), bf16[8,80,512]{2,1,0:T(8,128)(2,1)S(1)}, u32[]{:S(2)}, u32[]{:S(2)}) %all-to-all-start.3) | async-done | bytes 655392 | tf_op jit(solution)/shard_map/all_to_all | solution.py:133
  148.7 0.1 reduce_sum.25
  148.8 0.6 slice_bitcast_fusion.2
  (10 shorter events, 0.1 us)
Async XLA Ops:
  35.1 5.4 %copy-start.2 = (s32[32,2]{0,1:T(2,128)S(1)}, s32[32,2]{0,1:T(2,128)}, u32[]{:S(2)}) copy-start(s32[32,2]{0,1:T(2,128)} %param.9) | copy-start | bytes 772
  35.1 5.6 %copy-start.3 = (s32[32,2]{0,1:T(2,128)S(1)}, s32[32,2]{0,1:T(2,128)}, u32[]{:S(2)}) copy-start(s32[32,2]{0,1:T(2,128)} %param.11) | copy-start | bytes 772
  35.1 35.5 %copy-start = (bf16[32,128,128]{2,1,0:T(8,128)(2,1)S(1)}, bf16[32,128,128]{2,1,0:T(8,128)(2,1)}, u32[]{:S(2)}) copy-start(bf16[32,128,128]{2,1,0:T(8,128)(2,1)} %w_in.3) | copy-start | bytes 3145732
  35.1 35.5 %copy-start.1 = (bf16[32,128,128]{2,1,0:T(8,128)(2,1)S(1)}, bf16[32,128,128]{2,1,0:T(8,128)(2,1)}, u32[]{:S(2)}) copy-start(bf16[32,128,128]{2,1,0:T(8,128)(2,1)} %w_out.3) | copy-start | bytes 3145732
  35.1 35.5 %all-to-all-start.1 = ((bf16[4,640,512]{2,1,0:T(8,128)(2,1)}), bf16[4,640,512]{2,1,0:T(8,128)(2,1)}, u32[]{:S(2)}, u32[]{:S(2)}) async-start(bf16[4,640,512]{2,1,0:T(8,128)(2,1)} %broadcast_in_dim.15), calls=%async_computation.1 | async-start | bytes 5242880 | tf_op jit(solution)/shard_map/all_to_all | solution.py:133
  76.4 9.7 %collective-permute-start = (bf16[8,512,128]{2,1,0:T(8,128)(2,1)S(1)}, bf16[8,512,128]{2,1,0:T(8,128)(2,1)S(1)}, u32[]{:S(2)}, u32[]{:S(2)}) collective-permute-start(bf16[8,512,128]{2,1,0:T(8,128)(2,1)S(1)} %get-tuple-element.11), channel_id=1, source_target_pairs={{0,32},{32,0},{1,33},{33,1},{2,34},{34,2},{3,35},{35,3},{4,36},{36... | collective-permute-start | bytes 3145736 | tf_op jit(solution)/shard_map/ppermute | solution.py:148
  87.3 35.7 %all-to-all-start.2 = ((bf16[4,640,512]{2,1,0:T(8,128)(2,1)}), bf16[4,640,512]{2,1,0:T(8,128)(2,1)S(1)}, u32[]{:S(2)}, u32[]{:S(2)}) async-start(bf16[4,640,512]{2,1,0:T(8,128)(2,1)} %bitcast.5), calls=%async_computation.2 | async-start | bytes 5242880 | tf_op jit(solution)/shard_map/all_to_all | solution.py:133
  91.0 42.1 %reduce-scatter.2.cloned.1.call-start = ((), (), s32[]{:S(2)}) async-start(), calls=%async_computation.5 | async-start | bytes 1179648 | tf_op jit(solution)/shard_map/reduce_scatter | solution.py:152
  124.5 24.2 %all-to-all-start.3 = ((bf16[8,80,512]{2,1,0:T(8,128)(2,1)}), bf16[8,80,512]{2,1,0:T(8,128)(2,1)S(1)}, u32[]{:S(2)}, u32[]{:S(2)}) async-start(bf16[8,80,512]{2,1,0:T(8,128)(2,1)} %bitcast.6), calls=%async_computation.3 | async-start | bytes 1310720 | tf_op jit(solution)/shard_map/all_to_all | solution.py:133
Sparse Core Ops, SparseCore 0:
  94.7 38.4 reduce-scatter.1

commit v2 on v1

v2 whole, which is shorter than its diff:
```python
import functools
import math

import jax
import jax.numpy as jnp
from jax import lax
from jax.experimental import pallas as pl
from jax.experimental.pallas import tpu as pltpu
from jax.sharding import Mesh
from jax.sharding import PartitionSpec as P

Z, C, X, Y = 8, 2, 4, 8
BLK = 128
CAP = 32
ROWS = 5
COLS = 20
T = 256
FEAT = COLS * BLK
OWN = FEAT // (X * Y)
SUB = BLK // (Z * C)

ROOT_COEFF = math.sqrt(2.0 / math.pi)
CUBIC_COEFF = 0.044715


def gelu_pair(pre):
    tanh_val = jnp.tanh(ROOT_COEFF * (pre + CUBIC_COEFF * pre * pre * pre))
    values = 0.5 * pre * (1.0 + tanh_val)
    slopes = 0.5 * (1.0 + tanh_val) + 0.5 * pre * (1.0 - tanh_val * tanh_val) * ROOT_COEFF * (
        1.0 + 3.0 * CUBIC_COEFF * pre * pre
    )
    return values, slopes


def dot(a, b, dims):
    return lax.dot_general(a, b, (dims, ((), ())), preferred_element_type=jnp.float32)


def place(lists, s):
    row, col = lists[2 * s], lists[2 * s + 1]
    live = jnp.where(row >= 0, 1.0, 0.0).astype(jnp.float32)
    row = jnp.maximum(row, 0)
    return row, pl.multiple_of(jnp.maximum(col, 0) * BLK, BLK), live


def forward_kernel(in_l, out_l, x, w_in, w_out, act, slope, part, hidden, total):
    hidden[...] = jnp.zeros_like(hidden)
    total[...] = jnp.zeros_like(total)

    def up(s, carry):
        row, col, live = place(in_l, s)
        hidden[row] += dot(w_in[s], x[pl.ds(col, BLK), :], ((1,), (0,))) * live
        return carry

    def down(s, carry):
        row, col, live = place(out_l, s)
        total[pl.ds(col, BLK), :] += dot(w_out[s], act[row], ((0,), (0,))) * live
        return carry

    lax.fori_loop(0, CAP, up, 0, unroll=8)
    for row in range(ROWS):
        values, slopes = gelu_pair(hidden[row])
        act[row] = values.astype(act.dtype)
        slope[row] = slopes
    lax.fori_loop(0, CAP, down, 0, unroll=8)
    part[...] = total[...].astype(part.dtype)


def backward_kernel(in_l, out_l, g, slope, w_in, w_out, dh, part, d_act, total):
    d_act[...] = jnp.zeros_like(d_act)
    total[...] = jnp.zeros_like(total)

    def up(s, carry):
        row, col, live = place(out_l, s)
        d_act[row] += dot(w_out[s], g[pl.ds(col, BLK), :], ((1,), (0,))) * live
        return carry

    def down(s, carry):
        row, col, live = place(in_l, s)
        total[pl.ds(col, BLK), :] += dot(w_in[s], dh[row], ((0,), (0,))) * live
        return carry

    lax.fori_loop(0, CAP, up, 0, unroll=8)
    for row in range(ROWS):
        dh[row] = (d_act[row] * slope[row]).astype(dh.dtype)
    lax.fori_loop(0, CAP, down, 0, unroll=8)
    part[...] = total[...].astype(part.dtype)


def grads_kernel(core, in_l, out_l, x, g, act, dh, keep, send):
    first = core[0] == 0
    scale = float(T * Z * C) ** -0.5

    def pair(p, carry):
        for which, (lists, units, wide) in enumerate(((out_l, act, g), (in_l, dh, x))):
            parts = []
            for i in range(2):
                row, col, live = place(lists, 2 * p + i)
                part = dot(units[row], wide[pl.ds(col, BLK), :], ((1,), (1,)))
                parts.append((part * (live * scale)).reshape(Z, C, SUB, BLK))
            both = jnp.stack(parts, axis=2).reshape(Z, C, 2 * SUB, BLK)
            at = pl.multiple_of((which * CAP + 2 * p) * SUB, 2 * SUB)
            keep[:, pl.ds(at, 2 * SUB), :] = jnp.where(first, both[:, 0], both[:, 1]).astype(
                keep.dtype
            )
            send[:, pl.ds(at, 2 * SUB), :] = jnp.where(first, both[:, 1], both[:, 0]).astype(
                send.dtype
            )
        return carry

    lax.fori_loop(0, CAP // 2, pair, 0, unroll=4)


SMEM = pl.BlockSpec(memory_space=pltpu.SMEM)
VMEM = pl.BlockSpec(memory_space=pltpu.VMEM)
LIMIT = pltpu.CompilerParams(vmem_limit_bytes=48 * 1024 * 1024)
UNITS = (ROWS, BLK, T)
INTERPRET = False


def shape(dims, dtype=jnp.bfloat16):
    return jax.ShapeDtypeStruct(dims, dtype)


def call(kernel, outs, scalars, arrays, scratch=()):
    return pl.pallas_call(
        kernel,
        out_shape=outs,
        in_specs=[SMEM] * len(scalars) + [VMEM] * len(arrays),
        out_specs=[VMEM] * len(outs),
        scratch_shapes=[pltpu.VMEM(dims, jnp.float32) for dims in scratch],
        compiler_params=LIMIT,
        interpret=INTERPRET,
    )(*scalars, *arrays)


def forward(in_l, out_l, x, w_in, w_out):
    outs = (shape(UNITS), shape(UNITS, jnp.float32), shape((FEAT, T)))
    return call(forward_kernel, outs, (in_l, out_l), (x, w_in, w_out), (UNITS, (FEAT, T)))


def backward(in_l, out_l, g, slope, w_in, w_out):
    outs = (shape(UNITS), shape((FEAT, T)))
    return call(backward_kernel, outs, (in_l, out_l), (g, slope, w_in, w_out), (UNITS, (FEAT, T)))


def block_grads(core, in_l, out_l, x, g, act, dh):
    half = shape((Z, 2 * CAP * SUB, BLK))
    return call(grads_kernel, (half, half), (core, in_l, out_l), (x, g, act, dh))


def exchange(x, axis):
    return lax.all_to_all(x, axis, split_axis=0, concat_axis=0)


def spread(x, axis, size):
    return exchange(jnp.broadcast_to(x[None], (size,) + x.shape), axis)


def added(parts):
    return jnp.sum(parts.astype(jnp.float32), axis=0).astype(parts.dtype)


def body(tokens, cotangent, in_blocks, in_lists, out_blocks, out_lists):
    bf, f32 = jnp.bfloat16, jnp.float32
    in_l, out_l = in_lists.reshape(-1), out_lists.reshape(-1)
    core = lax.axis_index("c").astype(jnp.int32).reshape(1)
    x = spread(tokens.T, "y", Y).reshape(Y * OWN, T)
    g = spread(cotangent.T, ("x", "y"), X * Y).reshape(FEAT, T)
    x = spread(x, "x", X).reshape(FEAT, T)
    act, slope, y_part = forward(in_l, out_l, x, in_blocks, out_blocks)
    y_part = exchange(y_part.reshape(X, Y * OWN, T), "x")
    dh, dx_part = backward(in_l, out_l, g, slope, in_blocks, out_blocks)
    dx_part = exchange(dx_part.reshape(X * Y, OWN, T), ("x", "y"))
    keep, send = block_grads(core, in_l, out_l, x, g, act, dh)
    got = lax.ppermute(send, "c", [(0, 1), (1, 0)])
    grads = exchange((keep.astype(f32) + got.astype(f32)).astype(bf), "z")
    y_part = exchange(added(y_part).reshape(Y, OWN, T), "y")
    grads = added(grads).reshape(2, CAP, SUB, BLK)
    return added(y_part).T, added(dx_part).T, grads[1], grads[0]


def solution(mesh):
    fine = Mesh(mesh.devices.reshape(Z, C, X, Y), ("z", "c", "x", "y"))
    dp, mp = ("z", "c"), ("x", "y")
    blocks, lists = P(mp, None, None), P(mp, None)
    return jax.shard_map(
        body,
        mesh=fine,
        in_specs=(P(dp, mp), P(dp, mp), blocks, lists, blocks, lists),
        out_specs=(P(dp, mp), P(dp, mp), P(mp, dp, None), P(mp, dp, None)),
        check_vma=False,
    )
```

time: 157 us -> 190 us (1.21)
  the two profiles are of different devices: /device:TPU:1 before, /device:TPU:8 now
where the time goes in v2:
time: 190 us; the launch traced here: 189 us
  waiting for transfers between devices  88.9 us (47%)
  starting transfers between devices  36.9 us (19%)
  blocking collectives  36.4 us (19%)
  Pallas kernels  9.77 us (5%)
  local copies, waits for them, and re-layouts  8.47 us (4%)
  other arithmetic  7.53 us (4%)
    all_to_all x5, waiting for transfers between devices, exchange(): return lax.all_to_all(x, axis, split_axis=0, concat_axis=0)  86.3 us
    all_to_all x2, blocking collectives, exchange(): return lax.all_to_all(x, axis, split_axis=0, concat_axis=0)  36.4 us
    all_to_all x5, starting transfers between devices, exchange(): return lax.all_to_all(x, axis, split_axis=0, concat_axis=0)  35 us
    pallas_call x3, Pallas kernels, call(): pl.pallas_call(kernel, out_shape=outs, in_specs=[SMEM] * len(scalars) + [...  9.77 us
    reduce_sum x4, other arithmetic, added(): return jnp.sum(parts.astype(jnp.float32), axis=0).astype(parts.dtype)  6.29 us
    unnamed x30, local copies, waits for them, and re-layouts  4.47 us
  transfers between devices with their start and end apart: 6, of which 6 were waited for; matrix products, arithmetic and copies ran while one was open for 4% of the time, Pallas kernels for 3%

profile of v2, /device:TPU:8, one launch (start us, length us, event | category | flops | bytes accessed | tf_op | source)
XLA Modules:
  0.0 188.8 jit_solution(18103679078356735503)
XLA Ops:
  1.4 19.2 %all_to_all.35 = bf16[8,80,256]{2,1,0:T(8,128)(2,1)S(1)} all-to-all(bf16[8,80,256]{2,1,0:T(8,128)(2,1)S(1)} %broadcast_in_dim.8), channel_id=1, replica_groups=mesh['z'=8,'c'=2,'x'=4,'y'=8] {'y'}, dimensions={0} | all-to-all | bytes 655360 | tf_op jit(solution)/shard_map/all_to_all | solution.py:153
  20.6 1.2 broadcast_in_dim.10
  21.8 4.4 %all-to-all-start.1 = ((bf16[4,640,256]{2,1,0:T(8,128)(2,1)}), bf16[4,640,256]{2,1,0:T(8,128)(2,1)S(1)}, u32[]{:S(2)}, u32[]{:S(2)}) async-start(bf16[4,640,256]{2,1,0:T(8,128)(2,1)} %broadcast_in_dim.10), calls=%async_computation.1 | async-start | bytes 2621440 | tf_op jit(solution)/shard_map/all_to_all | solution.py:153
  26.6 14.8 %all-to-all-done.1 = bf16[4,640,256]{2,1,0:T(8,128)(2,1)S(1)} async-done(((bf16[4,640,256]{2,1,0:T(8,128)(2,1)}), bf16[4,640,256]{2,1,0:T(8,128)(2,1)S(1)}, u32[]{:S(2)}, u32[]{:S(2)}) %all-to-all-start.1) | async-done | bytes 1310752 | tf_op jit(solution)/shard_map/all_to_all | solution.py:153
  41.4 3.9 %shard_map.93 = (bf16[5,128,256]{2,1,0:T(8,128)(2,1)S(1)}, f32[5,128,256]{2,1,0:T(8,128)S(1)}, bf16[2560,256]{1,0:T(8,128)(2,1)S(1)}) custom-call(s32[64]{0:T(128)S(1)} %reshape.40.in_l, s32[64]{0:T(128)S(1)} %reshape.41.out_l, bf16[2560,256]{1,0:T(8,128)(2,1)S(1)} %bitcast.15, bf16[32,128,128]{2,1,0:T(8,128)(2,1)S(1)} %copy-done, ...), custom_call_target="tpu_custom_call" | custom-call | tf_op jit(solution)/shard_map/pallas_call | solution.py:126
  45.3 17.2 %all_to_all.36 = bf16[4,640,256]{2,1,0:T(8,128)(2,1)} all-to-all(bf16[4,640,256]{2,1,0:T(8,128)(2,1)S(1)} %bitcast.20), channel_id=1, replica_groups=mesh['z'=8,'c'=2,'x'=4,'y'=8] {'x'}, dimensions={0} | all-to-all | bytes 2621440 | tf_op jit(solution)/shard_map/all_to_all | solution.py:153
  63.7 9.2 %all-to-all-start.4 = ((bf16[32,80,256]{2,1,0:T(8,128)(2,1)}), bf16[32,80,256]{2,1,0:T(8,128)(2,1)S(1)}, u32[]{:S(2)}, u32[]{:S(2)}) async-start(bf16[32,80,256]{2,1,0:T(8,128)(2,1)} %broadcast_in_dim.22), calls=%async_computation.4 | async-start | bytes 2621440 | tf_op jit(solution)/shard_map/all_to_all | solution.py:153
  73.0 2.4 %reduce_sum.48 = bf16[640,256]{1,0:T(8,128)(2,1)} reduce(bf16[4,640,256]{2,1,0:T(8,128)(2,1)} %all_to_all.36, bf16[]{:T(256)} %constant.9.clone.1), dimensions={0}, to_apply=%region_0.0 | reduce | flops 491520 | bytes 1638402 | tf_op jit(solution)/shard_map/reduce_sum | solution.py:161
  75.3 29.2 %all-to-all-done.4 = bf16[32,80,256]{2,1,0:T(8,128)(2,1)S(1)} async-done(((bf16[32,80,256]{2,1,0:T(8,128)(2,1)}), bf16[32,80,256]{2,1,0:T(8,128)(2,1)S(1)}, u32[]{:S(2)}, u32[]{:S(2)}) %all-to-all-start.4) | async-done | bytes 1310752 | tf_op jit(solution)/shard_map/all_to_all | solution.py:153
  104.5 4.0 %all-to-all-start.3 = ((bf16[8,80,256]{2,1,0:T(8,128)(2,1)}), bf16[8,80,256]{2,1,0:T(8,128)(2,1)}, u32[]{:S(2)}, u32[]{:S(2)}) async-start(bf16[8,80,256]{2,1,0:T(8,128)(2,1)} %bitcast.21), calls=%async_computation.3 | async-start | bytes 655360 | tf_op jit(solution)/shard_map/all_to_all | solution.py:153
  108.6 1.2 copy-done.1
  109.8 1.2 copy-done.3
  111.0 3.5 %shard_map.94 = (bf16[5,128,256]{2,1,0:T(8,128)(2,1)S(1)}, bf16[2560,256]{1,0:T(8,128)(2,1)S(1)}) custom-call(s32[64]{0:T(128)S(1)} %reshape.40.in_l, s32[64]{0:T(128)S(1)} %reshape.41.out_l, bf16[2560,256]{1,0:T(8,128)(2,1)S(1)} %bitcast.17, f32[5,128,256]{2,1,0:T(8,128)S(1)} %copy-done.6, bf16[32,128,128]{2,1,0:T(8,128)(2,1)S(1)} %copy-done.1, ...), custom_call_target="tpu_custom_call" | custom-call | tf_op jit(solution)/shard_map/pallas_call | solution.py:126
  116.4 1.4 all-to-all-done.3
  117.8 7.0 %all-to-all-start.5 = ((bf16[32,80,256]{2,1,0:T(8,128)(2,1)}), bf16[32,80,256]{2,1,0:T(8,128)(2,1)}, u32[]{:S(2)}, u32[]{:S(2)}) async-start(bf16[32,80,256]{2,1,0:T(8,128)(2,1)} %bitcast.19), calls=%async_computation.5 | async-start | bytes 2621440 | tf_op jit(solution)/shard_map/all_to_all | solution.py:153
  124.9 2.3 %shard_map.95 = (bf16[8,512,128]{2,1,0:T(8,128)(2,1)S(1)}, bf16[8,512,128]{2,1,0:T(8,128)(2,1)S(1)}) custom-call(s32[1]{0:T(128)} %bitcast.10.core, s32[64]{0:T(128)S(1)} %reshape.40.in_l, s32[64]{0:T(128)S(1)} %reshape.41.out_l, bf16[2560,256]{1,0:T(8,128)(2,1)S(1)} %bitcast.16, bf16[2560,256]{1,0:T(8,128)(2,1)S(1)} %bitcast.18, ...), custom_call_target="tpu_custom_call" | custom-call | tf_op jit(solution)/shard_map/pallas_call | solution.py:126
  127.2 1.9 %collective-permute-start = (bf16[8,512,128]{2,1,0:T(8,128)(2,1)S(1)}, bf16[8,512,128]{2,1,0:T(8,128)(2,1)S(1)}, u32[]{:S(2)}, u32[]{:S(2)}) collective-permute-start(bf16[8,512,128]{2,1,0:T(8,128)(2,1)S(1)} %get-tuple-element.17), channel_id=1, source_target_pairs={{0,32},{32,0},{1,33},{33,1},{2,34},{34,2},{3,35},{35,3},{4,36},{36... | collective-permute-start | bytes 3145736 | tf_op jit(solution)/shard_map/ppermute | solution.py:176
  129.2 2.6 %collective-permute-done = bf16[8,512,128]{2,1,0:T(8,128)(2,1)S(1)} collective-permute-done((bf16[8,512,128]{2,1,0:T(8,128)(2,1)S(1)}, bf16[8,512,128]{2,1,0:T(8,128)(2,1)S(1)}, u32[]{:S(2)}, u32[]{:S(2)}) %collective-permute-start) | collective-permute-done | bytes 1048608 | tf_op jit(solution)/shard_map/ppermute | solution.py:176
  131.8 1.2 add_convert_fusion
  133.0 21.6 %all-to-all-done.5 = bf16[32,80,256]{2,1,0:T(8,128)(2,1)} async-done(((bf16[32,80,256]{2,1,0:T(8,128)(2,1)}), bf16[32,80,256]{2,1,0:T(8,128)(2,1)}, u32[]{:S(2)}, u32[]{:S(2)}) %all-to-all-start.5) | async-done | bytes 1310752 | tf_op jit(solution)/shard_map/all_to_all | solution.py:153
  154.6 10.3 %all-to-all-start.6 = ((bf16[8,512,128]{2,1,0:T(8,128)(2,1)}), bf16[8,512,128]{2,1,0:T(8,128)(2,1)S(1)}, u32[]{:S(2)}, u32[]{:S(2)}) async-start(bf16[8,512,128]{2,1,0:T(8,128)(2,1)} %add_convert_fusion), calls=%async_computation.6 | async-start | bytes 2097152 | tf_op jit(solution)/shard_map/all_to_all | solution.py:153
  164.9 1.6 reduce_sum.49
  166.5 2.1 %reduce_sum.50 = bf16[80,256]{1,0:T(8,128)(2,1)} reduce(bf16[32,80,256]{2,1,0:T(8,128)(2,1)} %all-to-all-done.5, bf16[]{:T(256)} %constant.9.clone.1), dimensions={0}, to_apply=%region_2.0 | reduce | flops 634880 | bytes 1351682 | tf_op jit(solution)/shard_map/reduce_sum | solution.py:161
  168.7 19.3 %all-to-all-done.6 = bf16[8,512,128]{2,1,0:T(8,128)(2,1)S(1)} async-done(((bf16[8,512,128]{2,1,0:T(8,128)(2,1)}), bf16[8,512,128]{2,1,0:T(8,128)(2,1)S(1)}, u32[]{:S(2)}, u32[]{:S(2)}) %all-to-all-start.6) | async-done | bytes 1048608 | tf_op jit(solution)/shard_map/all_to_all | solution.py:153
  (34 shorter events, 5.0 us)
Async XLA Ops:
  21.8 4.5 %copy-start.12 = (s32[32,2]{0,1:T(2,128)S(1)}, s32[32,2]{0,1:T(2,128)}, u32[]{:S(2)}) copy-start(s32[32,2]{0,1:T(2,128)} %param.9) | copy-start | bytes 772
  21.8 4.6 %copy-start.13 = (s32[32,2]{0,1:T(2,128)S(1)}, s32[32,2]{0,1:T(2,128)}, u32[]{:S(2)}) copy-start(s32[32,2]{0,1:T(2,128)} %param.11) | copy-start | bytes 772
  21.8 19.6 %copy-start = (bf16[32,128,128]{2,1,0:T(8,128)(2,1)S(1)}, bf16[32,128,128]{2,1,0:T(8,128)(2,1)}, u32[]{:S(2)}) copy-start(bf16[32,128,128]{2,1,0:T(8,128)(2,1)} %w_in.3) | copy-start | bytes 3145732
  21.8 19.6 %copy-start.2 = (bf16[32,128,128]{2,1,0:T(8,128)(2,1)S(1)}, bf16[32,128,128]{2,1,0:T(8,128)(2,1)}, u32[]{:S(2)}) copy-start(bf16[32,128,128]{2,1,0:T(8,128)(2,1)} %w_out.3) | copy-start | bytes 3145732
  21.8 19.6 %all-to-all-start.1 = ((bf16[4,640,256]{2,1,0:T(8,128)(2,1)}), bf16[4,640,256]{2,1,0:T(8,128)(2,1)S(1)}, u32[]{:S(2)}, u32[]{:S(2)}) async-start(bf16[4,640,256]{2,1,0:T(8,128)(2,1)} %broadcast_in_dim.10), calls=%async_computation.1 | async-start | bytes 2621440 | tf_op jit(solution)/shard_map/all_to_all | solution.py:153
  45.3 17.3 %copy-start.5 = (f32[5,128,256]{2,1,0:T(8,128)}, f32[5,128,256]{2,1,0:T(8,128)S(1)}, u32[]{:S(2)}) copy-start(f32[5,128,256]{2,1,0:T(8,128)S(1)} %get-tuple-element.12.slope) | copy-start | bytes 1966084
  45.3 17.2 %copy-start.7 = (bf16[5,128,256]{2,1,0:T(8,128)(2,1)}, bf16[5,128,256]{2,1,0:T(8,128)(2,1)S(1)}, u32[]{:S(2)}) copy-start(bf16[5,128,256]{2,1,0:T(8,128)(2,1)S(1)} %get-tuple-element.14.act) | copy-start | bytes 983044
  45.3 17.2 %copy-start.11 = (bf16[256,80]{0,1:T(8,128)(2,1)S(1)}, bf16[256,80]{0,1:T(8,128)(2,1)}, u32[]{:S(2)}) copy-start(bf16[256,80]{0,1:T(8,128)(2,1)} %param.7) | copy-start | bytes 122884
  63.7 40.8 %all-to-all-start.4 = ((bf16[32,80,256]{2,1,0:T(8,128)(2,1)}), bf16[32,80,256]{2,1,0:T(8,128)(2,1)S(1)}, u32[]{:S(2)}, u32[]{:S(2)}) async-start(bf16[32,80,256]{2,1,0:T(8,128)(2,1)} %broadcast_in_dim.22), calls=%async_computation.4 | async-start | bytes 2621440 | tf_op jit(solution)/shard_map/all_to_all | solution.py:153
  73.0 35.6 %copy-start.6 = (f32[5,128,256]{2,1,0:T(8,128)S(1)}, f32[5,128,256]{2,1,0:T(8,128)}, u32[]{:S(2)}) copy-start(f32[5,128,256]{2,1,0:T(8,128)} %copy-done.5) | copy-start | bytes 1966084
  104.5 13.3 %all-to-all-start.3 = ((bf16[8,80,256]{2,1,0:T(8,128)(2,1)}), bf16[8,80,256]{2,1,0:T(8,128)(2,1)}, u32[]{:S(2)}, u32[]{:S(2)}) async-start(bf16[8,80,256]{2,1,0:T(8,128)(2,1)} %bitcast.21), calls=%async_computation.3 | async-start | bytes 655360 | tf_op jit(solution)/shard_map/all_to_all | solution.py:153
  108.6 1.2 copy-start.1
  109.8 1.2 copy-start.3
  114.6 1.1 copy-start.4
  115.6 0.7 copy-start.9
  117.8 7.1 %copy-start.8 = (bf16[5,128,256]{2,1,0:T(8,128)(2,1)S(1)}, bf16[5,128,256]{2,1,0:T(8,128)(2,1)}, u32[]{:S(2)}) copy-start(bf16[5,128,256]{2,1,0:T(8,128)(2,1)} %copy-done.7) | copy-start | bytes 983044
  117.8 7.1 %copy-start.10 = (bf16[5,128,256]{2,1,0:T(8,128)(2,1)S(1)}, bf16[5,128,256]{2,1,0:T(8,128)(2,1)}, u32[]{:S(2)}) copy-start(bf16[5,128,256]{2,1,0:T(8,128)(2,1)} %copy-done.9) | copy-start | bytes 983044
  117.8 36.8 %all-to-all-start.5 = ((bf16[32,80,256]{2,1,0:T(8,128)(2,1)}), bf16[32,80,256]{2,1,0:T(8,128)(2,1)}, u32[]{:S(2)}, u32[]{:S(2)}) async-start(bf16[32,80,256]{2,1,0:T(8,128)(2,1)} %bitcast.19), calls=%async_computation.5 | async-start | bytes 2621440 | tf_op jit(solution)/shard_map/all_to_all | solution.py:153
  127.2 4.6 %collective-permute-start = (bf16[8,512,128]{2,1,0:T(8,128)(2,1)S(1)}, bf16[8,512,128]{2,1,0:T(8,128)(2,1)S(1)}, u32[]{:S(2)}, u32[]{:S(2)}) collective-permute-start(bf16[8,512,128]{2,1,0:T(8,128)(2,1)S(1)} %get-tuple-element.17), channel_id=1, source_target_pairs={{0,32},{32,0},{1,33},{33,1},{2,34},{34,2},{3,35},{35,3},{4,36},{36... | collective-permute-start | bytes 3145736 | tf_op jit(solution)/shard_map/ppermute | solution.py:176
  154.6 33.4 %all-to-all-start.6 = ((bf16[8,512,128]{2,1,0:T(8,128)(2,1)}), bf16[8,512,128]{2,1,0:T(8,128)(2,1)S(1)}, u32[]{:S(2)}, u32[]{:S(2)}) async-start(bf16[8,512,128]{2,1,0:T(8,128)(2,1)} %add_convert_fusion), calls=%async_computation.6 | async-start | bytes 2097152 | tf_op jit(solution)/shard_map/all_to_all | solution.py:153

commit v3 on v1

--- a/solution.py
+++ b/solution.py
@@ -43,7 +43,7 @@
     return row, pl.multiple_of(jnp.maximum(col, 0) * BLK, BLK), live
 
 
-def units_kernel(core, in_l, out_l, xg, w_in, w_out, keep, send, act, dh, hidden, d_act):
+def units_kernel(at_z, core, in_l, out_l, xg, w_in, w_out, keep, send, act, dh, hidden, d_act):
     hidden[...] = jnp.zeros_like(hidden)
     d_act[...] = jnp.zeros_like(d_act)
 
@@ -72,12 +72,12 @@
                 parts.append((part * (live * scale)).reshape(Z, C, SUB, BLK))
             both = jnp.stack(parts, axis=2).reshape(Z, C, 2 * SUB, BLK)
             at = pl.multiple_of((which * CAP + 2 * p) * SUB, 2 * SUB)
-            keep[:, pl.ds(at, 2 * SUB), :] = jnp.where(first, both[:, 0], both[:, 1]).astype(
-                keep.dtype
-            )
-            send[:, pl.ds(at, 2 * SUB), :] = jnp.where(first, both[:, 1], both[:, 0]).astype(
-                send.dtype
-            )
+            mine = jnp.where(first, both[:, 0], both[:, 1]).astype(keep.dtype)
+            others = jnp.where(first, both[:, 1], both[:, 0]).astype(send.dtype)
+            for z in range(Z):
+                step = lax.rem(z + Z - at_z[0], Z)
+                keep[step, pl.ds(at, 2 * SUB), :] = mine[z]
+                send[step, pl.ds(at, 2 * SUB), :] = others[z]
         return carry
 
     lax.fori_loop(0, CAP // 2, pair, 0, unroll=4)
@@ -97,24 +97,30 @@
     out[...] = total[...].astype(out.dtype)
 
 
+def pair_kernel(keep, got, *outs):
+    for step, out in enumerate(outs):
+        both = keep[step].astype(jnp.float32) + got[step].astype(jnp.float32)
+        out[...] = both.astype(out.dtype)
+
+
 SMEM = pl.BlockSpec(memory_space=pltpu.SMEM)
 VMEM = pl.BlockSpec(memory_space=pltpu.VMEM)
 LIMIT = pltpu.CompilerParams(vmem_limit_bytes=48 * 1024 * 1024)
 
 
-def units_call(core, in_l, out_l, xg, w_in, w_out, interpret=False):
+def units_call(at_z, core, in_l, out_l, xg, w_in, w_out, interpret=False):
     bf = jnp.bfloat16
     half = jax.ShapeDtypeStruct((Z, 2 * CAP * SUB, BLK), bf)
     rows = jax.ShapeDtypeStruct((ROWS, BLK, T), bf)
     return pl.pallas_call(
         units_kernel,
         out_shape=(half, half, rows, rows),
-        in_specs=[SMEM] * 3 + [VMEM] * 3,
+        in_specs=[SMEM] * 4 + [VMEM] * 3,
         out_specs=[VMEM] * 4,
         scratch_shapes=[pltpu.VMEM((ROWS, BLK, T), jnp.float32)] * 2,
         compiler_params=LIMIT,
         interpret=interpret,
-    )(core, in_l, out_l, xg, w_in, w_out)
+    )(at_z, core, in_l, out_l, xg, w_in, w_out)
 
 
 def partials_call(in_l, out_l, act, dh, w_in, w_out, interpret=False):
@@ -127,6 +133,17 @@
         compiler_params=LIMIT,
         interpret=interpret,
     )(in_l, out_l, act, dh, w_in, w_out)
+
+
+def pair_call(keep, got):
+    out = jax.ShapeDtypeStruct(keep.shape[1:], keep.dtype)
+    return pl.pallas_call(
+        pair_kernel,
+        out_shape=(out,) * Z,
+        in_specs=[VMEM] * 2,
+        out_specs=[VMEM] * Z,
+        compiler_params=LIMIT,
+    )(keep, got)
 
 
 def exchange(x, axis):
@@ -144,17 +161,25 @@
     along_y = spread(own, "y", Y).reshape(Y * OWN, 2 * T)
     xg = spread(along_y, "x", X).reshape(FEAT, 2 * T)
     core = lax.axis_index("c").astype(jnp.int32).reshape(1)
-    keep, send, act, dh = units_call(core, in_l, out_l, xg, in_blocks, out_blocks)
+    at_z = lax.axis_index("z").astype(jnp.int32).reshape(1)
+    keep, send, act, dh = units_call(at_z, core, in_l, out_l, xg, in_blocks, out_blocks)
     got = lax.ppermute(send, "c", [(0, 1), (1, 0)])
     parts = partials_call(in_l, out_l, act, dh, in_blocks, out_blocks)
-    grads = (keep.astype(f32) + got.astype(f32)).astype(bf)
-    grads, parts = lax.optimization_barrier((grads, parts))
-    grads = lax.psum_scatter(grads, "z", scatter_dimension=0)
+    steps = pair_call(keep, got)
+    steps, parts = lax.optimization_barrier((steps, parts))
     parts = exchange(parts.reshape(X, Y * OWN, 2 * T), "x")
+
+    def along_z(step):
+        return lax.ppermute(steps[step], "z", [(z, (z + step) % Z) for z in range(Z)])
+
+    early = [along_z(step) for step in range(2, Z - 1)]
+    parts, early = lax.optimization_barrier((parts, early))
+    moved = [*early, along_z(1), along_z(Z - 1)]
     parts = jnp.sum(parts.astype(f32), axis=0).astype(bf)
     parts = exchange(parts.reshape(Y, OWN, 2 * T), "y")
     sums = jnp.sum(parts.astype(f32), axis=0).astype(bf)
-    grads = grads.reshape(2, CAP, SUB, BLK)
+    grads = sum((m.astype(f32) for m in moved), steps[0].astype(f32))
+    grads = grads.astype(bf).reshape(2, CAP, SUB, BLK)
     return sums[:, :T].T, sums[:, T:].T, grads[1], grads[0]
 
 

time: 157 us -> 155 us (0.987)
  starting transfers between devices: 17.8 us -> 51.7 us
  waiting for transfers between devices: 80.8 us -> 57.6 us
  between operations: 14.1 us -> 0.77 us
    all_to_all x3, waiting for transfers between devices: 75.1 us -> 40.5 us  [exchange(): return lax.all_to_all(x, axis, split_axis=0, concat_axis=0)]
    ppermute x0 -> x7, starting transfers between devices: none -> 33 us  [along_z(): lax.ppermute(steps[step], 'z', [(z, (z + step) % Z) for z in range(Z)])]
    ppermute x0 -> x7, waiting for transfers between devices: none -> 17.1 us  [along_z(): lax.ppermute(steps[step], 'z', [(z, (z + step) % Z) for z in range(Z)])]
    reduce_scatter x1 -> x0, waiting for transfers between devices: 5.1 us -> none  [body(): grads = lax.psum_scatter(grads, 'z', scatter_dimension=0)]
    reduce_sum x1, other arithmetic: 1.41 us -> 3.17 us  [body(): parts = jnp.sum(parts.astype(f32), axis=0).astype(bf)]
  transfers between devices with their start and end apart: 5 -> 11, of which waited for: 4 -> 8; matrix products, arithmetic and copies ran while one was open for 2% -> 1% of each run, Pallas kernels for 3% -> 3%
where the time goes in v3:
time: 155 us; the launch traced here: 154 us
  waiting for transfers between devices  57.6 us (37%)
  starting transfers between devices  51.7 us (33%)
  blocking collectives  25.3 us (16%)
  Pallas kernels  10.9 us (7%)
  other arithmetic  4.21 us (3%)
  local copies, waits for them, and re-layouts  3.47 us (2%)
    all_to_all x3, waiting for transfers between devices, exchange(): return lax.all_to_all(x, axis, split_axis=0, concat_axis=0)  40.5 us
    ppermute x7, starting transfers between devices, along_z(): lax.ppermute(steps[step], 'z', [(z, (z + step) % Z) for z in range(Z)])  33 us
    all_to_all x1, blocking collectives, exchange(): return lax.all_to_all(x, axis, split_axis=0, concat_axis=0)  25.3 us
    ppermute x7, waiting for transfers between devices, along_z(): lax.ppermute(steps[step], 'z', [(z, (z + step) % Z) for z in range(Z)])  17.1 us
    all_to_all x3, starting transfers between devices, exchange(): return lax.all_to_all(x, axis, split_axis=0, concat_axis=0)  13.5 us
    pallas_call x1, Pallas kernels, units_call(): pl.pallas_call(units_kernel, out_shape=(half, half, rows, rows), in_specs...  6.07 us
    ppermute x1, starting transfers between devices, body(): got = lax.ppermute(send, 'c', [(0, 1), (1, 0)])  5.18 us
    pallas_call x1, Pallas kernels, partials_call(): pl.pallas_call(partials_kernel, out_shape=jax.ShapeDtypeStruct((FEAT, 2 *...  4.56 us
  transfers between devices with their start and end apart: 11, of which 8 were waited for; matrix products, arithmetic and copies ran while one was open for 1% of the time, Pallas kernels for 3%

profile of v3, /device:TPU:1, one launch (start us, length us, event | category | flops | bytes accessed | tf_op | source)
XLA Modules:
  0.0 154.0 jit_solution(15480779380373449357)
XLA Ops:
  0.6 0.8 pad_maximum_fusion
  1.5 25.3 %all_to_all.20 = bf16[8,80,512]{2,1,0:T(8,128)(2,1)S(1)} all-to-all(bf16[8,80,512]{2,1,0:T(8,128)(2,1)S(1)} %broadcast_in_dim.6), channel_id=1, replica_groups=mesh['z'=8,'c'=2,'x'=4,'y'=8] {'y'}, dimensions={0} | all-to-all | bytes 1310720 | tf_op jit(solution)/shard_map/all_to_all | solution.py:150
  26.8 1.7 %broadcast_in_dim.15 = bf16[4,640,512]{2,1,0:T(8,128)(2,1)} broadcast(bf16[640,512]{1,0:T(8,128)(2,1)S(1)} %bitcast.16), dimensions={1,2} | broadcast | bytes 3276800 | tf_op jit(solution)/shard_map/broadcast_in_dim | solution.py:154
  28.6 5.4 %all-to-all-start.1 = ((bf16[4,640,512]{2,1,0:T(8,128)(2,1)}), bf16[4,640,512]{2,1,0:T(8,128)(2,1)}, u32[]{:S(2)}, u32[]{:S(2)}) async-start(bf16[4,640,512]{2,1,0:T(8,128)(2,1)} %broadcast_in_dim.15), calls=%async_computation.1 | async-start | bytes 5242880 | tf_op jit(solution)/shard_map/all_to_all | solution.py:150
  34.4 29.6 %all-to-all-done.1 = bf16[4,640,512]{2,1,0:T(8,128)(2,1)} async-done(((bf16[4,640,512]{2,1,0:T(8,128)(2,1)}), bf16[4,640,512]{2,1,0:T(8,128)(2,1)}, u32[]{:S(2)}, u32[]{:S(2)}) %all-to-all-start.1) | async-done | bytes 2621472 | tf_op jit(solution)/shard_map/all_to_all | solution.py:150
  64.0 6.1 %shard_map.93 = (bf16[8,512,128]{2,1,0:T(8,128)(2,1)S(1)}, bf16[8,512,128]{2,1,0:T(8,128)(2,1)S(1)}, bf16[5,128,256]{2,1,0:T(8,128)(2,1)S(1)}, bf16[5,128,256]{2,1,0:T(8,128)(2,1)S(1)}) custom-call(s32[1]{0:T(128)} %bitcast.at_z, s32[1]{0:T(128)} %bitcast.1.core, s32[64]{0:T(128)S(1)} %reshape.38.in_l, s32[64]{0:T(128)S(1)} %reshape.39.out_l, ...), custom_call_target="tpu_custom_call" | custom-call | tf_op jit(solution)/shard_map/pallas_call | solution.py:115
  70.1 5.2 %collective-permute-start = (bf16[8,512,128]{2,1,0:T(8,128)(2,1)S(1)}, bf16[8,512,128]{2,1,0:T(8,128)(2,1)S(1)}, u32[]{:S(2)}, u32[]{:S(2)}) collective-permute-start(bf16[8,512,128]{2,1,0:T(8,128)(2,1)S(1)} %get-tuple-element.32), channel_id=1, source_target_pairs={{0,32},{32,0},{1,33},{33,1},{2,34},{34,2},{3,35},{35,3},{4,36},{36... | collective-permute-start | bytes 3145736 | tf_op jit(solution)/shard_map/ppermute | solution.py:166
  75.3 4.6 %shard_map.95 = bf16[2560,512]{1,0:T(8,128)(2,1)} custom-call(s32[64]{0:T(128)S(1)} %reshape.38.in_l, s32[64]{0:T(128)S(1)} %reshape.39.out_l, bf16[5,128,256]{2,1,0:T(8,128)(2,1)S(1)} %get-tuple-element.41.act, bf16[5,128,256]{2,1,0:T(8,128)(2,1)S(1)} %get-tuple-element.42.dh, bf16[32,128,128]{2,1,0:T(8,128)(2,1)S(1)} %copy-done, ...), custom_call_target="tpu_custom_call" | custom-call | tf_op jit(solution)/shard_map/pallas_call | solution.py:127
  80.1 4.6 %all-to-all-start.2 = ((bf16[4,640,512]{2,1,0:T(8,128)(2,1)}), bf16[4,640,512]{2,1,0:T(8,128)(2,1)}, u32[]{:S(2)}, u32[]{:S(2)}) async-start(bf16[4,640,512]{2,1,0:T(8,128)(2,1)} %bitcast.6), calls=%async_computation.2 | async-start | bytes 5242880 | tf_op jit(solution)/shard_map/all_to_all | solution.py:150
  84.7 6.0 %collective-permute-start.1 = (bf16[512,128]{1,0:T(8,128)(2,1)S(1)}, bf16[512,128]{1,0:T(8,128)(2,1)S(1)}, u32[]{:S(2)}, u32[]{:S(2)}) collective-permute-start(bf16[512,128]{1,0:T(8,128)(2,1)S(1)} %get-tuple-element.44), channel_id=1, source_target_pairs={{0,128},{64,192},{128,256},{192,320},{256,384},{320,448},{384,0},{... | collective-permute-start | bytes 393224 | tf_op jit(solution)/shard_map/ppermute | solution.py:173
  90.7 7.9 %collective-permute-start.2 = (bf16[512,128]{1,0:T(8,128)(2,1)S(1)}, bf16[512,128]{1,0:T(8,128)(2,1)S(1)}, u32[]{:S(2)}, u32[]{:S(2)}) collective-permute-start(bf16[512,128]{1,0:T(8,128)(2,1)S(1)} %get-tuple-element.45), channel_id=1, source_target_pairs={{0,192},{64,256},{128,320},{192,384},{256,448},{320,0},{384,64},{4... | collective-permute-start | bytes 393224 | tf_op jit(solution)/shard_map/ppermute | solution.py:173
  98.6 3.7 %collective-permute-start.3 = (bf16[512,128]{1,0:T(8,128)(2,1)S(1)}, bf16[512,128]{1,0:T(8,128)(2,1)S(1)}, u32[]{:S(2)}, u32[]{:S(2)}) collective-permute-start(bf16[512,128]{1,0:T(8,128)(2,1)S(1)} %get-tuple-element.46), channel_id=1, source_target_pairs={{0,256},{64,320},{128,384},{192,448},{256,0},{320,64},{384,128},{4... | collective-permute-start | bytes 393224 | tf_op jit(solution)/shard_map/ppermute | solution.py:173
  102.4 5.5 %collective-permute-start.4 = (bf16[512,128]{1,0:T(8,128)(2,1)S(1)}, bf16[512,128]{1,0:T(8,128)(2,1)S(1)}, u32[]{:S(2)}, u32[]{:S(2)}) collective-permute-start(bf16[512,128]{1,0:T(8,128)(2,1)S(1)} %get-tuple-element.47), channel_id=1, source_target_pairs={{0,320},{64,384},{128,448},{192,0},{256,64},{320,128},{384,192},{4... | collective-permute-start | bytes 393224 | tf_op jit(solution)/shard_map/ppermute | solution.py:173
  107.9 3.4 %collective-permute-start.5 = (bf16[512,128]{1,0:T(8,128)(2,1)S(1)}, bf16[512,128]{1,0:T(8,128)(2,1)S(1)}, u32[]{:S(2)}, u32[]{:S(2)}) collective-permute-start(bf16[512,128]{1,0:T(8,128)(2,1)S(1)} %get-tuple-element.48), channel_id=1, source_target_pairs={{0,384},{64,448},{128,0},{192,64},{256,128},{320,192},{384,256},{4... | collective-permute-start | bytes 393224 | tf_op jit(solution)/shard_map/ppermute | solution.py:173
  111.4 4.4 %collective-permute-done.3 = bf16[512,128]{1,0:T(8,128)(2,1)S(1)} collective-permute-done((bf16[512,128]{1,0:T(8,128)(2,1)S(1)}, bf16[512,128]{1,0:T(8,128)(2,1)S(1)}, u32[]{:S(2)}, u32[]{:S(2)}) %collective-permute-start.3) | collective-permute-done | bytes 131104 | tf_op jit(solution)/shard_map/ppermute | solution.py:173
  116.3 9.6 %collective-permute-done.5 = bf16[512,128]{1,0:T(8,128)(2,1)S(1)} collective-permute-done((bf16[512,128]{1,0:T(8,128)(2,1)S(1)}, bf16[512,128]{1,0:T(8,128)(2,1)S(1)}, u32[]{:S(2)}, u32[]{:S(2)}) %collective-permute-start.5) | collective-permute-done | bytes 131104 | tf_op jit(solution)/shard_map/ppermute | solution.py:173
  125.9 3.2 %reduce_sum.24 = bf16[640,512]{1,0:T(8,128)(2,1)} reduce(bf16[4,640,512]{2,1,0:T(8,128)(2,1)} %all-to-all-done.2, bf16[]{:T(256)} %constant.15.clone.1), dimensions={0}, to_apply=%region_0.0 | reduce | flops 983040 | bytes 3276802 | tf_op jit(solution)/shard_map/reduce_sum | solution.py:178
  129.0 3.5 %all-to-all-start.3 = ((bf16[8,80,512]{2,1,0:T(8,128)(2,1)}), bf16[8,80,512]{2,1,0:T(8,128)(2,1)S(1)}, u32[]{:S(2)}, u32[]{:S(2)}) async-start(bf16[8,80,512]{2,1,0:T(8,128)(2,1)} %bitcast.7), calls=%async_computation.3 | async-start | bytes 1310720 | tf_op jit(solution)/shard_map/all_to_all | solution.py:150
  132.6 1.9 %collective-permute-start.6 = (bf16[512,128]{1,0:T(8,128)(2,1)S(1)}, bf16[512,128]{1,0:T(8,128)(2,1)S(1)}, u32[]{:S(2)}, u32[]{:S(2)}) collective-permute-start(bf16[512,128]{1,0:T(8,128)(2,1)S(1)} %get-tuple-element.56), channel_id=1, source_target_pairs={{0,64},{64,128},{128,192},{192,256},{256,320},{320,384},{384,448},... | collective-permute-start | bytes 393224 | tf_op jit(solution)/shard_map/ppermute | solution.py:173
  134.5 4.6 %collective-permute-start.7 = (bf16[512,128]{1,0:T(8,128)(2,1)S(1)}, bf16[512,128]{1,0:T(8,128)(2,1)S(1)}, u32[]{:S(2)}, u32[]{:S(2)}) collective-permute-start(bf16[512,128]{1,0:T(8,128)(2,1)S(1)} %get-tuple-element.57), channel_id=1, source_target_pairs={{0,448},{64,0},{128,64},{192,128},{256,192},{320,256},{384,320},{4... | collective-permute-start | bytes 393224 | tf_op jit(solution)/shard_map/ppermute | solution.py:173
  139.1 1.2 collective-permute-done.6
  140.3 1.3 collective-permute-done.7
  141.7 0.7 slice_bitcast_fusion
  142.4 10.9 %all-to-all-done.3 = bf16[8,80,512]{2,1,0:T(8,128)(2,1)S(1)} async-done(((bf16[8,80,512]{2,1,0:T(8,128)(2,1)}), bf16[8,80,512]{2,1,0:T(8,128)(2,1)S(1)}, u32[]{:S(2)}, u32[]{:S(2)}) %all-to-all-start.3) | async-done | bytes 655392 | tf_op jit(solution)/shard_map/all_to_all | solution.py:150
  (22 shorter events, 2.2 us)
Async XLA Ops:
  28.5 5.4 %copy-start.2 = (s32[32,2]{0,1:T(2,128)S(1)}, s32[32,2]{0,1:T(2,128)}, u32[]{:S(2)}) copy-start(s32[32,2]{0,1:T(2,128)} %param.9) | copy-start | bytes 772
  28.5 5.6 %copy-start.3 = (s32[32,2]{0,1:T(2,128)S(1)}, s32[32,2]{0,1:T(2,128)}, u32[]{:S(2)}) copy-start(s32[32,2]{0,1:T(2,128)} %param.11) | copy-start | bytes 772
  28.6 35.5 %copy-start = (bf16[32,128,128]{2,1,0:T(8,128)(2,1)S(1)}, bf16[32,128,128]{2,1,0:T(8,128)(2,1)}, u32[]{:S(2)}) copy-start(bf16[32,128,128]{2,1,0:T(8,128)(2,1)} %w_in.3) | copy-start | bytes 3145732
  28.6 35.5 %copy-start.1 = (bf16[32,128,128]{2,1,0:T(8,128)(2,1)S(1)}, bf16[32,128,128]{2,1,0:T(8,128)(2,1)}, u32[]{:S(2)}) copy-start(bf16[32,128,128]{2,1,0:T(8,128)(2,1)} %w_out.3) | copy-start | bytes 3145732
  28.6 35.5 %all-to-all-start.1 = ((bf16[4,640,512]{2,1,0:T(8,128)(2,1)}), bf16[4,640,512]{2,1,0:T(8,128)(2,1)}, u32[]{:S(2)}, u32[]{:S(2)}) async-start(bf16[4,640,512]{2,1,0:T(8,128)(2,1)} %broadcast_in_dim.15), calls=%async_computation.1 | async-start | bytes 5242880 | tf_op jit(solution)/shard_map/all_to_all | solution.py:150
  70.1 9.8 %collective-permute-start = (bf16[8,512,128]{2,1,0:T(8,128)(2,1)S(1)}, bf16[8,512,128]{2,1,0:T(8,128)(2,1)S(1)}, u32[]{:S(2)}, u32[]{:S(2)}) collective-permute-start(bf16[8,512,128]{2,1,0:T(8,128)(2,1)S(1)} %get-tuple-element.32), channel_id=1, source_target_pairs={{0,32},{32,0},{1,33},{33,1},{2,34},{34,2},{3,35},{35,3},{4,36},{36... | collective-permute-start | bytes 3145736 | tf_op jit(solution)/shard_map/ppermute | solution.py:166
  80.1 45.8 %all-to-all-start.2 = ((bf16[4,640,512]{2,1,0:T(8,128)(2,1)}), bf16[4,640,512]{2,1,0:T(8,128)(2,1)}, u32[]{:S(2)}, u32[]{:S(2)}) async-start(bf16[4,640,512]{2,1,0:T(8,128)(2,1)} %bitcast.6), calls=%async_computation.2 | async-start | bytes 5242880 | tf_op jit(solution)/shard_map/all_to_all | solution.py:150
  84.7 26.6 %collective-permute-start.1 = (bf16[512,128]{1,0:T(8,128)(2,1)S(1)}, bf16[512,128]{1,0:T(8,128)(2,1)S(1)}, u32[]{:S(2)}, u32[]{:S(2)}) collective-permute-start(bf16[512,128]{1,0:T(8,128)(2,1)S(1)} %get-tuple-element.44), channel_id=1, source_target_pairs={{0,128},{64,192},{128,256},{192,320},{256,384},{320,448},{384,0},{... | collective-permute-start | bytes 393224 | tf_op jit(solution)/shard_map/ppermute | solution.py:173
  90.7 20.7 %collective-permute-start.2 = (bf16[512,128]{1,0:T(8,128)(2,1)S(1)}, bf16[512,128]{1,0:T(8,128)(2,1)S(1)}, u32[]{:S(2)}, u32[]{:S(2)}) collective-permute-start(bf16[512,128]{1,0:T(8,128)(2,1)S(1)} %get-tuple-element.45), channel_id=1, source_target_pairs={{0,192},{64,256},{128,320},{192,384},{256,448},{320,0},{384,64},{4... | collective-permute-start | bytes 393224 | tf_op jit(solution)/shard_map/ppermute | solution.py:173
  98.6 17.1 %collective-permute-start.3 = (bf16[512,128]{1,0:T(8,128)(2,1)S(1)}, bf16[512,128]{1,0:T(8,128)(2,1)S(1)}, u32[]{:S(2)}, u32[]{:S(2)}) collective-permute-start(bf16[512,128]{1,0:T(8,128)(2,1)S(1)} %get-tuple-element.46), channel_id=1, source_target_pairs={{0,256},{64,320},{128,384},{192,448},{256,0},{320,64},{384,128},{4... | collective-permute-start | bytes 393224 | tf_op jit(solution)/shard_map/ppermute | solution.py:173
  102.4 13.9 %collective-permute-start.4 = (bf16[512,128]{1,0:T(8,128)(2,1)S(1)}, bf16[512,128]{1,0:T(8,128)(2,1)S(1)}, u32[]{:S(2)}, u32[]{:S(2)}) collective-permute-start(bf16[512,128]{1,0:T(8,128)(2,1)S(1)} %get-tuple-element.47), channel_id=1, source_target_pairs={{0,320},{64,384},{128,448},{192,0},{256,64},{320,128},{384,192},{4... | collective-permute-start | bytes 393224 | tf_op jit(solution)/shard_map/ppermute | solution.py:173
  107.9 18.0 %collective-permute-start.5 = (bf16[512,128]{1,0:T(8,128)(2,1)S(1)}, bf16[512,128]{1,0:T(8,128)(2,1)S(1)}, u32[]{:S(2)}, u32[]{:S(2)}) collective-permute-start(bf16[512,128]{1,0:T(8,128)(2,1)S(1)} %get-tuple-element.48), channel_id=1, source_target_pairs={{0,384},{64,448},{128,0},{192,64},{256,128},{320,192},{384,256},{4... | collective-permute-start | bytes 393224 | tf_op jit(solution)/shard_map/ppermute | solution.py:173
  129.0 24.2 %all-to-all-start.3 = ((bf16[8,80,512]{2,1,0:T(8,128)(2,1)}), bf16[8,80,512]{2,1,0:T(8,128)(2,1)S(1)}, u32[]{:S(2)}, u32[]{:S(2)}) async-start(bf16[8,80,512]{2,1,0:T(8,128)(2,1)} %bitcast.7), calls=%async_computation.3 | async-start | bytes 1310720 | tf_op jit(solution)/shard_map/all_to_all | solution.py:150
  132.6 7.7 %collective-permute-start.6 = (bf16[512,128]{1,0:T(8,128)(2,1)S(1)}, bf16[512,128]{1,0:T(8,128)(2,1)S(1)}, u32[]{:S(2)}, u32[]{:S(2)}) collective-permute-start(bf16[512,128]{1,0:T(8,128)(2,1)S(1)} %get-tuple-element.56), channel_id=1, source_target_pairs={{0,64},{64,128},{128,192},{192,256},{256,320},{320,384},{384,448},... | collective-permute-start | bytes 393224 | tf_op jit(solution)/shard_map/ppermute | solution.py:173
  134.5 7.1 %collective-permute-start.7 = (bf16[512,128]{1,0:T(8,128)(2,1)S(1)}, bf16[512,128]{1,0:T(8,128)(2,1)S(1)}, u32[]{:S(2)}, u32[]{:S(2)}) collective-permute-start(bf16[512,128]{1,0:T(8,128)(2,1)S(1)} %get-tuple-element.57), channel_id=1, source_target_pairs={{0,448},{64,0},{128,64},{192,128},{256,192},{320,256},{384,320},{4... | collective-permute-start | bytes 393224 | tf_op jit(solution)/shard_map/ppermute | solution.py:173

commit v4 on v3

--- a/solution.py
+++ b/solution.py
@@ -43,6 +43,12 @@
     return row, pl.multiple_of(jnp.maximum(col, 0) * BLK, BLK), live
 
 
+def slot_of(z, target):
+    odd = lax.rem(target + Z - z, 2)
+    base = z + odd * (1 - 2 * lax.rem(z, 2))
+    return odd * (Z // 2) + lax.rem(target + Z - base, Z) // 2
+
+
 def units_kernel(at_z, core, in_l, out_l, xg, w_in, w_out, keep, send, act, dh, hidden, d_act):
     hidden[...] = jnp.zeros_like(hidden)
     d_act[...] = jnp.zeros_like(d_act)
@@ -62,6 +68,7 @@
 
     first = core[0] == 0
     scale = float(T * Z * C) ** -0.5
+    slots = [slot_of(at_z[0], z) for z in range(Z)]
 
     def pair(p, carry):
         for which, (lists, units, lo) in enumerate(((out_l, act, T), (in_l, dh, 0))):
@@ -74,10 +81,9 @@
             at = pl.multiple_of((which * CAP + 2 * p) * SUB, 2 * SUB)
             mine = jnp.where(first, both[:, 0], both[:, 1]).astype(keep.dtype)
             others = jnp.where(first, both[:, 1], both[:, 0]).astype(send.dtype)
-            for z in range(Z):
-                step = lax.rem(z + Z - at_z[0], Z)
-                keep[step, pl.ds(at, 2 * SUB), :] = mine[z]
-                send[step, pl.ds(at, 2 * SUB), :] = others[z]
+            for z, slot in enumerate(slots):
+                keep[slot, pl.ds(at, 2 * SUB), :] = mine[z]
+                send[slot, pl.ds(at, 2 * SUB), :] = others[z]
         return carry
 
     lax.fori_loop(0, CAP // 2, pair, 0, unroll=4)
@@ -97,15 +103,22 @@
     out[...] = total[...].astype(out.dtype)
 
 
-def pair_kernel(keep, got, *outs):
-    for step, out in enumerate(outs):
-        both = keep[step].astype(jnp.float32) + got[step].astype(jnp.float32)
+def cores_kernel(keep, got, near, far):
+    for slot in range(Z):
+        both = keep[slot].astype(jnp.float32) + got[slot].astype(jnp.float32)
+        out = near if slot < Z // 2 else far
+        out[slot % (Z // 2)] = both.astype(out.dtype)
+
+
+def pairs_kernel(near, got, *outs):
+    for slot, out in enumerate(outs):
+        both = near[slot].astype(jnp.float32) + got[slot].astype(jnp.float32)
         out[...] = both.astype(out.dtype)
 
 
 SMEM = pl.BlockSpec(memory_space=pltpu.SMEM)
 VMEM = pl.BlockSpec(memory_space=pltpu.VMEM)
-LIMIT = pltpu.CompilerParams(vmem_limit_bytes=48 * 1024 * 1024)
+LIMIT = pltpu.CompilerParams(vmem_limit_bytes=24 * 1024 * 1024)
 
 
 def units_call(at_z, core, in_l, out_l, xg, w_in, w_out, interpret=False):
@@ -135,15 +148,14 @@
     )(in_l, out_l, act, dh, w_in, w_out)
 
 
-def pair_call(keep, got):
-    out = jax.ShapeDtypeStruct(keep.shape[1:], keep.dtype)
+def add_call(kernel, one, other, outs):
     return pl.pallas_call(
-        pair_kernel,
-        out_shape=(out,) * Z,
+        kernel,
+        out_shape=tuple(jax.ShapeDtypeStruct(dims, one.dtype) for dims in outs),
         in_specs=[VMEM] * 2,
-        out_specs=[VMEM] * Z,
+        out_specs=[VMEM] * len(outs),
         compiler_params=LIMIT,
-    )(keep, got)
+    )(one, other)
 
 
 def exchange(x, axis):
@@ -158,27 +170,29 @@
     bf, f32 = jnp.bfloat16, jnp.float32
     in_l, out_l = in_lists.reshape(-1), out_lists.reshape(-1)
     own = jnp.concatenate([tokens.T, cotangent.T], axis=1)
+    core = lax.axis_index("c").astype(jnp.int32).reshape(1)
+    at_z = lax.axis_index("z").astype(jnp.int32).reshape(1)
+    own, in_l, out_l, core, at_z = lax.optimization_barrier((own, in_l, out_l, core, at_z))
     along_y = spread(own, "y", Y).reshape(Y * OWN, 2 * T)
     xg = spread(along_y, "x", X).reshape(FEAT, 2 * T)
-    core = lax.axis_index("c").astype(jnp.int32).reshape(1)
-    at_z = lax.axis_index("z").astype(jnp.int32).reshape(1)
     keep, send, act, dh = units_call(at_z, core, in_l, out_l, xg, in_blocks, out_blocks)
     got = lax.ppermute(send, "c", [(0, 1), (1, 0)])
     parts = partials_call(in_l, out_l, act, dh, in_blocks, out_blocks)
-    steps = pair_call(keep, got)
-    steps, parts = lax.optimization_barrier((steps, parts))
+    half = (Z // 2,) + keep.shape[1:]
+    near, far = add_call(cores_kernel, keep, got, (half, half))
+    near, far, parts = lax.optimization_barrier((near, far, parts))
     parts = exchange(parts.reshape(X, Y * OWN, 2 * T), "x")
-
-    def along_z(step):
-        return lax.ppermute(steps[step], "z", [(z, (z + step) % Z) for z in range(Z)])
-
-    early = [along_z(step) for step in range(2, Z - 1)]
-    parts, early = lax.optimization_barrier((parts, early))
-    moved = [*early, along_z(1), along_z(Z - 1)]
+    got = lax.ppermute(far, "z", [(z, z ^ 1) for z in range(Z)])
+    parts, got = lax.optimization_barrier((parts, got))
+    own, *steps = add_call(pairs_kernel, near, got, (half[1:],) * (Z // 2))
+    moved = [
+        lax.ppermute(step, "z", [(z, (z + 2 * k) % Z) for z in range(Z)])
+        for k, step in enumerate(steps, 1)
+    ]
     parts = jnp.sum(parts.astype(f32), axis=0).astype(bf)
     parts = exchange(parts.reshape(Y, OWN, 2 * T), "y")
     sums = jnp.sum(parts.astype(f32), axis=0).astype(bf)
-    grads = sum((m.astype(f32) for m in moved), steps[0].astype(f32))
+    grads = sum((m.astype(f32) for m in moved), own.astype(f32))
     grads = grads.astype(bf).reshape(2, CAP, SUB, BLK)
     return sums[:, :T].T, sums[:, T:].T, grads[1], grads[0]
 

time: 155 us -> 152 us (0.981)
  blocking collectives: 25.3 us -> 60.1 us
  waiting for transfers between devices: 57.6 us -> 38.1 us
  starting transfers between devices: 51.7 us -> 35.3 us
    all_to_all x1 -> x2, blocking collectives: 25.3 us -> 60.1 us  [exchange(): return lax.all_to_all(x, axis, split_axis=0, concat_axis=0)]
    all_to_all x3 -> x2, waiting for transfers between devices: 40.5 us -> 15.8 us  [exchange(): return lax.all_to_all(x, axis, split_axis=0, concat_axis=0)]
    ppermute x7 -> x4, starting transfers between devices: 33 us -> 22 us  [the longest x3 18 us: body(): lax.ppermute(step, 'z', [(z, (z + 2 * k) % Z) for z in range(Z)])]
    all_to_all x3 -> x2, starting transfers between devices: 13.5 us -> 8.1 us  [exchange(): return lax.all_to_all(x, axis, split_axis=0, concat_axis=0)]
    ppermute x7 -> x4, waiting for transfers between devices: 17.1 us -> 22.3 us  [the longest x1 12.4 us: body(): got = lax.ppermute(far, 'z', [(z, z ^ 1) for z in range(Z)])]
  transfers between devices with their start and end apart: 11 -> 7, of which waited for: 8 -> 4; matrix products, arithmetic and copies ran while one was open for 1% -> 0% of each run, Pallas kernels for 3% -> 3%
where the time goes in v4:
time: 152 us; the launch traced here: 151 us
  blocking collectives  60.1 us (40%)
  waiting for transfers between devices  38.1 us (25%)
  starting transfers between devices  35.3 us (23%)
  Pallas kernels  9.53 us (6%)
  other arithmetic  4.15 us (3%)
  local copies, waits for them, and re-layouts  3.29 us (2%)
    all_to_all x2, blocking collectives, exchange(): return lax.all_to_all(x, axis, split_axis=0, concat_axis=0)  60.1 us
    ppermute x3, starting transfers between devices, body(): lax.ppermute(step, 'z', [(z, (z + 2 * k) % Z) for z in range(Z)])  18 us
    all_to_all x2, waiting for transfers between devices, exchange(): return lax.all_to_all(x, axis, split_axis=0, concat_axis=0)  15.8 us
    ppermute x1, waiting for transfers between devices, body(): got = lax.ppermute(far, 'z', [(z, z ^ 1) for z in range(Z)])  12.4 us
    ppermute x3, waiting for transfers between devices, body(): lax.ppermute(step, 'z', [(z, (z + 2 * k) % Z) for z in range(Z)])  9.94 us
    all_to_all x2, starting transfers between devices, exchange(): return lax.all_to_all(x, axis, split_axis=0, concat_axis=0)  8.1 us
    ppermute x1, starting transfers between devices, body(): got = lax.ppermute(send, 'c', [(0, 1), (1, 0)])  5.22 us
    pallas_call x1, Pallas kernels, units_call(): pl.pallas_call(units_kernel, out_shape=(half, half, rows, rows), in_specs...  4.61 us
  transfers between devices with their start and end apart: 7, of which 4 were waited for; matrix products, arithmetic and copies ran while one was open for 0% of the time, Pallas kernels for 3%

profile of v4, /device:TPU:1, one launch (start us, length us, event | category | flops | bytes accessed | tf_op | source)
XLA Modules:
  0.0 151.3 jit_solution(12956608468579611841)
XLA Ops:
  0.6 0.8 copy.14
  1.5 0.8 copy.15
  2.4 0.8 pad_maximum_fusion
  3.2 25.3 %all_to_all.20 = bf16[8,80,512]{2,1,0:T(8,128)(2,1)S(1)} all-to-all(bf16[8,80,512]{2,1,0:T(8,128)(2,1)S(1)} %broadcast_in_dim.6), channel_id=1, replica_groups=mesh['z'=8,'c'=2,'x'=4,'y'=8] {'y'}, dimensions={0} | all-to-all | bytes 1310720 | tf_op jit(solution)/shard_map/all_to_all | solution.py:162
  28.6 0.2 broadcast_in_dim.15
  28.8 34.8 %all_to_all.21 = bf16[4,640,512]{2,1,0:T(8,128)(2,1)S(1)} all-to-all(bf16[4,640,512]{2,1,0:T(8,128)(2,1)S(1)} %broadcast_in_dim.15), channel_id=1, replica_groups=mesh['z'=8,'c'=2,'x'=4,'y'=8] {'x'}, dimensions={0} | all-to-all | bytes 5242880 | tf_op jit(solution)/shard_map/all_to_all | solution.py:162
  63.6 4.6 %shard_map.93 = (bf16[8,512,128]{2,1,0:T(8,128)(2,1)S(1)}, bf16[8,512,128]{2,1,0:T(8,128)(2,1)S(1)}, bf16[5,128,256]{2,1,0:T(8,128)(2,1)S(1)}, bf16[5,128,256]{2,1,0:T(8,128)(2,1)S(1)}) custom-call(s32[1]{0:T(128)} %bitcast.3.at_z, s32[1]{0:T(128)} %bitcast.2.core, s32[64]{0:T(128)S(1)} %reshape.36.in_l, s32[64]{0:T(128)S(1)} %reshape.37.out_l, ...), custom_call_target="tpu_custom_call" | custom-call | tf_op jit(solution)/shard_map/pallas_call | solution.py:128
  68.2 5.2 %collective-permute-start = (bf16[8,512,128]{2,1,0:T(8,128)(2,1)S(1)}, bf16[8,512,128]{2,1,0:T(8,128)(2,1)S(1)}, u32[]{:S(2)}, u32[]{:S(2)}) collective-permute-start(bf16[8,512,128]{2,1,0:T(8,128)(2,1)S(1)} %get-tuple-element.30), channel_id=1, source_target_pairs={{0,32},{32,0},{1,33},{33,1},{2,34},{34,2},{3,35},{35,3},{4,36},{36... | collective-permute-start | bytes 3145736 | tf_op jit(solution)/shard_map/ppermute | solution.py:179
  73.5 4.6 %shard_map.95 = bf16[2560,512]{1,0:T(8,128)(2,1)} custom-call(s32[64]{0:T(128)S(1)} %reshape.36.in_l, s32[64]{0:T(128)S(1)} %reshape.37.out_l, bf16[5,128,256]{2,1,0:T(8,128)(2,1)S(1)} %get-tuple-element.33.act, bf16[5,128,256]{2,1,0:T(8,128)(2,1)S(1)} %get-tuple-element.34.dh, bf16[32,128,128]{2,1,0:T(8,128)(2,1)S(1)} %copy-done, ...), custom_call_target="tpu_custom_call" | custom-call | tf_op jit(solution)/shard_map/pallas_call | solution.py:140
  78.0 0.2 shard_map.94
  78.3 4.6 %all-to-all-start.2 = ((bf16[4,640,512]{2,1,0:T(8,128)(2,1)}), bf16[4,640,512]{2,1,0:T(8,128)(2,1)}, u32[]{:S(2)}, u32[]{:S(2)}) async-start(bf16[4,640,512]{2,1,0:T(8,128)(2,1)} %bitcast.6), calls=%async_computation.2 | async-start | bytes 5242880 | tf_op jit(solution)/shard_map/all_to_all | solution.py:162
  82.8 4.0 %collective-permute-start.1 = (bf16[4,512,128]{2,1,0:T(8,128)(2,1)S(1)}, bf16[4,512,128]{2,1,0:T(8,128)(2,1)S(1)}, u32[]{:S(2)}, u32[]{:S(2)}) collective-permute-start(bf16[4,512,128]{2,1,0:T(8,128)(2,1)S(1)} %get-tuple-element.36), channel_id=1, source_target_pairs={{0,64},{64,0},{128,192},{192,128},{256,320},{320,256},{384,448},{4... | collective-permute-start | bytes 1572872 | tf_op jit(solution)/shard_map/ppermute | solution.py:185
  86.8 12.4 %collective-permute-done.1.got = bf16[4,512,128]{2,1,0:T(8,128)(2,1)S(1)} collective-permute-done((bf16[4,512,128]{2,1,0:T(8,128)(2,1)S(1)}, bf16[4,512,128]{2,1,0:T(8,128)(2,1)S(1)}, u32[]{:S(2)}, u32[]{:S(2)}) %collective-permute-start.1) | collective-permute-done | bytes 524320 | tf_op jit(solution)/shard_map/ppermute | solution.py:185
  99.2 15.8 %all-to-all-done.2 = bf16[4,640,512]{2,1,0:T(8,128)(2,1)} async-done(((bf16[4,640,512]{2,1,0:T(8,128)(2,1)}), bf16[4,640,512]{2,1,0:T(8,128)(2,1)}, u32[]{:S(2)}, u32[]{:S(2)}) %all-to-all-start.2) | async-done | bytes 2621472 | tf_op jit(solution)/shard_map/all_to_all | solution.py:162
  115.0 3.2 %reduce_sum.24 = bf16[640,512]{1,0:T(8,128)(2,1)} reduce(bf16[4,640,512]{2,1,0:T(8,128)(2,1)} %all-to-all-done.2, bf16[]{:T(256)} %constant.15.clone.1), dimensions={0}, to_apply=%region_0.0 | reduce | flops 983040 | bytes 3276802 | tf_op jit(solution)/shard_map/reduce_sum | solution.py:192
  118.2 3.5 %all-to-all-start.3 = ((bf16[8,80,512]{2,1,0:T(8,128)(2,1)}), bf16[8,80,512]{2,1,0:T(8,128)(2,1)S(1)}, u32[]{:S(2)}, u32[]{:S(2)}) async-start(bf16[8,80,512]{2,1,0:T(8,128)(2,1)} %bitcast.7), calls=%async_computation.3 | async-start | bytes 1310720 | tf_op jit(solution)/shard_map/all_to_all | solution.py:162
  121.7 0.1 shard_map.96
  121.9 5.8 %collective-permute-start.2 = (bf16[512,128]{1,0:T(8,128)(2,1)S(1)}, bf16[512,128]{1,0:T(8,128)(2,1)S(1)}, u32[]{:S(2)}, u32[]{:S(2)}) collective-permute-start(bf16[512,128]{1,0:T(8,128)(2,1)S(1)} %get-tuple-element.41), channel_id=1, source_target_pairs={{0,128},{64,192},{128,256},{192,320},{256,384},{320,448},{384,0},{... | collective-permute-start | bytes 393224 | tf_op jit(solution)/shard_map/ppermute | solution.py:189
  127.7 8.8 %collective-permute-start.3 = (bf16[512,128]{1,0:T(8,128)(2,1)S(1)}, bf16[512,128]{1,0:T(8,128)(2,1)S(1)}, u32[]{:S(2)}, u32[]{:S(2)}) collective-permute-start(bf16[512,128]{1,0:T(8,128)(2,1)S(1)} %get-tuple-element.42), channel_id=1, source_target_pairs={{0,256},{64,320},{128,384},{192,448},{256,0},{320,64},{384,128},{4... | collective-permute-start | bytes 393224 | tf_op jit(solution)/shard_map/ppermute | solution.py:189
  136.5 3.4 %collective-permute-start.4 = (bf16[512,128]{1,0:T(8,128)(2,1)S(1)}, bf16[512,128]{1,0:T(8,128)(2,1)S(1)}, u32[]{:S(2)}, u32[]{:S(2)}) collective-permute-start(bf16[512,128]{1,0:T(8,128)(2,1)S(1)} %get-tuple-element.43), channel_id=1, source_target_pairs={{0,384},{64,448},{128,0},{192,64},{256,128},{320,192},{384,256},{4... | collective-permute-start | bytes 393224 | tf_op jit(solution)/shard_map/ppermute | solution.py:189
  139.9 4.8 %collective-permute-done.3 = bf16[512,128]{1,0:T(8,128)(2,1)S(1)} collective-permute-done((bf16[512,128]{1,0:T(8,128)(2,1)S(1)}, bf16[512,128]{1,0:T(8,128)(2,1)S(1)}, u32[]{:S(2)}, u32[]{:S(2)}) %collective-permute-start.3) | collective-permute-done | bytes 131104 | tf_op jit(solution)/shard_map/ppermute | solution.py:189
  144.7 5.1 %collective-permute-done.4 = bf16[512,128]{1,0:T(8,128)(2,1)S(1)} collective-permute-done((bf16[512,128]{1,0:T(8,128)(2,1)S(1)}, bf16[512,128]{1,0:T(8,128)(2,1)S(1)}, u32[]{:S(2)}, u32[]{:S(2)}) %collective-permute-start.4) | collective-permute-done | bytes 131104 | tf_op jit(solution)/shard_map/ppermute | solution.py:189
  149.9 0.7 slice_bitcast_fusion
  150.7 0.6 slice_bitcast_fusion.2
  (12 shorter events, 0.4 us)
Async XLA Ops:
  28.8 34.8 %copy-start = (bf16[32,128,128]{2,1,0:T(8,128)(2,1)S(1)}, bf16[32,128,128]{2,1,0:T(8,128)(2,1)}, u32[]{:S(2)}) copy-start(bf16[32,128,128]{2,1,0:T(8,128)(2,1)} %w_in.3) | copy-start | bytes 3145732
  28.8 34.8 %copy-start.1 = (bf16[32,128,128]{2,1,0:T(8,128)(2,1)S(1)}, bf16[32,128,128]{2,1,0:T(8,128)(2,1)}, u32[]{:S(2)}) copy-start(bf16[32,128,128]{2,1,0:T(8,128)(2,1)} %w_out.3) | copy-start | bytes 3145732
  68.2 9.8 %collective-permute-start = (bf16[8,512,128]{2,1,0:T(8,128)(2,1)S(1)}, bf16[8,512,128]{2,1,0:T(8,128)(2,1)S(1)}, u32[]{:S(2)}, u32[]{:S(2)}) collective-permute-start(bf16[8,512,128]{2,1,0:T(8,128)(2,1)S(1)} %get-tuple-element.30), channel_id=1, source_target_pairs={{0,32},{32,0},{1,33},{33,1},{2,34},{34,2},{3,35},{35,3},{4,36},{36... | collective-permute-start | bytes 3145736 | tf_op jit(solution)/shard_map/ppermute | solution.py:179
  78.3 36.7 %all-to-all-start.2 = ((bf16[4,640,512]{2,1,0:T(8,128)(2,1)}), bf16[4,640,512]{2,1,0:T(8,128)(2,1)}, u32[]{:S(2)}, u32[]{:S(2)}) async-start(bf16[4,640,512]{2,1,0:T(8,128)(2,1)} %bitcast.6), calls=%async_computation.2 | async-start | bytes 5242880 | tf_op jit(solution)/shard_map/all_to_all | solution.py:162
  82.8 16.4 %collective-permute-start.1 = (bf16[4,512,128]{2,1,0:T(8,128)(2,1)S(1)}, bf16[4,512,128]{2,1,0:T(8,128)(2,1)S(1)}, u32[]{:S(2)}, u32[]{:S(2)}) collective-permute-start(bf16[4,512,128]{2,1,0:T(8,128)(2,1)S(1)} %get-tuple-element.36), channel_id=1, source_target_pairs={{0,64},{64,0},{128,192},{192,128},{256,320},{320,256},{384,448},{4... | collective-permute-start | bytes 1572872 | tf_op jit(solution)/shard_map/ppermute | solution.py:185
  118.2 32.4 %all-to-all-start.3 = ((bf16[8,80,512]{2,1,0:T(8,128)(2,1)}), bf16[8,80,512]{2,1,0:T(8,128)(2,1)S(1)}, u32[]{:S(2)}, u32[]{:S(2)}) async-start(bf16[8,80,512]{2,1,0:T(8,128)(2,1)} %bitcast.7), calls=%async_computation.3 | async-start | bytes 1310720 | tf_op jit(solution)/shard_map/all_to_all | solution.py:162
  121.9 18.1 %collective-permute-start.2 = (bf16[512,128]{1,0:T(8,128)(2,1)S(1)}, bf16[512,128]{1,0:T(8,128)(2,1)S(1)}, u32[]{:S(2)}, u32[]{:S(2)}) collective-permute-start(bf16[512,128]{1,0:T(8,128)(2,1)S(1)} %get-tuple-element.41), channel_id=1, source_target_pairs={{0,128},{64,192},{128,256},{192,320},{256,384},{320,448},{384,0},{... | collective-permute-start | bytes 393224 | tf_op jit(solution)/shard_map/ppermute | solution.py:189
  127.7 17.0 %collective-permute-start.3 = (bf16[512,128]{1,0:T(8,128)(2,1)S(1)}, bf16[512,128]{1,0:T(8,128)(2,1)S(1)}, u32[]{:S(2)}, u32[]{:S(2)}) collective-permute-start(bf16[512,128]{1,0:T(8,128)(2,1)S(1)} %get-tuple-element.42), channel_id=1, source_target_pairs={{0,256},{64,320},{128,384},{192,448},{256,0},{320,64},{384,128},{4... | collective-permute-start | bytes 393224 | tf_op jit(solution)/shard_map/ppermute | solution.py:189
  136.5 13.3 %collective-permute-start.4 = (bf16[512,128]{1,0:T(8,128)(2,1)S(1)}, bf16[512,128]{1,0:T(8,128)(2,1)S(1)}, u32[]{:S(2)}, u32[]{:S(2)}) collective-permute-start(bf16[512,128]{1,0:T(8,128)(2,1)S(1)} %get-tuple-element.43), channel_id=1, source_target_pairs={{0,384},{64,448},{128,0},{192,64},{256,128},{320,192},{384,256},{4... | collective-permute-start | bytes 393224 | tf_op jit(solution)/shard_map/ppermute | solution.py:189

commit v5 on v1

v5 whole, which is shorter than its diff:
```python
import math

import jax
import jax.numpy as jnp
from jax import lax
from jax.experimental import pallas as pl
from jax.experimental.pallas import tpu as pltpu
from jax.sharding import Mesh
from jax.sharding import PartitionSpec as P

Z, C, X, Y = 8, 2, 4, 8
BLK = 128
CAP = 32
ROWS = 5
COLS = 20
T = 256
FEAT = COLS * BLK
OWN = FEAT // (X * Y)
SUB = BLK // (Z * C)
NEAR = 4
FAR = X * Y // NEAR
HALF = Z // 2
UNITS = (ROWS, BLK, T)
STEP = (2 * CAP * SUB, BLK)

ROOT_COEFF = math.sqrt(2.0 / math.pi)
CUBIC_COEFF = 0.044715


def owner_at(core, near, far):
    x = lax.rem(2 * (far // (Y // 2)) + near // 2 + core, X)
    y = lax.rem(2 * (far % (Y // 2)) + near % 2 + core, Y)
    return x * Y + y


def device_at(core, near, far):
    x = (2 * (far // (Y // 2)) + near // 2 + core) % X
    y = (2 * (far % (Y // 2)) + near % 2 + core) % Y
    return (core * X + x) * Y + y


NEAR_GROUPS = [[device_at(c, n, f) for n in range(NEAR)] for c in range(C) for f in range(FAR)]
FAR_GROUPS = [[device_at(c, n, f) for f in range(FAR)] for c in range(C) for n in range(NEAR)]


def slot_of(z, target):
    odd = lax.rem(target + Z - z, 2)
    base = z + odd * (1 - 2 * lax.rem(z, 2))
    return odd * HALF + lax.rem(target + Z - base, Z) // 2


def gelu_pair(pre):
    tanh_val = jnp.tanh(ROOT_COEFF * (pre + CUBIC_COEFF * pre * pre * pre))
    values = 0.5 * pre * (1.0 + tanh_val)
    slopes = 0.5 * (1.0 + tanh_val) + 0.5 * pre * (1.0 - tanh_val * tanh_val) * ROOT_COEFF * (
        1.0 + 3.0 * CUBIC_COEFF * pre * pre
    )
    return values, slopes


def dot(a, b, dims):
    return lax.dot_general(a, b, (dims, ((), ())), preferred_element_type=jnp.float32)


def place(lists, s):
    row, col = lists[0, s], lists[1, s]
    live = jnp.where(row >= 0, 1.0, 0.0).astype(jnp.float32)
    row = jnp.maximum(row, 0)
    return row, pl.multiple_of(jnp.maximum(col, 0) * BLK, BLK), live


def features(core, near, far):
    return pl.ds(pl.multiple_of(owner_at(core, near, far) * OWN, OWN), OWN)


def units_kernel(where, in_l, out_l, parts, w_in, w_out, keep, send, act, dh, xg, hidden, d_act):
    core, z = where[0], where[1]
    for near in range(NEAR):
        for far in range(FAR):
            xg[features(core, near, far), :] = parts[near, far]
    hidden[...] = jnp.zeros_like(hidden)
    d_act[...] = jnp.zeros_like(d_act)

    def product(s, carry):
        row, col, live = place(in_l, s)
        hidden[row] += dot(w_in[s], xg[pl.ds(col, BLK), :T], ((1,), (0,))) * live
        row, col, live = place(out_l, s)
        d_act[row] += dot(w_out[s], xg[pl.ds(col, BLK), T:], ((1,), (0,))) * live
        return carry

    lax.fori_loop(0, CAP, product, 0, unroll=8)
    for row in range(ROWS):
        values, slopes = gelu_pair(hidden[row])
        act[row] = values.astype(act.dtype)
        dh[row] = (d_act[row] * slopes).astype(dh.dtype)

    first = core == 0
    scale = float(T * Z * C) ** -0.5
    slots = [
        [slot_of(lax.rem(z + Z - c, Z), lax.rem(target + Z - c, Z)) for target in range(Z)]
        for c in (core, 1 - core)
    ]

    def pair(p, carry):
        for which, (lists, units, lo) in enumerate(((out_l, act, T), (in_l, dh, 0))):
            two = []
            for i in range(2):
                row, col, live = place(lists, 2 * p + i)
                part = dot(units[row], xg[pl.ds(col, BLK), lo : lo + T], ((1,), (1,)))
                two.append((part * (live * scale)).reshape(Z, C, SUB, BLK))
            both = jnp.stack(two, axis=2).reshape(Z, C, 2 * SUB, BLK)
            at = pl.multiple_of((which * CAP + 2 * p) * SUB, 2 * SUB)
            mine = jnp.where(first, both[:, 0], both[:, 1]).astype(keep.dtype)
            others = jnp.where(first, both[:, 1], both[:, 0]).astype(send.dtype)
            for target in range(Z):
                keep[slots[0][target], pl.ds(at, 2 * SUB), :] = mine[target]
                send[slots[1][target], pl.ds(at, 2 * SUB), :] = others[target]
        return carry

    lax.fori_loop(0, CAP // 2, pair, 0, unroll=4)


def add_products(lists, units, weights, total):
    total[...] = jnp.zeros_like(total)

    def product(s, carry):
        row, col, live = place(lists, s)
        total[pl.ds(col, BLK), :] += dot(weights[s], units[row], ((0,), (0,))) * live
        return carry

    lax.fori_loop(0, CAP, product, 0, unroll=8)


def output_kernel(lists, act, w_out, part, total):
    add_products(lists, act, w_out, total)
    part[...] = total[...].astype(part.dtype)


def partials_kernel(where, lists, dh, w_in, y_part, parts, total):
    add_products(lists, dh, w_in, total)
    for near in range(NEAR):
        for far in range(FAR):
            rows = features(where[0], near, far)
            parts[near, far, :, :T] = y_part[rows, :]
            parts[near, far, :, T:] = total[rows, :].astype(parts.dtype)


def cores_kernel(keep, got, near, far):
    for slot in range(Z):
        both = keep[slot].astype(jnp.float32) + got[slot].astype(jnp.float32)
        out = near if slot < HALF else far
        out[slot % HALF] = both.astype(out.dtype)


def pairs_kernel(near, got, *outs):
    for slot, out in enumerate(outs):
        both = near[slot].astype(jnp.float32) + got[slot].astype(jnp.float32)
        out[...] = both.astype(out.dtype)


def last_kernel(*refs):
    *moved, out_grad, in_grad = refs
    rows = CAP * SUB
    for i, grad in enumerate((out_grad, in_grad)):
        part = slice(i * rows, (i + 1) * rows)
        grad[...] = sum(m[part, :].astype(jnp.float32) for m in moved).astype(grad.dtype)


def near_sum_kernel(parts, out):
    for far in range(FAR):
        total = sum(parts[near, far].astype(jnp.float32) for near in range(NEAR))
        out[far] = total.astype(out.dtype)


def far_sum_kernel(parts, y, dx):
    total = sum(parts[far].astype(jnp.float32) for far in range(FAR)).astype(y.dtype)
    y[...] = total[:, :T]
    dx[...] = total[:, T:]


SMEM = pl.BlockSpec(memory_space=pltpu.SMEM)
VMEM = pl.BlockSpec(memory_space=pltpu.VMEM)
LIMIT = pltpu.CompilerParams(vmem_limit_bytes=24 * 1024 * 1024)
INTERPRET = False


def call(kernel, scalars, arrays, outs, scratch=()):
    bf = jnp.bfloat16
    return pl.pallas_call(
        kernel,
        out_shape=tuple(jax.ShapeDtypeStruct(dims, bf) for dims in outs),
        in_specs=[SMEM] * len(scalars) + [VMEM] * len(arrays),
        out_specs=[VMEM] * len(outs),
        scratch_shapes=[pltpu.VMEM(*dims) for dims in scratch],
        compiler_params=LIMIT,
        interpret=INTERPRET,
    )(*scalars, *arrays)


def units_call(where, in_l, out_l, parts, w_in, w_out):
    f32 = jnp.float32
    scratch = (((FEAT, 2 * T), jnp.bfloat16), (UNITS, f32), (UNITS, f32))
    outs = ((Z,) + STEP, (Z,) + STEP, UNITS, UNITS)
    return call(units_kernel, (where, in_l, out_l), (parts, w_in, w_out), outs, scratch)


def output_call(lists, act, w_out):
    scratch = (((FEAT, T), jnp.float32),)
    return call(output_kernel, (lists,), (act, w_out), ((FEAT, T),), scratch)[0]


def partials_call(where, lists, dh, w_in, y_part):
    scratch = (((FEAT, T), jnp.float32),)
    outs = ((NEAR, FAR, OWN, 2 * T),)
    return call(partials_kernel, (where, lists), (dh, w_in, y_part), outs, scratch)[0]


def exchange(x, groups):
    return lax.all_to_all(
        x, ("c", "x", "y"), split_axis=0, concat_axis=0, axis_index_groups=groups
    )


def spread(x, groups):
    return exchange(jnp.broadcast_to(x[None], (len(groups[0]),) + x.shape), groups)


def neighbour(z, c):
    return ((z - c) % Z ^ 1) + c


def body(tokens, cotangent, in_blocks, in_lists, out_blocks, out_lists):
    in_l, out_l = in_lists.T, out_lists.T
    own = jnp.concatenate([tokens.T, cotangent.T], axis=1)
    where = jnp.stack([lax.axis_index("c"), lax.axis_index("z")]).astype(jnp.int32)
    own, where = lax.optimization_barrier((own, where))
    parts = spread(spread(own, FAR_GROUPS), NEAR_GROUPS)
    keep, send, act, dh = units_call(where, in_l, out_l, parts, in_blocks, out_blocks)
    got = lax.ppermute(send, "c", [(0, 1), (1, 0)])
    y_part = output_call(out_l, act, out_blocks)
    y_part, got = lax.optimization_barrier((y_part, got))
    near, far = call(cores_kernel, (), (keep, got), ((HALF,) + STEP,) * 2)
    near, far, dh = lax.optimization_barrier((near, far, dh))
    pairs = [
        (z * C + c, neighbour(z, c) % Z * C + c) for z in range(Z) for c in range(C)
    ]
    got = lax.ppermute(far, ("z", "c"), pairs)
    parts = partials_call(where, in_l, dh, in_blocks, y_part)
    parts = exchange(parts, NEAR_GROUPS)
    own, *steps = call(pairs_kernel, (), (near, got), (STEP,) * HALF)
    moved = [
        lax.ppermute(step, "z", [(z, (z + 2 * k) % Z) for z in range(Z)])
        for k, step in enumerate(steps, 1)
    ]
    parts, moved[0], moved[1] = lax.optimization_barrier((parts, moved[0], moved[1]))
    (parts,) = call(near_sum_kernel, (), (parts,), ((FAR, OWN, 2 * T),))
    parts = exchange(parts, FAR_GROUPS)
    y, dx = call(far_sum_kernel, (), (parts,), ((OWN, T),) * 2)
    grads = call(last_kernel, (), (own, *moved), ((CAP * SUB, BLK),) * 2)
    out_grad, in_grad = (grad.reshape(CAP, SUB, BLK) for grad in grads)
    return y.T, dx.T, in_grad, out_grad


def solution(mesh):
    fine = Mesh(mesh.devices.reshape(Z, C, X, Y), ("z", "c", "x", "y"))
    dp, mp = ("z", "c"), ("x", "y")
    blocks, lists = P(mp, None, None), P(mp, None)
    return jax.shard_map(
        body,
        mesh=fine,
        in_specs=(P(dp, mp), P(dp, mp), blocks, lists, blocks, lists),
        out_specs=(P(dp, mp), P(dp, mp), P(mp, dp, None), P(mp, dp, None)),
        check_vma=False,
    )
```

time: 157 us -> 136 us (0.87)
  waiting for transfers between devices: 80.8 us -> 27.1 us
  blocking collectives: 25.3 us -> 49.7 us
  starting transfers between devices: 17.8 us -> 40.4 us
  between operations: 14.1 us -> 0.79 us
  other arithmetic: 3.56 us -> 0.88 us
  Pallas kernels: 10.4 us -> 12.5 us
    all_to_all x3 -> x2, waiting for transfers between devices: 75.1 us -> 7.06 us  [exchange(): lax.all_to_all(x, ('c', 'x', 'y'), split_axis=0, concat_axis=0, axis_inde...]
    all_to_all x1 -> x2, blocking collectives: 25.3 us -> 49.7 us  [exchange(): lax.all_to_all(x, ('c', 'x', 'y'), split_axis=0, concat_axis=0, axis_inde...]
    ppermute x0 -> x4, starting transfers between devices: none -> 22.3 us  [the longest x3 11.6 us: body(): lax.ppermute(step, 'z', [(z, (z + 2 * k) % Z) for z in range(Z)])]
    ppermute x0 -> x4, waiting for transfers between devices: none -> 20 us  [the longest x3 13.2 us: body(): lax.ppermute(step, 'z', [(z, (z + 2 * k) % Z) for z in range(Z)])]
    reduce_scatter x1 -> x0, waiting for transfers between devices: 5.1 us -> none  [body(): grads = lax.psum_scatter(grads, 'z', scatter_dimension=0)]
    unnamed x10 -> x16, local copies, waits for them, and re-layouts: 0.19 us -> 2.95 us
    pallas_call x2 -> x8, Pallas kernels: 10.4 us -> 12.5 us  [call(): pl.pallas_call(kernel, out_shape=tuple((jax.ShapeDtypeStruct(dims, bf) fo...]
    all_to_all x3 -> x2, starting transfers between devices: 12.6 us -> 12.1 us  [exchange(): lax.all_to_all(x, ('c', 'x', 'y'), split_axis=0, concat_axis=0, axis_inde...]
  transfers between devices with their start and end apart: 5 -> 7, of which waited for: 4 -> 5; matrix products, arithmetic and copies ran while one was open for 2% -> 0% of each run, Pallas kernels for 3% -> 2%
where the time goes in v5:
time: 136 us; the launch traced here: 135 us
  blocking collectives  49.7 us (37%)
  starting transfers between devices  40.4 us (30%)
  waiting for transfers between devices  27.1 us (20%)
  Pallas kernels  12.5 us (9%)
  local copies, waits for them, and re-layouts  3.29 us (2%)
    all_to_all x2, blocking collectives, exchange(): lax.all_to_all(x, ('c', 'x', 'y'), split_axis=0, concat_axis=0, axis_inde...  49.7 us
    ppermute x3, waiting for transfers between devices, body(): lax.ppermute(step, 'z', [(z, (z + 2 * k) % Z) for z in range(Z)])  13.2 us
    pallas_call x8, Pallas kernels, call(): pl.pallas_call(kernel, out_shape=tuple((jax.ShapeDtypeStruct(dims, bf) fo...  12.5 us
    all_to_all x2, starting transfers between devices, exchange(): lax.all_to_all(x, ('c', 'x', 'y'), split_axis=0, concat_axis=0, axis_inde...  12.1 us
    ppermute x3, starting transfers between devices, body(): lax.ppermute(step, 'z', [(z, (z + 2 * k) % Z) for z in range(Z)])  11.6 us
    ppermute x1, starting transfers between devices, body(): got = lax.ppermute(far, ('z', 'c'), pairs)  10.7 us
    all_to_all x2, waiting for transfers between devices, exchange(): lax.all_to_all(x, ('c', 'x', 'y'), split_axis=0, concat_axis=0, axis_inde...  7.06 us
    ppermute x1, waiting for transfers between devices, body(): got = lax.ppermute(far, ('z', 'c'), pairs)  6.77 us
  transfers between devices with their start and end apart: 7, of which 5 were waited for; matrix products, arithmetic and copies ran while one was open for 0% of the time, Pallas kernels for 2%

profile of v5, /device:TPU:1, one launch (start us, length us, event | category | flops | bytes accessed | tf_op | source)
XLA Modules:
  0.0 134.7 jit_solution(18123994688465099509)
XLA Ops:
  0.7 0.8 pad_maximum_fusion
  1.6 28.0 %all_to_all.20 = bf16[8,80,512]{2,1,0:T(8,128)(2,1)S(1)} all-to-all(bf16[8,80,512]{2,1,0:T(8,128)(2,1)S(1)} %broadcast_in_dim.4), channel_id=1, replica_groups={{0,2,4,6,16,18,20,22},{1,3,5,7,17,19,21,23},{8,10,12,14,24,26,28,30},{9..., dimensions={0} | all-to-all | bytes 1310720 | tf_op jit(solution)/shard_map/all_to_all | solution.py:219
  29.9 21.7 %all_to_all.21.parts = bf16[4,8,80,512]{3,2,1,0:T(8,128)(2,1)S(1)} all-to-all(bf16[4,8,80,512]{3,2,1,0:T(8,128)(2,1)S(1)} %broadcast_in_dim.5), channel_id=1, replica_groups={{0,1,8,9},{2,3,10,11},{4,5,12,13},{6,7,14,15},{16,17,24,25},{18,19,26,2..., dimensions={0} | all-to-all | bytes 5242880 | tf_op jit(solution)/shard_map/all_to_all | solution.py:219
  51.6 5.1 %shard_map.93 = (bf16[8,512,128]{2,1,0:T(8,128)(2,1)S(1)}, bf16[8,512,128]{2,1,0:T(8,128)(2,1)S(1)}, bf16[5,128,256]{2,1,0:T(8,128)(2,1)S(1)}, bf16[5,128,256]{2,1,0:T(8,128)(2,1)S(1)}) custom-call(s32[2]{0:T(128)S(1)} %pad_add_fusion.where, s32[2,32]{1,0:T(2,128)S(1)} %bitcast.12, s32[2,32]{1,0:T(2,128)S(1)} %bitcast.10, ...), custom_call_target="tpu_custom_call" | custom-call | tf_op jit(solution)/shard_map/pallas_call | solution.py:189
  56.7 6.1 %collective-permute-start = (bf16[8,512,128]{2,1,0:T(8,128)(2,1)S(1)}, bf16[8,512,128]{2,1,0:T(8,128)(2,1)S(1)}, u32[]{:S(2)}, u32[]{:S(2)}) collective-permute-start(bf16[8,512,128]{2,1,0:T(8,128)(2,1)S(1)} %get-tuple-element.32), channel_id=1, source_target_pairs={{0,32},{32,0},{1,33},{33,1},{2,34},{34,2},{3,35},{35,3},{4,36},{36... | collective-permute-start | bytes 3145736 | tf_op jit(solution)/shard_map/ppermute | solution.py:239
  62.8 2.2 %shard_map.94.y_part = bf16[2560,256]{1,0:T(8,128)(2,1)S(1)} custom-call(s32[2,32]{1,0:T(2,128)S(1)} %bitcast.11, bf16[5,128,256]{2,1,0:T(8,128)(2,1)S(1)} %get-tuple-element.31.act, bf16[32,128,128]{2,1,0:T(8,128)(2,1)S(1)} %copy-done.1), custom_call_target="tpu_custom_call" | custom-call | tf_op jit(solution)/shard_map/pallas_call | solution.py:189
  65.3 0.8 copy-done.5
  66.1 2.3 %shard_map.96 = bf16[4,8,80,512]{3,2,1,0:T(8,128)(2,1)S(1)} custom-call(s32[2]{0:T(128)S(1)} %pad_add_fusion.where, s32[2,32]{1,0:T(2,128)S(1)} %bitcast.13, bf16[5,128,256]{2,1,0:T(8,128)(2,1)S(1)} %get-tuple-element.37.dh, bf16[32,128,128]{2,1,0:T(8,128)(2,1)S(1)} %copy-done.2, bf16[2560,256]{1,0:T(8,128)(2,1)S(1)} %shard_map.94.y_part), custom_call_target="tpu_custom_call" | custom-call | tf_op jit(solution)/shard_map/pallas_call | solution.py:189
  68.4 1.5 %copy-done = bf16[4,8,80,512]{3,2,1,0:T(8,128)(2,1)} copy-done((bf16[4,8,80,512]{3,2,1,0:T(8,128)(2,1)}, bf16[4,8,80,512]{3,2,1,0:T(8,128)(2,1)S(1)}, u32[]{:S(2)}) %copy-start) | copy-done | bytes 2621464
  69.9 6.1 %all-to-all-start.2 = ((bf16[4,8,80,512]{3,2,1,0:T(8,128)(2,1)}), bf16[4,8,80,512]{3,2,1,0:T(8,128)(2,1)S(1)}, u32[]{:S(2)}, u32[]{:S(2)}) async-start(bf16[4,8,80,512]{3,2,1,0:T(8,128)(2,1)} %copy-done), calls=%async_computation.2 | async-start | bytes 5242880 | tf_op jit(solution)/shard_map/all_to_all | solution.py:219
  75.9 10.7 %collective-permute-start.1 = (bf16[4,512,128]{2,1,0:T(8,128)(2,1)}, bf16[4,512,128]{2,1,0:T(8,128)(2,1)S(1)}, u32[]{:S(2)}, u32[]{:S(2)}) collective-permute-start(bf16[4,512,128]{2,1,0:T(8,128)(2,1)} %copy-done.5), channel_id=1, source_target_pairs={{0,64},{32,480},{64,0},{96,160},{128,192},{160,96},{192,128},{224,... | collective-permute-start | bytes 1572872 | tf_op jit(solution)/shard_map/ppermute | solution.py:247
  86.6 6.8 %collective-permute-done.1.got = bf16[4,512,128]{2,1,0:T(8,128)(2,1)S(1)} collective-permute-done((bf16[4,512,128]{2,1,0:T(8,128)(2,1)}, bf16[4,512,128]{2,1,0:T(8,128)(2,1)S(1)}, u32[]{:S(2)}, u32[]{:S(2)}) %collective-permute-start.1) | collective-permute-done | bytes 524320 | tf_op jit(solution)/shard_map/ppermute | solution.py:247
  93.5 0.6 copy-done.6
  94.1 2.0 %collective-permute-start.2 = (bf16[512,128]{1,0:T(8,128)(2,1)S(1)}, bf16[512,128]{1,0:T(8,128)(2,1)S(1)}, u32[]{:S(2)}, u32[]{:S(2)}) collective-permute-start(bf16[512,128]{1,0:T(8,128)(2,1)S(1)} %get-tuple-element.41), channel_id=1, source_target_pairs={{0,128},{64,192},{128,256},{192,320},{256,384},{320,448},{384,0},{... | collective-permute-start | bytes 393224 | tf_op jit(solution)/shard_map/ppermute | solution.py:252
  96.2 5.7 %collective-permute-start.3 = (bf16[512,128]{1,0:T(8,128)(2,1)S(1)}, bf16[512,128]{1,0:T(8,128)(2,1)S(1)}, u32[]{:S(2)}, u32[]{:S(2)}) collective-permute-start(bf16[512,128]{1,0:T(8,128)(2,1)S(1)} %get-tuple-element.42), channel_id=1, source_target_pairs={{0,256},{64,320},{128,384},{192,448},{256,0},{320,64},{384,128},{4... | collective-permute-start | bytes 393224 | tf_op jit(solution)/shard_map/ppermute | solution.py:252
  101.9 1.2 collective-permute-done.2.refs_1_
  103.1 6.6 %collective-permute-done.3.refs_2_ = bf16[512,128]{1,0:T(8,128)(2,1)S(1)} collective-permute-done((bf16[512,128]{1,0:T(8,128)(2,1)S(1)}, bf16[512,128]{1,0:T(8,128)(2,1)S(1)}, u32[]{:S(2)}, u32[]{:S(2)}) %collective-permute-start.3) | collective-permute-done | bytes 131104 | tf_op jit(solution)/shard_map/ppermute | solution.py:252
  109.7 1.2 shard_map.98
  110.9 6.0 %all-to-all-start.3 = ((bf16[8,80,512]{2,1,0:T(8,128)(2,1)}), bf16[8,80,512]{2,1,0:T(8,128)(2,1)S(1)}, u32[]{:S(2)}, u32[]{:S(2)}) async-start(bf16[8,80,512]{2,1,0:T(8,128)(2,1)} %shard_map.98), calls=%async_computation.3 | async-start | bytes 1310720 | tf_op jit(solution)/shard_map/all_to_all | solution.py:219
  116.9 3.9 %collective-permute-start.4 = (bf16[512,128]{1,0:T(8,128)(2,1)S(1)}, bf16[512,128]{1,0:T(8,128)(2,1)S(1)}, u32[]{:S(2)}, u32[]{:S(2)}) collective-permute-start(bf16[512,128]{1,0:T(8,128)(2,1)S(1)} %copy-done.7), channel_id=1, source_target_pairs={{0,384},{64,448},{128,0},{192,64},{256,128},{320,192},{384,256},{4... | collective-permute-start | bytes 393224 | tf_op jit(solution)/shard_map/ppermute | solution.py:252
  120.8 5.4 %collective-permute-done.4.refs_3_ = bf16[512,128]{1,0:T(8,128)(2,1)S(1)} collective-permute-done((bf16[512,128]{1,0:T(8,128)(2,1)S(1)}, bf16[512,128]{1,0:T(8,128)(2,1)S(1)}, u32[]{:S(2)}, u32[]{:S(2)}) %collective-permute-start.4) | collective-permute-done | bytes 131104 | tf_op jit(solution)/shard_map/ppermute | solution.py:252
  126.2 0.7 shard_map.100
  126.9 7.1 %all-to-all-done.3.parts = bf16[8,80,512]{2,1,0:T(8,128)(2,1)S(1)} async-done(((bf16[8,80,512]{2,1,0:T(8,128)(2,1)}), bf16[8,80,512]{2,1,0:T(8,128)(2,1)S(1)}, u32[]{:S(2)}, u32[]{:S(2)}) %all-to-all-start.3) | async-done | bytes 655392 | tf_op jit(solution)/shard_map/all_to_all | solution.py:219
  134.0 0.7 shard_map.99
  (20 shorter events, 0.9 us)
Async XLA Ops:
  29.9 21.7 %copy-start.1 = (bf16[32,128,128]{2,1,0:T(8,128)(2,1)S(1)}, bf16[32,128,128]{2,1,0:T(8,128)(2,1)}, u32[]{:S(2)}) copy-start(bf16[32,128,128]{2,1,0:T(8,128)(2,1)} %w_out.3) | copy-start | bytes 3145732
  29.9 21.7 %copy-start.2 = (bf16[32,128,128]{2,1,0:T(8,128)(2,1)S(1)}, bf16[32,128,128]{2,1,0:T(8,128)(2,1)}, u32[]{:S(2)}) copy-start(bf16[32,128,128]{2,1,0:T(8,128)(2,1)} %w_in.3) | copy-start | bytes 3145732
  29.9 21.7 %copy-start.3 = (s32[32,2]{0,1:T(2,128)S(1)}, s32[32,2]{0,1:T(2,128)}, u32[]{:S(2)}) copy-start(s32[32,2]{0,1:T(2,128)} %param.11) | copy-start | bytes 772
  29.9 21.7 %copy-start.4 = (s32[32,2]{0,1:T(2,128)S(1)}, s32[32,2]{0,1:T(2,128)}, u32[]{:S(2)}) copy-start(s32[32,2]{0,1:T(2,128)} %param.9) | copy-start | bytes 772
  56.7 8.4 %collective-permute-start = (bf16[8,512,128]{2,1,0:T(8,128)(2,1)S(1)}, bf16[8,512,128]{2,1,0:T(8,128)(2,1)S(1)}, u32[]{:S(2)}, u32[]{:S(2)}) collective-permute-start(bf16[8,512,128]{2,1,0:T(8,128)(2,1)S(1)} %get-tuple-element.32), channel_id=1, source_target_pairs={{0,32},{32,0},{1,33},{33,1},{2,34},{34,2},{3,35},{35,3},{4,36},{36... | collective-permute-start | bytes 3145736 | tf_op jit(solution)/shard_map/ppermute | solution.py:239
  65.3 0.8 copy-start.5
  68.4 1.5 %copy-start = (bf16[4,8,80,512]{3,2,1,0:T(8,128)(2,1)}, bf16[4,8,80,512]{3,2,1,0:T(8,128)(2,1)S(1)}, u32[]{:S(2)}) copy-start(bf16[4,8,80,512]{3,2,1,0:T(8,128)(2,1)S(1)} %shard_map.96) | copy-start | bytes 7864324
  69.9 39.8 %all-to-all-start.2 = ((bf16[4,8,80,512]{3,2,1,0:T(8,128)(2,1)}), bf16[4,8,80,512]{3,2,1,0:T(8,128)(2,1)S(1)}, u32[]{:S(2)}, u32[]{:S(2)}) async-start(bf16[4,8,80,512]{3,2,1,0:T(8,128)(2,1)} %copy-done), calls=%async_computation.2 | async-start | bytes 5242880 | tf_op jit(solution)/shard_map/all_to_all | solution.py:219
  75.9 17.4 %collective-permute-start.1 = (bf16[4,512,128]{2,1,0:T(8,128)(2,1)}, bf16[4,512,128]{2,1,0:T(8,128)(2,1)S(1)}, u32[]{:S(2)}, u32[]{:S(2)}) collective-permute-start(bf16[4,512,128]{2,1,0:T(8,128)(2,1)} %copy-done.5), channel_id=1, source_target_pairs={{0,64},{32,480},{64,0},{96,160},{128,192},{160,96},{192,128},{224,... | collective-permute-start | bytes 1572872 | tf_op jit(solution)/shard_map/ppermute | solution.py:247
  93.5 0.7 copy-start.6
  94.1 22.8 %copy-start.7 = (bf16[512,128]{1,0:T(8,128)(2,1)S(1)}, bf16[512,128]{1,0:T(8,128)(2,1)}, u32[]{:S(2)}) copy-start(bf16[512,128]{1,0:T(8,128)(2,1)} %copy-done.6) | copy-start | bytes 393220
  94.1 9.0 %collective-permute-start.2 = (bf16[512,128]{1,0:T(8,128)(2,1)S(1)}, bf16[512,128]{1,0:T(8,128)(2,1)S(1)}, u32[]{:S(2)}, u32[]{:S(2)}) collective-permute-start(bf16[512,128]{1,0:T(8,128)(2,1)S(1)} %get-tuple-element.41), channel_id=1, source_target_pairs={{0,128},{64,192},{128,256},{192,320},{256,384},{320,448},{384,0},{... | collective-permute-start | bytes 393224 | tf_op jit(solution)/shard_map/ppermute | solution.py:252
  96.2 13.5 %collective-permute-start.3 = (bf16[512,128]{1,0:T(8,128)(2,1)S(1)}, bf16[512,128]{1,0:T(8,128)(2,1)S(1)}, u32[]{:S(2)}, u32[]{:S(2)}) collective-permute-start(bf16[512,128]{1,0:T(8,128)(2,1)S(1)} %get-tuple-element.42), channel_id=1, source_target_pairs={{0,256},{64,320},{128,384},{192,448},{256,0},{320,64},{384,128},{4... | collective-permute-start | bytes 393224 | tf_op jit(solution)/shard_map/ppermute | solution.py:252
  110.9 23.1 %all-to-all-start.3 = ((bf16[8,80,512]{2,1,0:T(8,128)(2,1)}), bf16[8,80,512]{2,1,0:T(8,128)(2,1)S(1)}, u32[]{:S(2)}, u32[]{:S(2)}) async-start(bf16[8,80,512]{2,1,0:T(8,128)(2,1)} %shard_map.98), calls=%async_computation.3 | async-start | bytes 1310720 | tf_op jit(solution)/shard_map/all_to_all | solution.py:219
  116.9 9.3 %collective-permute-start.4 = (bf16[512,128]{1,0:T(8,128)(2,1)S(1)}, bf16[512,128]{1,0:T(8,128)(2,1)S(1)}, u32[]{:S(2)}, u32[]{:S(2)}) collective-permute-start(bf16[512,128]{1,0:T(8,128)(2,1)S(1)} %copy-done.7), channel_id=1, source_target_pairs={{0,384},{64,448},{128,0},{192,64},{256,128},{320,192},{384,256},{4... | collective-permute-start | bytes 393224 | tf_op jit(solution)/shard_map/ppermute | solution.py:252

commit v6 on v5

--- a/solution.py
+++ b/solution.py
@@ -252,7 +252,7 @@
         lax.ppermute(step, "z", [(z, (z + 2 * k) % Z) for z in range(Z)])
         for k, step in enumerate(steps, 1)
     ]
-    parts, moved[0], moved[1] = lax.optimization_barrier((parts, moved[0], moved[1]))
+    parts, moved[1] = lax.optimization_barrier((parts, moved[1]))
     (parts,) = call(near_sum_kernel, (), (parts,), ((FAR, OWN, 2 * T),))
     parts = exchange(parts, FAR_GROUPS)
     y, dx = call(far_sum_kernel, (), (parts,), ((OWN, T),) * 2)

time: 136 us -> 129 us (0.949)
  waiting for transfers between devices: 27.1 us -> 18.5 us
  starting transfers between devices: 40.4 us -> 42.8 us
    ppermute x3, waiting for transfers between devices: 13.2 us -> 8.58 us  [body(): lax.ppermute(step, 'z', [(z, (z + 2 * k) % Z) for z in range(Z)])]
    all_to_all x2, waiting for transfers between devices: 7.06 us -> 3.12 us  [exchange(): lax.all_to_all(x, ('c', 'x', 'y'), split_axis=0, concat_axis=0, axis_inde...]
    all_to_all x2, starting transfers between devices: 12.1 us -> 14.1 us  [exchange(): lax.all_to_all(x, ('c', 'x', 'y'), split_axis=0, concat_axis=0, axis_inde...]
    unnamed x16 -> x12, local copies, waits for them, and re-layouts: 2.95 us -> 2.3 us
  transfers between devices with their start and end apart: 7 -> 7, of which waited for: 5 -> 6; matrix products, arithmetic and copies ran while one was open for 0% -> 0% of each run, Pallas kernels for 2% -> 2%
where the time goes in v6:
time: 129 us; the launch traced here: 128 us
  blocking collectives  49.7 us (39%)
  starting transfers between devices  42.8 us (33%)
  waiting for transfers between devices  18.5 us (14%)
  Pallas kernels  12.5 us (10%)
  local copies, waits for them, and re-layouts  2.65 us (2%)
    all_to_all x2, blocking collectives, exchange(): lax.all_to_all(x, ('c', 'x', 'y'), split_axis=0, concat_axis=0, axis_inde...  49.7 us
    all_to_all x2, starting transfers between devices, exchange(): lax.all_to_all(x, ('c', 'x', 'y'), split_axis=0, concat_axis=0, axis_inde...  14.1 us
    pallas_call x8, Pallas kernels, call(): pl.pallas_call(kernel, out_shape=tuple((jax.ShapeDtypeStruct(dims, bf) fo...  12.5 us
    ppermute x3, starting transfers between devices, body(): lax.ppermute(step, 'z', [(z, (z + 2 * k) % Z) for z in range(Z)])  11.9 us
    ppermute x1, starting transfers between devices, body(): got = lax.ppermute(far, ('z', 'c'), pairs)  10.7 us
    ppermute x3, waiting for transfers between devices, body(): lax.ppermute(step, 'z', [(z, (z + 2 * k) % Z) for z in range(Z)])  8.58 us
    ppermute x1, waiting for transfers between devices, body(): got = lax.ppermute(far, ('z', 'c'), pairs)  6.77 us
    ppermute x1, starting transfers between devices, body(): got = lax.ppermute(send, 'c', [(0, 1), (1, 0)])  6.09 us
  transfers between devices with their start and end apart: 7, of which 6 were waited for; matrix products, arithmetic and copies ran while one was open for 0% of the time, Pallas kernels for 2%

profile of v6, /device:TPU:1, one launch (start us, length us, event | category | flops | bytes accessed | tf_op | source)
XLA Modules:
  0.0 127.8 jit_solution(13259433905494679564)
XLA Ops:
  0.7 0.8 pad_maximum_fusion
  1.6 28.0 %all_to_all.20 = bf16[8,80,512]{2,1,0:T(8,128)(2,1)S(1)} all-to-all(bf16[8,80,512]{2,1,0:T(8,128)(2,1)S(1)} %broadcast_in_dim.4), channel_id=1, replica_groups={{0,2,4,6,16,18,20,22},{1,3,5,7,17,19,21,23},{8,10,12,14,24,26,28,30},{9..., dimensions={0} | all-to-all | bytes 1310720 | tf_op jit(solution)/shard_map/all_to_all | solution.py:219
  29.6 0.3 broadcast_in_dim.5
  29.9 21.7 %all_to_all.21.parts = bf16[4,8,80,512]{3,2,1,0:T(8,128)(2,1)S(1)} all-to-all(bf16[4,8,80,512]{3,2,1,0:T(8,128)(2,1)S(1)} %broadcast_in_dim.5), channel_id=1, replica_groups={{0,1,8,9},{2,3,10,11},{4,5,12,13},{6,7,14,15},{16,17,24,25},{18,19,26,2..., dimensions={0} | all-to-all | bytes 5242880 | tf_op jit(solution)/shard_map/all_to_all | solution.py:219
  51.6 5.0 %shard_map.93 = (bf16[8,512,128]{2,1,0:T(8,128)(2,1)S(1)}, bf16[8,512,128]{2,1,0:T(8,128)(2,1)S(1)}, bf16[5,128,256]{2,1,0:T(8,128)(2,1)S(1)}, bf16[5,128,256]{2,1,0:T(8,128)(2,1)S(1)}) custom-call(s32[2]{0:T(128)S(1)} %pad_add_fusion.where, s32[2,32]{1,0:T(2,128)S(1)} %bitcast.12, s32[2,32]{1,0:T(2,128)S(1)} %bitcast.10, ...), custom_call_target="tpu_custom_call" | custom-call | tf_op jit(solution)/shard_map/pallas_call | solution.py:189
  56.7 6.1 %collective-permute-start = (bf16[8,512,128]{2,1,0:T(8,128)(2,1)S(1)}, bf16[8,512,128]{2,1,0:T(8,128)(2,1)S(1)}, u32[]{:S(2)}, u32[]{:S(2)}) collective-permute-start(bf16[8,512,128]{2,1,0:T(8,128)(2,1)S(1)} %get-tuple-element.31), channel_id=1, source_target_pairs={{0,32},{32,0},{1,33},{33,1},{2,34},{34,2},{3,35},{35,3},{4,36},{36... | collective-permute-start | bytes 3145736 | tf_op jit(solution)/shard_map/ppermute | solution.py:239
  62.8 2.2 %shard_map.94.y_part = bf16[2560,256]{1,0:T(8,128)(2,1)S(1)} custom-call(s32[2,32]{1,0:T(2,128)S(1)} %bitcast.11, bf16[5,128,256]{2,1,0:T(8,128)(2,1)S(1)} %get-tuple-element.30.act, bf16[32,128,128]{2,1,0:T(8,128)(2,1)S(1)} %copy-done.1), custom_call_target="tpu_custom_call" | custom-call | tf_op jit(solution)/shard_map/pallas_call | solution.py:189
  65.3 0.8 copy-done.5
  66.1 2.3 %shard_map.96 = bf16[4,8,80,512]{3,2,1,0:T(8,128)(2,1)S(1)} custom-call(s32[2]{0:T(128)S(1)} %pad_add_fusion.where, s32[2,32]{1,0:T(2,128)S(1)} %bitcast.13, bf16[5,128,256]{2,1,0:T(8,128)(2,1)S(1)} %get-tuple-element.36.dh, bf16[32,128,128]{2,1,0:T(8,128)(2,1)S(1)} %copy-done.2, bf16[2560,256]{1,0:T(8,128)(2,1)S(1)} %shard_map.94.y_part), custom_call_target="tpu_custom_call" | custom-call | tf_op jit(solution)/shard_map/pallas_call | solution.py:189
  68.4 1.5 %copy-done = bf16[4,8,80,512]{3,2,1,0:T(8,128)(2,1)} copy-done((bf16[4,8,80,512]{3,2,1,0:T(8,128)(2,1)}, bf16[4,8,80,512]{3,2,1,0:T(8,128)(2,1)S(1)}, u32[]{:S(2)}) %copy-start) | copy-done | bytes 2621464
  69.9 6.1 %all-to-all-start.2 = ((bf16[4,8,80,512]{3,2,1,0:T(8,128)(2,1)}), bf16[4,8,80,512]{3,2,1,0:T(8,128)(2,1)S(1)}, u32[]{:S(2)}, u32[]{:S(2)}) async-start(bf16[4,8,80,512]{3,2,1,0:T(8,128)(2,1)} %copy-done), calls=%async_computation.2 | async-start | bytes 5242880 | tf_op jit(solution)/shard_map/all_to_all | solution.py:219
  76.0 10.7 %collective-permute-start.1 = (bf16[4,512,128]{2,1,0:T(8,128)(2,1)}, bf16[4,512,128]{2,1,0:T(8,128)(2,1)S(1)}, u32[]{:S(2)}, u32[]{:S(2)}) collective-permute-start(bf16[4,512,128]{2,1,0:T(8,128)(2,1)} %copy-done.5), channel_id=1, source_target_pairs={{0,64},{32,480},{64,0},{96,160},{128,192},{160,96},{192,128},{224,... | collective-permute-start | bytes 1572872 | tf_op jit(solution)/shard_map/ppermute | solution.py:247
  86.6 6.8 %collective-permute-done.1.got = bf16[4,512,128]{2,1,0:T(8,128)(2,1)S(1)} collective-permute-done((bf16[4,512,128]{2,1,0:T(8,128)(2,1)}, bf16[4,512,128]{2,1,0:T(8,128)(2,1)S(1)}, u32[]{:S(2)}, u32[]{:S(2)}) %collective-permute-start.1) | collective-permute-done | bytes 524320 | tf_op jit(solution)/shard_map/ppermute | solution.py:247
  93.5 4.5 %collective-permute-start.2 = (bf16[512,128]{1,0:T(8,128)(2,1)S(1)}, bf16[512,128]{1,0:T(8,128)(2,1)S(1)}, u32[]{:S(2)}, u32[]{:S(2)}) collective-permute-start(bf16[512,128]{1,0:T(8,128)(2,1)S(1)} %get-tuple-element.40), channel_id=1, source_target_pairs={{0,256},{64,320},{128,384},{192,448},{256,0},{320,64},{384,128},{4... | collective-permute-start | bytes 393224 | tf_op jit(solution)/shard_map/ppermute | solution.py:252
  98.1 5.2 %collective-permute-done.2.refs_2_ = bf16[512,128]{1,0:T(8,128)(2,1)S(1)} collective-permute-done((bf16[512,128]{1,0:T(8,128)(2,1)S(1)}, bf16[512,128]{1,0:T(8,128)(2,1)S(1)}, u32[]{:S(2)}, u32[]{:S(2)}) %collective-permute-start.2) | collective-permute-done | bytes 131104 | tf_op jit(solution)/shard_map/ppermute | solution.py:252
  103.2 1.2 shard_map.98
  104.4 8.1 %all-to-all-start.3 = ((bf16[8,80,512]{2,1,0:T(8,128)(2,1)}), bf16[8,80,512]{2,1,0:T(8,128)(2,1)S(1)}, u32[]{:S(2)}, u32[]{:S(2)}) async-start(bf16[8,80,512]{2,1,0:T(8,128)(2,1)} %shard_map.98), calls=%async_computation.3 | async-start | bytes 1310720 | tf_op jit(solution)/shard_map/all_to_all | solution.py:219
  112.5 1.9 %collective-permute-start.3 = (bf16[512,128]{1,0:T(8,128)(2,1)S(1)}, bf16[512,128]{1,0:T(8,128)(2,1)S(1)}, u32[]{:S(2)}, u32[]{:S(2)}) collective-permute-start(bf16[512,128]{1,0:T(8,128)(2,1)S(1)} %get-tuple-element.45), channel_id=1, source_target_pairs={{0,128},{64,192},{128,256},{192,320},{256,384},{320,448},{384,0},{... | collective-permute-start | bytes 393224 | tf_op jit(solution)/shard_map/ppermute | solution.py:252
  114.4 5.5 %collective-permute-start.4 = (bf16[512,128]{1,0:T(8,128)(2,1)S(1)}, bf16[512,128]{1,0:T(8,128)(2,1)S(1)}, u32[]{:S(2)}, u32[]{:S(2)}) collective-permute-start(bf16[512,128]{1,0:T(8,128)(2,1)S(1)} %get-tuple-element.47), channel_id=1, source_target_pairs={{0,384},{64,448},{128,0},{192,64},{256,128},{320,192},{384,256},{4... | collective-permute-start | bytes 393224 | tf_op jit(solution)/shard_map/ppermute | solution.py:252
  119.9 1.9 %collective-permute-done.3.refs_1_ = bf16[512,128]{1,0:T(8,128)(2,1)S(1)} collective-permute-done((bf16[512,128]{1,0:T(8,128)(2,1)S(1)}, bf16[512,128]{1,0:T(8,128)(2,1)S(1)}, u32[]{:S(2)}, u32[]{:S(2)}) %collective-permute-start.3) | collective-permute-done | bytes 131104 | tf_op jit(solution)/shard_map/ppermute | solution.py:252
  121.8 1.5 %collective-permute-done.4.refs_3_ = bf16[512,128]{1,0:T(8,128)(2,1)S(1)} collective-permute-done((bf16[512,128]{1,0:T(8,128)(2,1)S(1)}, bf16[512,128]{1,0:T(8,128)(2,1)S(1)}, u32[]{:S(2)}, u32[]{:S(2)}) %collective-permute-start.4) | collective-permute-done | bytes 131104 | tf_op jit(solution)/shard_map/ppermute | solution.py:252
  123.3 0.7 shard_map.100
  124.0 3.1 %all-to-all-done.3.parts = bf16[8,80,512]{2,1,0:T(8,128)(2,1)S(1)} async-done(((bf16[8,80,512]{2,1,0:T(8,128)(2,1)}), bf16[8,80,512]{2,1,0:T(8,128)(2,1)S(1)}, u32[]{:S(2)}, u32[]{:S(2)}) %all-to-all-start.3) | async-done | bytes 655392 | tf_op jit(solution)/shard_map/all_to_all | solution.py:219
  127.1 0.7 shard_map.99
  (16 shorter events, 0.6 us)
Async XLA Ops:
  29.9 21.7 %copy-start.1 = (bf16[32,128,128]{2,1,0:T(8,128)(2,1)S(1)}, bf16[32,128,128]{2,1,0:T(8,128)(2,1)}, u32[]{:S(2)}) copy-start(bf16[32,128,128]{2,1,0:T(8,128)(2,1)} %w_out.3) | copy-start | bytes 3145732
  29.9 21.7 %copy-start.2 = (bf16[32,128,128]{2,1,0:T(8,128)(2,1)S(1)}, bf16[32,128,128]{2,1,0:T(8,128)(2,1)}, u32[]{:S(2)}) copy-start(bf16[32,128,128]{2,1,0:T(8,128)(2,1)} %w_in.3) | copy-start | bytes 3145732
  29.9 21.7 %copy-start.3 = (s32[32,2]{0,1:T(2,128)S(1)}, s32[32,2]{0,1:T(2,128)}, u32[]{:S(2)}) copy-start(s32[32,2]{0,1:T(2,128)} %param.11) | copy-start | bytes 772
  29.9 21.7 %copy-start.4 = (s32[32,2]{0,1:T(2,128)S(1)}, s32[32,2]{0,1:T(2,128)}, u32[]{:S(2)}) copy-start(s32[32,2]{0,1:T(2,128)} %param.9) | copy-start | bytes 772
  56.7 8.4 %collective-permute-start = (bf16[8,512,128]{2,1,0:T(8,128)(2,1)S(1)}, bf16[8,512,128]{2,1,0:T(8,128)(2,1)S(1)}, u32[]{:S(2)}, u32[]{:S(2)}) collective-permute-start(bf16[8,512,128]{2,1,0:T(8,128)(2,1)S(1)} %get-tuple-element.31), channel_id=1, source_target_pairs={{0,32},{32,0},{1,33},{33,1},{2,34},{34,2},{3,35},{35,3},{4,36},{36... | collective-permute-start | bytes 3145736 | tf_op jit(solution)/shard_map/ppermute | solution.py:239
  65.3 0.8 copy-start.5
  68.4 1.5 %copy-start = (bf16[4,8,80,512]{3,2,1,0:T(8,128)(2,1)}, bf16[4,8,80,512]{3,2,1,0:T(8,128)(2,1)S(1)}, u32[]{:S(2)}) copy-start(bf16[4,8,80,512]{3,2,1,0:T(8,128)(2,1)S(1)} %shard_map.96) | copy-start | bytes 7864324
  69.9 33.3 %all-to-all-start.2 = ((bf16[4,8,80,512]{3,2,1,0:T(8,128)(2,1)}), bf16[4,8,80,512]{3,2,1,0:T(8,128)(2,1)S(1)}, u32[]{:S(2)}, u32[]{:S(2)}) async-start(bf16[4,8,80,512]{3,2,1,0:T(8,128)(2,1)} %copy-done), calls=%async_computation.2 | async-start | bytes 5242880 | tf_op jit(solution)/shard_map/all_to_all | solution.py:219
  76.0 17.4 %collective-permute-start.1 = (bf16[4,512,128]{2,1,0:T(8,128)(2,1)}, bf16[4,512,128]{2,1,0:T(8,128)(2,1)S(1)}, u32[]{:S(2)}, u32[]{:S(2)}) collective-permute-start(bf16[4,512,128]{2,1,0:T(8,128)(2,1)} %copy-done.5), channel_id=1, source_target_pairs={{0,64},{32,480},{64,0},{96,160},{128,192},{160,96},{192,128},{224,... | collective-permute-start | bytes 1572872 | tf_op jit(solution)/shard_map/ppermute | solution.py:247
  93.5 9.7 %collective-permute-start.2 = (bf16[512,128]{1,0:T(8,128)(2,1)S(1)}, bf16[512,128]{1,0:T(8,128)(2,1)S(1)}, u32[]{:S(2)}, u32[]{:S(2)}) collective-permute-start(bf16[512,128]{1,0:T(8,128)(2,1)S(1)} %get-tuple-element.40), channel_id=1, source_target_pairs={{0,256},{64,320},{128,384},{192,448},{256,0},{320,64},{384,128},{4... | collective-permute-start | bytes 393224 | tf_op jit(solution)/shard_map/ppermute | solution.py:252
  104.4 22.7 %all-to-all-start.3 = ((bf16[8,80,512]{2,1,0:T(8,128)(2,1)}), bf16[8,80,512]{2,1,0:T(8,128)(2,1)S(1)}, u32[]{:S(2)}, u32[]{:S(2)}) async-start(bf16[8,80,512]{2,1,0:T(8,128)(2,1)} %shard_map.98), calls=%async_computation.3 | async-start | bytes 1310720 | tf_op jit(solution)/shard_map/all_to_all | solution.py:219
  112.5 9.3 %collective-permute-start.3 = (bf16[512,128]{1,0:T(8,128)(2,1)S(1)}, bf16[512,128]{1,0:T(8,128)(2,1)S(1)}, u32[]{:S(2)}, u32[]{:S(2)}) collective-permute-start(bf16[512,128]{1,0:T(8,128)(2,1)S(1)} %get-tuple-element.45), channel_id=1, source_target_pairs={{0,128},{64,192},{128,256},{192,320},{256,384},{320,448},{384,0},{... | collective-permute-start | bytes 393224 | tf_op jit(solution)/shard_map/ppermute | solution.py:252
  114.4 8.9 %collective-permute-start.4 = (bf16[512,128]{1,0:T(8,128)(2,1)S(1)}, bf16[512,128]{1,0:T(8,128)(2,1)S(1)}, u32[]{:S(2)}, u32[]{:S(2)}) collective-permute-start(bf16[512,128]{1,0:T(8,128)(2,1)S(1)} %get-tuple-element.47), channel_id=1, source_target_pairs={{0,384},{64,448},{128,0},{192,64},{256,128},{320,192},{384,256},{4... | collective-permute-start | bytes 393224 | tf_op jit(solution)/shard_map/ppermute | solution.py:252

commit v7 on v6

--- a/solution.py
+++ b/solution.py
@@ -73,27 +73,55 @@
     return pl.ds(pl.multiple_of(owner_at(core, near, far) * OWN, OWN), OWN)
 
 
-def units_kernel(where, in_l, out_l, parts, w_in, w_out, keep, send, act, dh, xg, hidden, d_act):
-    core, z = where[0], where[1]
+def gather_features(core, parts, xg):
     for near in range(NEAR):
         for far in range(FAR):
             xg[features(core, near, far), :] = parts[near, far]
-    hidden[...] = jnp.zeros_like(hidden)
-    d_act[...] = jnp.zeros_like(d_act)
-
-    def product(s, carry):
+
+
+def partials_kernel(
+    where, in_l, out_l, xg_parts, w_in, w_out, act, dh, parts, xg, hidden, d_act, y, dx, stage, sems
+):
+    core = where[0]
+    gather_features(core, xg_parts, xg)
+    for total in (hidden, d_act, y, dx):
+        total[...] = jnp.zeros_like(total)
+
+    def up(s, carry):
         row, col, live = place(in_l, s)
         hidden[row] += dot(w_in[s], xg[pl.ds(col, BLK), :T], ((1,), (0,))) * live
         row, col, live = place(out_l, s)
         d_act[row] += dot(w_out[s], xg[pl.ds(col, BLK), T:], ((1,), (0,))) * live
         return carry
 
-    lax.fori_loop(0, CAP, product, 0, unroll=8)
+    def down(s, carry):
+        row, col, live = place(out_l, s)
+        y[pl.ds(col, BLK), :] += dot(w_out[s], act[row], ((0,), (0,))) * live
+        row, col, live = place(in_l, s)
+        dx[pl.ds(col, BLK), :] += dot(w_in[s], dh[row], ((0,), (0,))) * live
+        return carry
+
+    lax.fori_loop(0, CAP, up, 0, unroll=8)
     for row in range(ROWS):
         values, slopes = gelu_pair(hidden[row])
         act[row] = values.astype(act.dtype)
         dh[row] = (d_act[row] * slopes).astype(dh.dtype)
-
+    lax.fori_loop(0, CAP, down, 0, unroll=8)
+    copies = []
+    for near in range(NEAR):
+        for far in range(FAR):
+            rows = features(core, near, far)
+            stage[near, far, :, :T] = y[rows, :].astype(stage.dtype)
+            stage[near, far, :, T:] = dx[rows, :].astype(stage.dtype)
+        copies.append(pltpu.make_async_copy(stage.at[near], parts.at[near], sems.at[near]))
+        copies[-1].start()
+    for copy in copies:
+        copy.wait()
+
+
+def grads_kernel(where, in_l, out_l, xg_parts, act, dh, keep, send, xg):
+    core, z = where[0], where[1]
+    gather_features(core, xg_parts, xg)
     first = core == 0
     scale = float(T * Z * C) ** -0.5
     slots = [
@@ -120,31 +148,6 @@
     lax.fori_loop(0, CAP // 2, pair, 0, unroll=4)
 
 
-def add_products(lists, units, weights, total):
-    total[...] = jnp.zeros_like(total)
-
-    def product(s, carry):
-        row, col, live = place(lists, s)
-        total[pl.ds(col, BLK), :] += dot(weights[s], units[row], ((0,), (0,))) * live
-        return carry
-
-    lax.fori_loop(0, CAP, product, 0, unroll=8)
-
-
-def output_kernel(lists, act, w_out, part, total):
-    add_products(lists, act, w_out, total)
-    part[...] = total[...].astype(part.dtype)
-
-
-def partials_kernel(where, lists, dh, w_in, y_part, parts, total):
-    add_products(lists, dh, w_in, total)
-    for near in range(NEAR):
-        for far in range(FAR):
-            rows = features(where[0], near, far)
-            parts[near, far, :, :T] = y_part[rows, :]
-            parts[near, far, :, T:] = total[rows, :].astype(parts.dtype)
-
-
 def cores_kernel(keep, got, near, far):
     for slot in range(Z):
         both = keep[slot].astype(jnp.float32) + got[slot].astype(jnp.float32)
@@ -197,22 +200,30 @@
     )(*scalars, *arrays)
 
 
-def units_call(where, in_l, out_l, parts, w_in, w_out):
-    f32 = jnp.float32
-    scratch = (((FEAT, 2 * T), jnp.bfloat16), (UNITS, f32), (UNITS, f32))
-    outs = ((Z,) + STEP, (Z,) + STEP, UNITS, UNITS)
-    return call(units_kernel, (where, in_l, out_l), (parts, w_in, w_out), outs, scratch)
-
-
-def output_call(lists, act, w_out):
-    scratch = (((FEAT, T), jnp.float32),)
-    return call(output_kernel, (lists,), (act, w_out), ((FEAT, T),), scratch)[0]
-
-
-def partials_call(where, lists, dh, w_in, y_part):
-    scratch = (((FEAT, T), jnp.float32),)
-    outs = ((NEAR, FAR, OWN, 2 * T),)
-    return call(partials_kernel, (where, lists), (dh, w_in, y_part), outs, scratch)[0]
+def partials_call(where, in_l, out_l, xg_parts, w_in, w_out):
+    bf, f32 = jnp.bfloat16, jnp.float32
+    groups = (NEAR, FAR, OWN, 2 * T)
+    return pl.pallas_call(
+        partials_kernel,
+        out_shape=(*[jax.ShapeDtypeStruct(UNITS, bf)] * 2, pltpu.HBM(groups, bf)),
+        in_specs=[SMEM] * 3 + [VMEM] * 3,
+        out_specs=(VMEM, VMEM, pl.BlockSpec(memory_space=pltpu.HBM)),
+        scratch_shapes=[
+            pltpu.VMEM((FEAT, 2 * T), bf),
+            *[pltpu.VMEM(UNITS, f32)] * 2,
+            *[pltpu.VMEM((FEAT, T), f32)] * 2,
+            pltpu.VMEM(groups, bf),
+            pltpu.SemaphoreType.DMA((NEAR,)),
+        ],
+        compiler_params=LIMIT,
+        interpret=INTERPRET,
+    )(where, in_l, out_l, xg_parts, w_in, w_out)
+
+
+def grads_call(where, in_l, out_l, xg_parts, act, dh):
+    scratch = (((FEAT, 2 * T), jnp.bfloat16),)
+    outs = ((Z,) + STEP,) * 2
+    return call(grads_kernel, (where, in_l, out_l), (xg_parts, act, dh), outs, scratch)
 
 
 def exchange(x, groups):
@@ -234,25 +245,22 @@
     own = jnp.concatenate([tokens.T, cotangent.T], axis=1)
     where = jnp.stack([lax.axis_index("c"), lax.axis_index("z")]).astype(jnp.int32)
     own, where = lax.optimization_barrier((own, where))
-    parts = spread(spread(own, FAR_GROUPS), NEAR_GROUPS)
-    keep, send, act, dh = units_call(where, in_l, out_l, parts, in_blocks, out_blocks)
+    xg = spread(spread(own, FAR_GROUPS), NEAR_GROUPS)
+    act, dh, parts = partials_call(where, in_l, out_l, xg, in_blocks, out_blocks)
+    parts = exchange(parts, NEAR_GROUPS)
+    keep, send = grads_call(where, in_l, out_l, xg, act, dh)
     got = lax.ppermute(send, "c", [(0, 1), (1, 0)])
-    y_part = output_call(out_l, act, out_blocks)
-    y_part, got = lax.optimization_barrier((y_part, got))
     near, far = call(cores_kernel, (), (keep, got), ((HALF,) + STEP,) * 2)
-    near, far, dh = lax.optimization_barrier((near, far, dh))
     pairs = [
         (z * C + c, neighbour(z, c) % Z * C + c) for z in range(Z) for c in range(C)
     ]
     got = lax.ppermute(far, ("z", "c"), pairs)
-    parts = partials_call(where, in_l, dh, in_blocks, y_part)
-    parts = exchange(parts, NEAR_GROUPS)
+    parts, got = lax.optimization_barrier((parts, got))
     own, *steps = call(pairs_kernel, (), (near, got), (STEP,) * HALF)
     moved = [
         lax.ppermute(step, "z", [(z, (z + 2 * k) % Z) for z in range(Z)])
         for k, step in enumerate(steps, 1)
     ]
-    parts, moved[1] = lax.optimization_barrier((parts, moved[1]))
     (parts,) = call(near_sum_kernel, (), (parts,), ((FAR, OWN, 2 * T),))
     parts = exchange(parts, FAR_GROUPS)
     y, dx = call(far_sum_kernel, (), (parts,), ((OWN, T),) * 2)

time: 129 us -> 125 us (0.969)
  local copies, waits for them, and re-layouts: 2.65 us -> 0.36 us
  Pallas kernels: 12.5 us -> 14.4 us
  starting transfers between devices: 42.8 us -> 40.9 us
    pallas_call x0 -> x1, Pallas kernels: none -> 6.95 us  [partials_call(): pl.pallas_call(partials_kernel, out_shape=(*[jax.ShapeDtypeStruct(UNITS,...]
    pallas_call x8 -> x6, Pallas kernels: 12.5 us -> 7.5 us  [call(): pl.pallas_call(kernel, out_shape=tuple((jax.ShapeDtypeStruct(dims, bf) fo...]
    ppermute x1, starting transfers between devices: 6.09 us -> 2.13 us  [body(): got = lax.ppermute(send, 'c', [(0, 1), (1, 0)])]
    all_to_all x2, waiting for transfers between devices: 3.12 us -> 0.01 us  [exchange(): lax.all_to_all(x, ('c', 'x', 'y'), split_axis=0, concat_axis=0, axis_inde...]
    ppermute x1, waiting for transfers between devices: 0.06 us -> 2.42 us  [body(): got = lax.ppermute(send, 'c', [(0, 1), (1, 0)])]
    unnamed x12 -> x8, local copies, waits for them, and re-layouts: 2.3 us -> 0.03 us
    all_to_all x2, starting transfers between devices: 14.1 us -> 16.2 us  [exchange(): lax.all_to_all(x, ('c', 'x', 'y'), split_axis=0, concat_axis=0, axis_inde...]
  transfers between devices with their start and end apart: 7 -> 7, of which waited for: 6 -> 4; matrix products, arithmetic and copies ran while one was open for 0% -> 0% of each run, Pallas kernels for 2% -> 3%
where the time goes in v7:
time: 125 us; the launch traced here: 124 us
  blocking collectives  49.7 us (40%)
  starting transfers between devices  40.9 us (33%)
  waiting for transfers between devices  17.4 us (14%)
  Pallas kernels  14.4 us (12%)
    all_to_all x2, blocking collectives, exchange(): lax.all_to_all(x, ('c', 'x', 'y'), split_axis=0, concat_axis=0, axis_inde...  49.7 us
    all_to_all x2, starting transfers between devices, exchange(): lax.all_to_all(x, ('c', 'x', 'y'), split_axis=0, concat_axis=0, axis_inde...  16.2 us
    ppermute x3, starting transfers between devices, body(): lax.ppermute(step, 'z', [(z, (z + 2 * k) % Z) for z in range(Z)])  11.9 us
    ppermute x1, starting transfers between devices, body(): got = lax.ppermute(far, ('z', 'c'), pairs)  10.7 us
    ppermute x3, waiting for transfers between devices, body(): lax.ppermute(step, 'z', [(z, (z + 2 * k) % Z) for z in range(Z)])  8.4 us
    pallas_call x6, Pallas kernels, call(): pl.pallas_call(kernel, out_shape=tuple((jax.ShapeDtypeStruct(dims, bf) fo...  7.5 us
    pallas_call x1, Pallas kernels, partials_call(): pl.pallas_call(partials_kernel, out_shape=(*[jax.ShapeDtypeStruct(UNITS,...  6.95 us
    ppermute x1, waiting for transfers between devices, body(): got = lax.ppermute(far, ('z', 'c'), pairs)  6.56 us
  transfers between devices with their start and end apart: 7, of which 4 were waited for; matrix products, arithmetic and copies ran while one was open for 0% of the time, Pallas kernels for 3%

profile of v7, /device:TPU:1, one launch (start us, length us, event | category | flops | bytes accessed | tf_op | source)
XLA Modules:
  0.0 124.4 jit_solution(5499451023297733458)
XLA Ops:
  0.6 0.1 pad_add_fusion.where
  0.7 0.8 pad_maximum_fusion
  1.6 28.0 %all_to_all.20 = bf16[8,80,512]{2,1,0:T(8,128)(2,1)S(1)} all-to-all(bf16[8,80,512]{2,1,0:T(8,128)(2,1)S(1)} %broadcast_in_dim.4), channel_id=1, replica_groups={{0,2,4,6,16,18,20,22},{1,3,5,7,17,19,21,23},{8,10,12,14,24,26,28,30},{9..., dimensions={0} | all-to-all | bytes 1310720 | tf_op jit(solution)/shard_map/all_to_all | solution.py:230
  29.6 0.3 broadcast_in_dim.5
  29.9 0.0 copy-start
  29.9 21.7 %all_to_all.21.xg_parts = bf16[4,8,80,512]{3,2,1,0:T(8,128)(2,1)S(1)} all-to-all(bf16[4,8,80,512]{3,2,1,0:T(8,128)(2,1)S(1)} %broadcast_in_dim.5), channel_id=1, replica_groups={{0,1,8,9},{2,3,10,11},{4,5,12,13},{6,7,14,15},{16,17,24,25},{18,19,26,2..., dimensions={0} | all-to-all | bytes 5242880 | tf_op jit(solution)/shard_map/all_to_all | solution.py:230
  51.6 7.0 %shard_map.93 = (bf16[5,128,256]{2,1,0:T(8,128)(2,1)S(1)}, bf16[5,128,256]{2,1,0:T(8,128)(2,1)S(1)}, bf16[4,8,80,512]{3,2,1,0:T(8,128)(2,1)}) custom-call(s32[2]{0:T(128)S(1)} %pad_add_fusion.where, s32[2,32]{1,0:T(2,128)S(1)} %bitcast.10, s32[2,32]{1,0:T(2,128)S(1)} %bitcast.12, bf16[4,8,80,512]{3,2,1,0:T(8,128)(2,1)S(1)} %all_to_all.21.xg_parts, ...), custom_call_target="tpu_custom_call" | custom-call | tf_op jit(solution)/shard_map/pallas_call | solution.py:206
  58.6 8.5 %all-to-all-start.2 = ((bf16[4,8,80,512]{3,2,1,0:T(8,128)(2,1)}), bf16[4,8,80,512]{3,2,1,0:T(8,128)(2,1)}, u32[]{:S(2)}, u32[]{:S(2)}) async-start(bf16[4,8,80,512]{3,2,1,0:T(8,128)(2,1)} %get-tuple-element.25), calls=%async_computation.2 | async-start | bytes 5242880 | tf_op jit(solution)/shard_map/all_to_all | solution.py:230
  67.1 2.8 %shard_map.94 = (bf16[8,512,128]{2,1,0:T(8,128)(2,1)S(1)}, bf16[8,512,128]{2,1,0:T(8,128)(2,1)S(1)}) custom-call(s32[2]{0:T(128)S(1)} %pad_add_fusion.where, s32[2,32]{1,0:T(2,128)S(1)} %bitcast.11, s32[2,32]{1,0:T(2,128)S(1)} %bitcast.13, bf16[4,8,80,512]{3,2,1,0:T(8,128)(2,1)S(1)} %all_to_all.21.xg_parts, bf16[5,128,256]{2,1,0:T(8,128)(2,1)S(1)} %get-tuple-element.26.act, ...), custom_call_target="tpu_custom_call" | custom-call | tf_op jit(solution)/shard_map/pallas_call | solution.py:192
  69.9 2.1 %collective-permute-start = (bf16[8,512,128]{2,1,0:T(8,128)(2,1)S(1)}, bf16[8,512,128]{2,1,0:T(8,128)(2,1)S(1)}, u32[]{:S(2)}, u32[]{:S(2)}) collective-permute-start(bf16[8,512,128]{2,1,0:T(8,128)(2,1)S(1)} %get-tuple-element.29), channel_id=1, source_target_pairs={{0,32},{32,0},{1,33},{33,1},{2,34},{34,2},{3,35},{35,3},{4,36},{36... | collective-permute-start | bytes 3145736 | tf_op jit(solution)/shard_map/ppermute | solution.py:252
  72.1 2.4 %collective-permute-done.got = bf16[8,512,128]{2,1,0:T(8,128)(2,1)S(1)} collective-permute-done((bf16[8,512,128]{2,1,0:T(8,128)(2,1)S(1)}, bf16[8,512,128]{2,1,0:T(8,128)(2,1)S(1)}, u32[]{:S(2)}, u32[]{:S(2)}) %collective-permute-start) | collective-permute-done | bytes 1048608 | tf_op jit(solution)/shard_map/ppermute | solution.py:252
  74.5 0.2 shard_map.95
  74.7 10.7 %collective-permute-start.1 = (bf16[4,512,128]{2,1,0:T(8,128)(2,1)S(1)}, bf16[4,512,128]{2,1,0:T(8,128)(2,1)S(1)}, u32[]{:S(2)}, u32[]{:S(2)}) collective-permute-start(bf16[4,512,128]{2,1,0:T(8,128)(2,1)S(1)} %get-tuple-element.30), channel_id=1, source_target_pairs={{0,64},{32,480},{64,0},{96,160},{128,192},{160,96},{192,128},{224,... | collective-permute-start | bytes 1572872 | tf_op jit(solution)/shard_map/ppermute | solution.py:257
  85.4 6.6 %collective-permute-done.1.got = bf16[4,512,128]{2,1,0:T(8,128)(2,1)S(1)} collective-permute-done((bf16[4,512,128]{2,1,0:T(8,128)(2,1)S(1)}, bf16[4,512,128]{2,1,0:T(8,128)(2,1)S(1)}, u32[]{:S(2)}, u32[]{:S(2)}) %collective-permute-start.1) | collective-permute-done | bytes 524320 | tf_op jit(solution)/shard_map/ppermute | solution.py:257
  92.0 2.9 %shard_map.96 = bf16[8,80,512]{2,1,0:T(8,128)(2,1)} custom-call(bf16[4,8,80,512]{3,2,1,0:T(8,128)(2,1)} %all-to-all-done.2.parts), custom_call_target="tpu_custom_call" | custom-call | tf_op jit(solution)/shard_map/pallas_call | solution.py:192
  94.9 7.7 %all-to-all-start.3 = ((bf16[8,80,512]{2,1,0:T(8,128)(2,1)}), bf16[8,80,512]{2,1,0:T(8,128)(2,1)S(1)}, u32[]{:S(2)}, u32[]{:S(2)}) async-start(bf16[8,80,512]{2,1,0:T(8,128)(2,1)} %shard_map.96), calls=%async_computation.3 | async-start | bytes 1310720 | tf_op jit(solution)/shard_map/all_to_all | solution.py:230
  102.5 0.1 shard_map.98
  102.7 1.9 %collective-permute-start.2 = (bf16[512,128]{1,0:T(8,128)(2,1)S(1)}, bf16[512,128]{1,0:T(8,128)(2,1)S(1)}, u32[]{:S(2)}, u32[]{:S(2)}) collective-permute-start(bf16[512,128]{1,0:T(8,128)(2,1)S(1)} %get-tuple-element.37), channel_id=1, source_target_pairs={{0,128},{64,192},{128,256},{192,320},{256,384},{320,448},{384,0},{... | collective-permute-start | bytes 393224 | tf_op jit(solution)/shard_map/ppermute | solution.py:261
  104.6 5.7 %collective-permute-start.3 = (bf16[512,128]{1,0:T(8,128)(2,1)S(1)}, bf16[512,128]{1,0:T(8,128)(2,1)S(1)}, u32[]{:S(2)}, u32[]{:S(2)}) collective-permute-start(bf16[512,128]{1,0:T(8,128)(2,1)S(1)} %get-tuple-element.38), channel_id=1, source_target_pairs={{0,256},{64,320},{128,384},{192,448},{256,0},{320,64},{384,128},{4... | collective-permute-start | bytes 393224 | tf_op jit(solution)/shard_map/ppermute | solution.py:261
  110.3 4.3 %collective-permute-start.4 = (bf16[512,128]{1,0:T(8,128)(2,1)S(1)}, bf16[512,128]{1,0:T(8,128)(2,1)S(1)}, u32[]{:S(2)}, u32[]{:S(2)}) collective-permute-start(bf16[512,128]{1,0:T(8,128)(2,1)S(1)} %get-tuple-element.39), channel_id=1, source_target_pairs={{0,384},{64,448},{128,0},{192,64},{256,128},{320,192},{384,256},{4... | collective-permute-start | bytes 393224 | tf_op jit(solution)/shard_map/ppermute | solution.py:261
  114.6 3.5 %collective-permute-done.3.refs_2_ = bf16[512,128]{1,0:T(8,128)(2,1)S(1)} collective-permute-done((bf16[512,128]{1,0:T(8,128)(2,1)S(1)}, bf16[512,128]{1,0:T(8,128)(2,1)S(1)}, u32[]{:S(2)}, u32[]{:S(2)}) %collective-permute-start.3) | collective-permute-done | bytes 131104 | tf_op jit(solution)/shard_map/ppermute | solution.py:261
  118.1 4.9 %collective-permute-done.4.refs_3_ = bf16[512,128]{1,0:T(8,128)(2,1)S(1)} collective-permute-done((bf16[512,128]{1,0:T(8,128)(2,1)S(1)}, bf16[512,128]{1,0:T(8,128)(2,1)S(1)}, u32[]{:S(2)}, u32[]{:S(2)}) %collective-permute-start.4) | collective-permute-done | bytes 131104 | tf_op jit(solution)/shard_map/ppermute | solution.py:261
  123.0 0.7 shard_map.99
  123.7 0.7 shard_map.97
  (11 shorter events, 0.1 us)
Async XLA Ops:
  29.9 21.7 %copy-start = (bf16[32,128,128]{2,1,0:T(8,128)(2,1)S(1)}, bf16[32,128,128]{2,1,0:T(8,128)(2,1)}, u32[]{:S(2)}) copy-start(bf16[32,128,128]{2,1,0:T(8,128)(2,1)} %w_in.1) | copy-start | bytes 3145732
  29.9 21.7 %copy-start.1 = (bf16[32,128,128]{2,1,0:T(8,128)(2,1)S(1)}, bf16[32,128,128]{2,1,0:T(8,128)(2,1)}, u32[]{:S(2)}) copy-start(bf16[32,128,128]{2,1,0:T(8,128)(2,1)} %w_out.1) | copy-start | bytes 3145732
  29.9 21.7 %copy-start.2 = (s32[32,2]{0,1:T(2,128)S(1)}, s32[32,2]{0,1:T(2,128)}, u32[]{:S(2)}) copy-start(s32[32,2]{0,1:T(2,128)} %param.9) | copy-start | bytes 772
  29.9 21.7 %copy-start.3 = (s32[32,2]{0,1:T(2,128)S(1)}, s32[32,2]{0,1:T(2,128)}, u32[]{:S(2)}) copy-start(s32[32,2]{0,1:T(2,128)} %param.11) | copy-start | bytes 772
  58.6 33.4 %all-to-all-start.2 = ((bf16[4,8,80,512]{3,2,1,0:T(8,128)(2,1)}), bf16[4,8,80,512]{3,2,1,0:T(8,128)(2,1)}, u32[]{:S(2)}, u32[]{:S(2)}) async-start(bf16[4,8,80,512]{3,2,1,0:T(8,128)(2,1)} %get-tuple-element.25), calls=%async_computation.2 | async-start | bytes 5242880 | tf_op jit(solution)/shard_map/all_to_all | solution.py:230
  69.9 4.6 %collective-permute-start = (bf16[8,512,128]{2,1,0:T(8,128)(2,1)S(1)}, bf16[8,512,128]{2,1,0:T(8,128)(2,1)S(1)}, u32[]{:S(2)}, u32[]{:S(2)}) collective-permute-start(bf16[8,512,128]{2,1,0:T(8,128)(2,1)S(1)} %get-tuple-element.29), channel_id=1, source_target_pairs={{0,32},{32,0},{1,33},{33,1},{2,34},{34,2},{3,35},{35,3},{4,36},{36... | collective-permute-start | bytes 3145736 | tf_op jit(solution)/shard_map/ppermute | solution.py:252
  74.7 17.2 %collective-permute-start.1 = (bf16[4,512,128]{2,1,0:T(8,128)(2,1)S(1)}, bf16[4,512,128]{2,1,0:T(8,128)(2,1)S(1)}, u32[]{:S(2)}, u32[]{:S(2)}) collective-permute-start(bf16[4,512,128]{2,1,0:T(8,128)(2,1)S(1)} %get-tuple-element.30), channel_id=1, source_target_pairs={{0,64},{32,480},{64,0},{96,160},{128,192},{160,96},{192,128},{224,... | collective-permute-start | bytes 1572872 | tf_op jit(solution)/shard_map/ppermute | solution.py:257
  94.9 28.9 %all-to-all-start.3 = ((bf16[8,80,512]{2,1,0:T(8,128)(2,1)}), bf16[8,80,512]{2,1,0:T(8,128)(2,1)S(1)}, u32[]{:S(2)}, u32[]{:S(2)}) async-start(bf16[8,80,512]{2,1,0:T(8,128)(2,1)} %shard_map.96), calls=%async_computation.3 | async-start | bytes 1310720 | tf_op jit(solution)/shard_map/all_to_all | solution.py:230
  102.7 12.0 %collective-permute-start.2 = (bf16[512,128]{1,0:T(8,128)(2,1)S(1)}, bf16[512,128]{1,0:T(8,128)(2,1)S(1)}, u32[]{:S(2)}, u32[]{:S(2)}) collective-permute-start(bf16[512,128]{1,0:T(8,128)(2,1)S(1)} %get-tuple-element.37), channel_id=1, source_target_pairs={{0,128},{64,192},{128,256},{192,320},{256,384},{320,448},{384,0},{... | collective-permute-start | bytes 393224 | tf_op jit(solution)/shard_map/ppermute | solution.py:261
  104.6 13.5 %collective-permute-start.3 = (bf16[512,128]{1,0:T(8,128)(2,1)S(1)}, bf16[512,128]{1,0:T(8,128)(2,1)S(1)}, u32[]{:S(2)}, u32[]{:S(2)}) collective-permute-start(bf16[512,128]{1,0:T(8,128)(2,1)S(1)} %get-tuple-element.38), channel_id=1, source_target_pairs={{0,256},{64,320},{128,384},{192,448},{256,0},{320,64},{384,128},{4... | collective-permute-start | bytes 393224 | tf_op jit(solution)/shard_map/ppermute | solution.py:261
  110.3 12.7 %collective-permute-start.4 = (bf16[512,128]{1,0:T(8,128)(2,1)S(1)}, bf16[512,128]{1,0:T(8,128)(2,1)S(1)}, u32[]{:S(2)}, u32[]{:S(2)}) collective-permute-start(bf16[512,128]{1,0:T(8,128)(2,1)S(1)} %get-tuple-element.39), channel_id=1, source_target_pairs={{0,384},{64,448},{128,0},{192,64},{256,128},{320,192},{384,256},{4... | collective-permute-start | bytes 393224 | tf_op jit(solution)/shard_map/ppermute | solution.py:261

commit v8 on v7

--- a/solution.py
+++ b/solution.py
@@ -101,12 +101,12 @@
         dx[pl.ds(col, BLK), :] += dot(w_in[s], dh[row], ((0,), (0,))) * live
         return carry
 
-    lax.fori_loop(0, CAP, up, 0, unroll=8)
+    lax.fori_loop(0, CAP, up, 0, unroll=CAP)
     for row in range(ROWS):
         values, slopes = gelu_pair(hidden[row])
         act[row] = values.astype(act.dtype)
         dh[row] = (d_act[row] * slopes).astype(dh.dtype)
-    lax.fori_loop(0, CAP, down, 0, unroll=8)
+    lax.fori_loop(0, CAP, down, 0, unroll=CAP)
     copies = []
     for near in range(NEAR):
         for far in range(FAR):
@@ -170,9 +170,8 @@
 
 
 def near_sum_kernel(parts, out):
-    for far in range(FAR):
-        total = sum(parts[near, far].astype(jnp.float32) for near in range(NEAR))
-        out[far] = total.astype(out.dtype)
+    total = sum(parts[near].astype(jnp.float32) for near in range(NEAR))
+    out[...] = total.astype(out.dtype)
 
 
 def far_sum_kernel(parts, y, dx):
@@ -226,6 +225,19 @@
     return call(grads_kernel, (where, in_l, out_l), (xg_parts, act, dh), outs, scratch)
 
 
+def near_sum_call(parts):
+    block = (2, OWN, 2 * T)
+    return pl.pallas_call(
+        near_sum_kernel,
+        grid=(FAR // block[0],),
+        out_shape=jax.ShapeDtypeStruct(parts.shape[1:], parts.dtype),
+        in_specs=[pl.BlockSpec((NEAR,) + block, lambda i: (0, i, 0, 0))],
+        out_specs=pl.BlockSpec(block, lambda i: (i, 0, 0)),
+        compiler_params=LIMIT,
+        interpret=INTERPRET,
+    )(parts)
+
+
 def exchange(x, groups):
     return lax.all_to_all(
         x, ("c", "x", "y"), split_axis=0, concat_axis=0, axis_index_groups=groups
@@ -258,11 +270,10 @@
     parts, got = lax.optimization_barrier((parts, got))
     own, *steps = call(pairs_kernel, (), (near, got), (STEP,) * HALF)
     moved = [
-        lax.ppermute(step, "z", [(z, (z + 2 * k) % Z) for z in range(Z)])
-        for k, step in enumerate(steps, 1)
+        lax.ppermute(steps[k - 1], "z", [(z, (z + 2 * k) % Z) for z in range(Z)])
+        for k in (2, 1, 3)
     ]
-    (parts,) = call(near_sum_kernel, (), (parts,), ((FAR, OWN, 2 * T),))
-    parts = exchange(parts, FAR_GROUPS)
+    parts = exchange(near_sum_call(parts), FAR_GROUPS)
     y, dx = call(far_sum_kernel, (), (parts,), ((OWN, T),) * 2)
     grads = call(last_kernel, (), (own, *moved), ((CAP * SUB, BLK),) * 2)
     out_grad, in_grad = (grad.reshape(CAP, SUB, BLK) for grad in grads)

time: 125 us -> 123 us (0.984)
  waiting for transfers between devices: 17.4 us -> 15.4 us
    pallas_call x0 -> x1, Pallas kernels: none -> 3.72 us  [near_sum_call(): pl.pallas_call(near_sum_kernel, grid=(FAR // block[0],), out_shape=jax.Sh...]
    pallas_call x6 -> x5, Pallas kernels: 7.5 us -> 4.59 us  [call(): pl.pallas_call(kernel, out_shape=tuple((jax.ShapeDtypeStruct(dims, bf) fo...]
    ppermute x3, waiting for transfers between devices: 8.4 us -> 6.45 us  [body(): lax.ppermute(steps[k - 1], 'z', [(z, (z + 2 * k) % Z) for z in range(Z)])]
where the time goes in v8:
time: 123 us; the launch traced here: 122 us
  blocking collectives  49.7 us (40%)
  starting transfers between devices  40.9 us (33%)
  waiting for transfers between devices  15.4 us (13%)
  Pallas kernels  14.2 us (12%)
    all_to_all x2, blocking collectives, exchange(): lax.all_to_all(x, ('c', 'x', 'y'), split_axis=0, concat_axis=0, axis_inde...  49.7 us
    all_to_all x2, starting transfers between devices, exchange(): lax.all_to_all(x, ('c', 'x', 'y'), split_axis=0, concat_axis=0, axis_inde...  16.2 us
    ppermute x3, starting transfers between devices, body(): lax.ppermute(steps[k - 1], 'z', [(z, (z + 2 * k) % Z) for z in range(Z)])  11.9 us
    ppermute x1, starting transfers between devices, body(): got = lax.ppermute(far, ('z', 'c'), pairs)  10.7 us
    ppermute x1, waiting for transfers between devices, body(): got = lax.ppermute(far, ('z', 'c'), pairs)  6.56 us
    ppermute x3, waiting for transfers between devices, body(): lax.ppermute(steps[k - 1], 'z', [(z, (z + 2 * k) % Z) for z in range(Z)])  6.45 us
    pallas_call x1, Pallas kernels, partials_call(): pl.pallas_call(partials_kernel, out_shape=(*[jax.ShapeDtypeStruct(UNITS,...  5.88 us
    pallas_call x5, Pallas kernels, call(): pl.pallas_call(kernel, out_shape=tuple((jax.ShapeDtypeStruct(dims, bf) fo...  4.59 us
  transfers between devices with their start and end apart: 7, of which 4 were waited for; matrix products, arithmetic and copies ran while one was open for 0% of the time, Pallas kernels for 3%

profile of v8, /device:TPU:1, one launch (start us, length us, event | category | flops | bytes accessed | tf_op | source)
XLA Modules:
  0.0 122.2 jit_solution(16181600697998450591)
XLA Ops:
  0.6 0.1 pad_add_fusion.where
  0.7 0.8 pad_maximum_fusion
  1.6 28.0 %all_to_all.20 = bf16[8,80,512]{2,1,0:T(8,128)(2,1)S(1)} all-to-all(bf16[8,80,512]{2,1,0:T(8,128)(2,1)S(1)} %broadcast_in_dim.4), channel_id=1, replica_groups={{0,2,4,6,16,18,20,22},{1,3,5,7,17,19,21,23},{8,10,12,14,24,26,28,30},{9..., dimensions={0} | all-to-all | bytes 1310720 | tf_op jit(solution)/shard_map/all_to_all | solution.py:242
  29.6 0.3 broadcast_in_dim.5
  29.9 0.0 copy-start
  29.9 21.7 %all_to_all.21.xg_parts = bf16[4,8,80,512]{3,2,1,0:T(8,128)(2,1)S(1)} all-to-all(bf16[4,8,80,512]{3,2,1,0:T(8,128)(2,1)S(1)} %broadcast_in_dim.5), channel_id=1, replica_groups={{0,1,8,9},{2,3,10,11},{4,5,12,13},{6,7,14,15},{16,17,24,25},{18,19,26,2..., dimensions={0} | all-to-all | bytes 5242880 | tf_op jit(solution)/shard_map/all_to_all | solution.py:242
  51.6 5.9 %shard_map.93 = (bf16[5,128,256]{2,1,0:T(8,128)(2,1)S(1)}, bf16[5,128,256]{2,1,0:T(8,128)(2,1)S(1)}, bf16[4,8,80,512]{3,2,1,0:T(8,128)(2,1)}) custom-call(s32[2]{0:T(128)S(1)} %pad_add_fusion.where, s32[2,32]{1,0:T(2,128)S(1)} %bitcast.10, s32[2,32]{1,0:T(2,128)S(1)} %bitcast.12, bf16[4,8,80,512]{3,2,1,0:T(8,128)(2,1)S(1)} %all_to_all.21.xg_parts, ...), custom_call_target="tpu_custom_call" | custom-call | tf_op jit(solution)/shard_map/pallas_call | solution.py:205
  57.5 8.5 %all-to-all-start.2 = ((bf16[4,8,80,512]{3,2,1,0:T(8,128)(2,1)}), bf16[4,8,80,512]{3,2,1,0:T(8,128)(2,1)}, u32[]{:S(2)}, u32[]{:S(2)}) async-start(bf16[4,8,80,512]{3,2,1,0:T(8,128)(2,1)} %get-tuple-element.25), calls=%async_computation.2 | async-start | bytes 5242880 | tf_op jit(solution)/shard_map/all_to_all | solution.py:242
  66.0 2.8 %shard_map.94 = (bf16[8,512,128]{2,1,0:T(8,128)(2,1)S(1)}, bf16[8,512,128]{2,1,0:T(8,128)(2,1)S(1)}) custom-call(s32[2]{0:T(128)S(1)} %pad_add_fusion.where, s32[2,32]{1,0:T(2,128)S(1)} %bitcast.11, s32[2,32]{1,0:T(2,128)S(1)} %bitcast.13, bf16[4,8,80,512]{3,2,1,0:T(8,128)(2,1)S(1)} %all_to_all.21.xg_parts, bf16[5,128,256]{2,1,0:T(8,128)(2,1)S(1)} %get-tuple-element.26.act, ...), custom_call_target="tpu_custom_call" | custom-call | tf_op jit(solution)/shard_map/pallas_call | solution.py:191
  68.8 2.1 %collective-permute-start = (bf16[8,512,128]{2,1,0:T(8,128)(2,1)S(1)}, bf16[8,512,128]{2,1,0:T(8,128)(2,1)S(1)}, u32[]{:S(2)}, u32[]{:S(2)}) collective-permute-start(bf16[8,512,128]{2,1,0:T(8,128)(2,1)S(1)} %get-tuple-element.29), channel_id=1, source_target_pairs={{0,32},{32,0},{1,33},{33,1},{2,34},{34,2},{3,35},{35,3},{4,36},{36... | collective-permute-start | bytes 3145736 | tf_op jit(solution)/shard_map/ppermute | solution.py:264
  71.0 2.4 %collective-permute-done.got = bf16[8,512,128]{2,1,0:T(8,128)(2,1)S(1)} collective-permute-done((bf16[8,512,128]{2,1,0:T(8,128)(2,1)S(1)}, bf16[8,512,128]{2,1,0:T(8,128)(2,1)S(1)}, u32[]{:S(2)}, u32[]{:S(2)}) %collective-permute-start) | collective-permute-done | bytes 1048608 | tf_op jit(solution)/shard_map/ppermute | solution.py:264
  73.4 0.2 shard_map.95
  73.6 10.7 %collective-permute-start.1 = (bf16[4,512,128]{2,1,0:T(8,128)(2,1)S(1)}, bf16[4,512,128]{2,1,0:T(8,128)(2,1)S(1)}, u32[]{:S(2)}, u32[]{:S(2)}) collective-permute-start(bf16[4,512,128]{2,1,0:T(8,128)(2,1)S(1)} %get-tuple-element.30), channel_id=1, source_target_pairs={{0,64},{32,480},{64,0},{96,160},{128,192},{160,96},{192,128},{224,... | collective-permute-start | bytes 1572872 | tf_op jit(solution)/shard_map/ppermute | solution.py:269
  84.3 6.6 %collective-permute-done.1.got = bf16[4,512,128]{2,1,0:T(8,128)(2,1)S(1)} collective-permute-done((bf16[4,512,128]{2,1,0:T(8,128)(2,1)S(1)}, bf16[4,512,128]{2,1,0:T(8,128)(2,1)S(1)}, u32[]{:S(2)}, u32[]{:S(2)}) %collective-permute-start.1) | collective-permute-done | bytes 524320 | tf_op jit(solution)/shard_map/ppermute | solution.py:269
  90.9 3.7 %shard_map.96 = bf16[8,80,512]{2,1,0:T(8,128)(2,1)} custom-call(bf16[4,8,80,512]{3,2,1,0:T(8,128)(2,1)} %all-to-all-done.2.parts), custom_call_target="tpu_custom_call" | custom-call | tf_op jit(solution)/shard_map/pallas_call | solution.py:230
  94.6 7.7 %all-to-all-start.3 = ((bf16[8,80,512]{2,1,0:T(8,128)(2,1)}), bf16[8,80,512]{2,1,0:T(8,128)(2,1)S(1)}, u32[]{:S(2)}, u32[]{:S(2)}) async-start(bf16[8,80,512]{2,1,0:T(8,128)(2,1)} %shard_map.96), calls=%async_computation.3 | async-start | bytes 1310720 | tf_op jit(solution)/shard_map/all_to_all | solution.py:242
  102.3 0.1 shard_map.98
  102.4 4.5 %collective-permute-start.2 = (bf16[512,128]{1,0:T(8,128)(2,1)S(1)}, bf16[512,128]{1,0:T(8,128)(2,1)S(1)}, u32[]{:S(2)}, u32[]{:S(2)}) collective-permute-start(bf16[512,128]{1,0:T(8,128)(2,1)S(1)} %get-tuple-element.37), channel_id=1, source_target_pairs={{0,256},{64,320},{128,384},{192,448},{256,0},{320,64},{384,128},{4... | collective-permute-start | bytes 393224 | tf_op jit(solution)/shard_map/ppermute | solution.py:273
  107.0 3.1 %collective-permute-start.3 = (bf16[512,128]{1,0:T(8,128)(2,1)S(1)}, bf16[512,128]{1,0:T(8,128)(2,1)S(1)}, u32[]{:S(2)}, u32[]{:S(2)}) collective-permute-start(bf16[512,128]{1,0:T(8,128)(2,1)S(1)} %get-tuple-element.38), channel_id=1, source_target_pairs={{0,128},{64,192},{128,256},{192,320},{256,384},{320,448},{384,0},{... | collective-permute-start | bytes 393224 | tf_op jit(solution)/shard_map/ppermute | solution.py:273
  110.1 4.3 %collective-permute-start.4 = (bf16[512,128]{1,0:T(8,128)(2,1)S(1)}, bf16[512,128]{1,0:T(8,128)(2,1)S(1)}, u32[]{:S(2)}, u32[]{:S(2)}) collective-permute-start(bf16[512,128]{1,0:T(8,128)(2,1)S(1)} %get-tuple-element.39), channel_id=1, source_target_pairs={{0,384},{64,448},{128,0},{192,64},{256,128},{320,192},{384,256},{4... | collective-permute-start | bytes 393224 | tf_op jit(solution)/shard_map/ppermute | solution.py:273
  114.4 1.6 %collective-permute-done.2.refs_1_ = bf16[512,128]{1,0:T(8,128)(2,1)S(1)} collective-permute-done((bf16[512,128]{1,0:T(8,128)(2,1)S(1)}, bf16[512,128]{1,0:T(8,128)(2,1)S(1)}, u32[]{:S(2)}, u32[]{:S(2)}) %collective-permute-start.2) | collective-permute-done | bytes 131104 | tf_op jit(solution)/shard_map/ppermute | solution.py:273
  115.9 4.9 %collective-permute-done.4.refs_3_ = bf16[512,128]{1,0:T(8,128)(2,1)S(1)} collective-permute-done((bf16[512,128]{1,0:T(8,128)(2,1)S(1)}, bf16[512,128]{1,0:T(8,128)(2,1)S(1)}, u32[]{:S(2)}, u32[]{:S(2)}) %collective-permute-start.4) | collective-permute-done | bytes 131104 | tf_op jit(solution)/shard_map/ppermute | solution.py:273
  120.8 0.7 shard_map.99
  121.5 0.7 shard_map.97
  (11 shorter events, 0.1 us)
Async XLA Ops:
  29.9 21.7 %copy-start = (bf16[32,128,128]{2,1,0:T(8,128)(2,1)S(1)}, bf16[32,128,128]{2,1,0:T(8,128)(2,1)}, u32[]{:S(2)}) copy-start(bf16[32,128,128]{2,1,0:T(8,128)(2,1)} %w_in.1) | copy-start | bytes 3145732
  29.9 21.7 %copy-start.1 = (bf16[32,128,128]{2,1,0:T(8,128)(2,1)S(1)}, bf16[32,128,128]{2,1,0:T(8,128)(2,1)}, u32[]{:S(2)}) copy-start(bf16[32,128,128]{2,1,0:T(8,128)(2,1)} %w_out.1) | copy-start | bytes 3145732
  29.9 21.7 %copy-start.2 = (s32[32,2]{0,1:T(2,128)S(1)}, s32[32,2]{0,1:T(2,128)}, u32[]{:S(2)}) copy-start(s32[32,2]{0,1:T(2,128)} %param.9) | copy-start | bytes 772
  29.9 21.7 %copy-start.3 = (s32[32,2]{0,1:T(2,128)S(1)}, s32[32,2]{0,1:T(2,128)}, u32[]{:S(2)}) copy-start(s32[32,2]{0,1:T(2,128)} %param.11) | copy-start | bytes 772
  57.5 33.4 %all-to-all-start.2 = ((bf16[4,8,80,512]{3,2,1,0:T(8,128)(2,1)}), bf16[4,8,80,512]{3,2,1,0:T(8,128)(2,1)}, u32[]{:S(2)}, u32[]{:S(2)}) async-start(bf16[4,8,80,512]{3,2,1,0:T(8,128)(2,1)} %get-tuple-element.25), calls=%async_computation.2 | async-start | bytes 5242880 | tf_op jit(solution)/shard_map/all_to_all | solution.py:242
  68.8 4.6 %collective-permute-start = (bf16[8,512,128]{2,1,0:T(8,128)(2,1)S(1)}, bf16[8,512,128]{2,1,0:T(8,128)(2,1)S(1)}, u32[]{:S(2)}, u32[]{:S(2)}) collective-permute-start(bf16[8,512,128]{2,1,0:T(8,128)(2,1)S(1)} %get-tuple-element.29), channel_id=1, source_target_pairs={{0,32},{32,0},{1,33},{33,1},{2,34},{34,2},{3,35},{35,3},{4,36},{36... | collective-permute-start | bytes 3145736 | tf_op jit(solution)/shard_map/ppermute | solution.py:264
  73.6 17.2 %collective-permute-start.1 = (bf16[4,512,128]{2,1,0:T(8,128)(2,1)S(1)}, bf16[4,512,128]{2,1,0:T(8,128)(2,1)S(1)}, u32[]{:S(2)}, u32[]{:S(2)}) collective-permute-start(bf16[4,512,128]{2,1,0:T(8,128)(2,1)S(1)} %get-tuple-element.30), channel_id=1, source_target_pairs={{0,64},{32,480},{64,0},{96,160},{128,192},{160,96},{192,128},{224,... | collective-permute-start | bytes 1572872 | tf_op jit(solution)/shard_map/ppermute | solution.py:269
  94.6 26.9 %all-to-all-start.3 = ((bf16[8,80,512]{2,1,0:T(8,128)(2,1)}), bf16[8,80,512]{2,1,0:T(8,128)(2,1)S(1)}, u32[]{:S(2)}, u32[]{:S(2)}) async-start(bf16[8,80,512]{2,1,0:T(8,128)(2,1)} %shard_map.96), calls=%async_computation.3 | async-start | bytes 1310720 | tf_op jit(solution)/shard_map/all_to_all | solution.py:242
  102.4 13.5 %collective-permute-start.2 = (bf16[512,128]{1,0:T(8,128)(2,1)S(1)}, bf16[512,128]{1,0:T(8,128)(2,1)S(1)}, u32[]{:S(2)}, u32[]{:S(2)}) collective-permute-start(bf16[512,128]{1,0:T(8,128)(2,1)S(1)} %get-tuple-element.37), channel_id=1, source_target_pairs={{0,256},{64,320},{128,384},{192,448},{256,0},{320,64},{384,128},{4... | collective-permute-start | bytes 393224 | tf_op jit(solution)/shard_map/ppermute | solution.py:273
  107.0 9.0 %collective-permute-start.3 = (bf16[512,128]{1,0:T(8,128)(2,1)S(1)}, bf16[512,128]{1,0:T(8,128)(2,1)S(1)}, u32[]{:S(2)}, u32[]{:S(2)}) collective-permute-start(bf16[512,128]{1,0:T(8,128)(2,1)S(1)} %get-tuple-element.38), channel_id=1, source_target_pairs={{0,128},{64,192},{128,256},{192,320},{256,384},{320,448},{384,0},{... | collective-permute-start | bytes 393224 | tf_op jit(solution)/shard_map/ppermute | solution.py:273
  110.1 10.8 %collective-permute-start.4 = (bf16[512,128]{1,0:T(8,128)(2,1)S(1)}, bf16[512,128]{1,0:T(8,128)(2,1)S(1)}, u32[]{:S(2)}, u32[]{:S(2)}) collective-permute-start(bf16[512,128]{1,0:T(8,128)(2,1)S(1)} %get-tuple-element.39), channel_id=1, source_target_pairs={{0,384},{64,448},{128,0},{192,64},{256,128},{320,192},{384,256},{4... | collective-permute-start | bytes 393224 | tf_op jit(solution)/shard_map/ppermute | solution.py:273

commit v9 on v8

--- a/solution.py
+++ b/solution.py
@@ -80,7 +80,7 @@
 
 
 def partials_kernel(
-    where, in_l, out_l, xg_parts, w_in, w_out, act, dh, parts, xg, hidden, d_act, y, dx, stage, sems
+    where, in_l, out_l, xg_parts, w_in, w_out, act, dh, parts, xg, hidden, d_act, y, dx, sems
 ):
     core = where[0]
     gather_features(core, xg_parts, xg)
@@ -107,6 +107,7 @@
         act[row] = values.astype(act.dtype)
         dh[row] = (d_act[row] * slopes).astype(dh.dtype)
     lax.fori_loop(0, CAP, down, 0, unroll=CAP)
+    stage = xg.reshape(NEAR, FAR, OWN, 2 * T)
     copies = []
     for near in range(NEAR):
         for far in range(FAR):
@@ -145,7 +146,7 @@
                 send[slots[1][target], pl.ds(at, 2 * SUB), :] = others[target]
         return carry
 
-    lax.fori_loop(0, CAP // 2, pair, 0, unroll=4)
+    lax.fori_loop(0, CAP // 2, pair, 0, unroll=CAP // 2)
 
 
 def cores_kernel(keep, got, near, far):
@@ -169,9 +170,23 @@
         grad[...] = sum(m[part, :].astype(jnp.float32) for m in moved).astype(grad.dtype)
 
 
-def near_sum_kernel(parts, out):
-    total = sum(parts[near].astype(jnp.float32) for near in range(NEAR))
-    out[...] = total.astype(out.dtype)
+def near_sum_kernel(parts, out, held, total, in_sems, out_sems):
+    reads = [
+        pltpu.make_async_copy(parts.at[:, far], held.at[:, far], in_sems.at[far])
+        for far in range(FAR)
+    ]
+    writes = [
+        pltpu.make_async_copy(total.at[far], out.at[far], out_sems.at[far]) for far in range(FAR)
+    ]
+    for read in reads:
+        read.start()
+    for far in range(FAR):
+        reads[far].wait()
+        both = sum(held[near, far].astype(jnp.float32) for near in range(NEAR))
+        total[far] = both.astype(total.dtype)
+        writes[far].start()
+    for write in writes:
+        write.wait()
 
 
 def far_sum_kernel(parts, y, dx):
@@ -211,7 +226,6 @@
             pltpu.VMEM((FEAT, 2 * T), bf),
             *[pltpu.VMEM(UNITS, f32)] * 2,
             *[pltpu.VMEM((FEAT, T), f32)] * 2,
-            pltpu.VMEM(groups, bf),
             pltpu.SemaphoreType.DMA((NEAR,)),
         ],
         compiler_params=LIMIT,
@@ -226,13 +240,18 @@
 
 
 def near_sum_call(parts):
-    block = (2, OWN, 2 * T)
+    bf = parts.dtype
+    anywhere = pl.BlockSpec(memory_space=pl.ANY)
     return pl.pallas_call(
         near_sum_kernel,
-        grid=(FAR // block[0],),
-        out_shape=jax.ShapeDtypeStruct(parts.shape[1:], parts.dtype),
-        in_specs=[pl.BlockSpec((NEAR,) + block, lambda i: (0, i, 0, 0))],
-        out_specs=pl.BlockSpec(block, lambda i: (i, 0, 0)),
+        out_shape=pltpu.HBM(parts.shape[1:], bf),
+        in_specs=[anywhere],
+        out_specs=pl.BlockSpec(memory_space=pltpu.HBM),
+        scratch_shapes=[
+            pltpu.VMEM(parts.shape, bf),
+            pltpu.VMEM(parts.shape[1:], bf),
+            *[pltpu.SemaphoreType.DMA((FAR,))] * 2,
+        ],
         compiler_params=LIMIT,
         interpret=INTERPRET,
     )(parts)

time: 123 us -> 121 us (0.984)
  Pallas kernels: 14.2 us -> 12.2 us
    pallas_call x1, Pallas kernels: 3.72 us -> 2.47 us  [near_sum_call(): pl.pallas_call(near_sum_kernel, out_shape=pltpu.HBM(parts.shape[1:], bf),...]
where the time goes in v9:
time: 121 us; the launch traced here: 120 us
  blocking collectives  49.7 us (41%)
  starting transfers between devices  40.9 us (34%)
  waiting for transfers between devices  15.4 us (13%)
  Pallas kernels  12.2 us (10%)
    all_to_all x2, blocking collectives, exchange(): lax.all_to_all(x, ('c', 'x', 'y'), split_axis=0, concat_axis=0, axis_inde...  49.7 us
    all_to_all x2, starting transfers between devices, exchange(): lax.all_to_all(x, ('c', 'x', 'y'), split_axis=0, concat_axis=0, axis_inde...  16.2 us
    ppermute x3, starting transfers between devices, body(): lax.ppermute(steps[k - 1], 'z', [(z, (z + 2 * k) % Z) for z in range(Z)])  11.9 us
    ppermute x1, starting transfers between devices, body(): got = lax.ppermute(far, ('z', 'c'), pairs)  10.7 us
    ppermute x1, waiting for transfers between devices, body(): got = lax.ppermute(far, ('z', 'c'), pairs)  6.56 us
    ppermute x3, waiting for transfers between devices, body(): lax.ppermute(steps[k - 1], 'z', [(z, (z + 2 * k) % Z) for z in range(Z)])  6.43 us
    pallas_call x1, Pallas kernels, partials_call(): pl.pallas_call(partials_kernel, out_shape=(*[jax.ShapeDtypeStruct(UNITS,...  5.95 us
    pallas_call x5, Pallas kernels, call(): pl.pallas_call(kernel, out_shape=tuple((jax.ShapeDtypeStruct(dims, bf) fo...  3.82 us
  transfers between devices with their start and end apart: 7, of which 4 were waited for; matrix products, arithmetic and copies ran while one was open for 0% of the time, Pallas kernels for 3%

profile of v9, /device:TPU:1, one launch (start us, length us, event | category | flops | bytes accessed | tf_op | source)
XLA Modules:
  0.0 120.3 jit_solution(316801369595744635)
XLA Ops:
  0.6 0.1 pad_add_fusion.where
  0.7 0.8 pad_maximum_fusion
  1.6 28.0 %all_to_all.20 = bf16[8,80,512]{2,1,0:T(8,128)(2,1)S(1)} all-to-all(bf16[8,80,512]{2,1,0:T(8,128)(2,1)S(1)} %broadcast_in_dim.4), channel_id=1, replica_groups={{0,2,4,6,16,18,20,22},{1,3,5,7,17,19,21,23},{8,10,12,14,24,26,28,30},{9..., dimensions={0} | all-to-all | bytes 1310720 | tf_op jit(solution)/shard_map/all_to_all | solution.py:261
  29.6 0.3 broadcast_in_dim.5
  29.9 0.0 copy-start
  29.9 21.7 %all_to_all.21.xg_parts = bf16[4,8,80,512]{3,2,1,0:T(8,128)(2,1)S(1)} all-to-all(bf16[4,8,80,512]{3,2,1,0:T(8,128)(2,1)S(1)} %broadcast_in_dim.5), channel_id=1, replica_groups={{0,1,8,9},{2,3,10,11},{4,5,12,13},{6,7,14,15},{16,17,24,25},{18,19,26,2..., dimensions={0} | all-to-all | bytes 5242880 | tf_op jit(solution)/shard_map/all_to_all | solution.py:261
  51.6 5.9 %shard_map.93 = (bf16[5,128,256]{2,1,0:T(8,128)(2,1)S(1)}, bf16[5,128,256]{2,1,0:T(8,128)(2,1)S(1)}, bf16[4,8,80,512]{3,2,1,0:T(8,128)(2,1)}) custom-call(s32[2]{0:T(128)S(1)} %pad_add_fusion.where, s32[2,32]{1,0:T(2,128)S(1)} %bitcast.10, s32[2,32]{1,0:T(2,128)S(1)} %bitcast.12, bf16[4,8,80,512]{3,2,1,0:T(8,128)(2,1)S(1)} %all_to_all.21.xg_parts, ...), custom_call_target="tpu_custom_call" | custom-call | tf_op jit(solution)/shard_map/pallas_call | solution.py:220
  57.6 8.5 %all-to-all-start.2 = ((bf16[4,8,80,512]{3,2,1,0:T(8,128)(2,1)}), bf16[4,8,80,512]{3,2,1,0:T(8,128)(2,1)}, u32[]{:S(2)}, u32[]{:S(2)}) async-start(bf16[4,8,80,512]{3,2,1,0:T(8,128)(2,1)} %get-tuple-element.25), calls=%async_computation.2 | async-start | bytes 5242880 | tf_op jit(solution)/shard_map/all_to_all | solution.py:261
  66.1 2.1 %shard_map.94 = (bf16[8,512,128]{2,1,0:T(8,128)(2,1)S(1)}, bf16[8,512,128]{2,1,0:T(8,128)(2,1)S(1)}) custom-call(s32[2]{0:T(128)S(1)} %pad_add_fusion.where, s32[2,32]{1,0:T(2,128)S(1)} %bitcast.11, s32[2,32]{1,0:T(2,128)S(1)} %bitcast.13, bf16[4,8,80,512]{3,2,1,0:T(8,128)(2,1)S(1)} %all_to_all.21.xg_parts, bf16[5,128,256]{2,1,0:T(8,128)(2,1)S(1)} %get-tuple-element.26.act, ...), custom_call_target="tpu_custom_call" | custom-call | tf_op jit(solution)/shard_map/pallas_call | solution.py:206
  68.1 2.1 %collective-permute-start = (bf16[8,512,128]{2,1,0:T(8,128)(2,1)S(1)}, bf16[8,512,128]{2,1,0:T(8,128)(2,1)S(1)}, u32[]{:S(2)}, u32[]{:S(2)}) collective-permute-start(bf16[8,512,128]{2,1,0:T(8,128)(2,1)S(1)} %get-tuple-element.29), channel_id=1, source_target_pairs={{0,32},{32,0},{1,33},{33,1},{2,34},{34,2},{3,35},{35,3},{4,36},{36... | collective-permute-start | bytes 3145736 | tf_op jit(solution)/shard_map/ppermute | solution.py:283
  70.3 2.4 %collective-permute-done.got = bf16[8,512,128]{2,1,0:T(8,128)(2,1)S(1)} collective-permute-done((bf16[8,512,128]{2,1,0:T(8,128)(2,1)S(1)}, bf16[8,512,128]{2,1,0:T(8,128)(2,1)S(1)}, u32[]{:S(2)}, u32[]{:S(2)}) %collective-permute-start) | collective-permute-done | bytes 1048608 | tf_op jit(solution)/shard_map/ppermute | solution.py:283
  72.7 0.2 shard_map.95
  72.9 10.7 %collective-permute-start.1 = (bf16[4,512,128]{2,1,0:T(8,128)(2,1)S(1)}, bf16[4,512,128]{2,1,0:T(8,128)(2,1)S(1)}, u32[]{:S(2)}, u32[]{:S(2)}) collective-permute-start(bf16[4,512,128]{2,1,0:T(8,128)(2,1)S(1)} %get-tuple-element.30), channel_id=1, source_target_pairs={{0,64},{32,480},{64,0},{96,160},{128,192},{160,96},{192,128},{224,... | collective-permute-start | bytes 1572872 | tf_op jit(solution)/shard_map/ppermute | solution.py:288
  83.6 6.6 %collective-permute-done.1.got = bf16[4,512,128]{2,1,0:T(8,128)(2,1)S(1)} collective-permute-done((bf16[4,512,128]{2,1,0:T(8,128)(2,1)S(1)}, bf16[4,512,128]{2,1,0:T(8,128)(2,1)S(1)}, u32[]{:S(2)}, u32[]{:S(2)}) %collective-permute-start.1) | collective-permute-done | bytes 524320 | tf_op jit(solution)/shard_map/ppermute | solution.py:288
  90.2 2.5 %shard_map.96 = bf16[8,80,512]{2,1,0:T(8,128)(2,1)} custom-call(bf16[4,8,80,512]{3,2,1,0:T(8,128)(2,1)} %all-to-all-done.2.parts), custom_call_target="tpu_custom_call" | custom-call | tf_op jit(solution)/shard_map/pallas_call | solution.py:245
  92.7 7.7 %all-to-all-start.3 = ((bf16[8,80,512]{2,1,0:T(8,128)(2,1)}), bf16[8,80,512]{2,1,0:T(8,128)(2,1)S(1)}, u32[]{:S(2)}, u32[]{:S(2)}) async-start(bf16[8,80,512]{2,1,0:T(8,128)(2,1)} %shard_map.96), calls=%async_computation.3 | async-start | bytes 1310720 | tf_op jit(solution)/shard_map/all_to_all | solution.py:261
  100.4 0.1 shard_map.98
  100.5 4.5 %collective-permute-start.2 = (bf16[512,128]{1,0:T(8,128)(2,1)S(1)}, bf16[512,128]{1,0:T(8,128)(2,1)S(1)}, u32[]{:S(2)}, u32[]{:S(2)}) collective-permute-start(bf16[512,128]{1,0:T(8,128)(2,1)S(1)} %get-tuple-element.37), channel_id=1, source_target_pairs={{0,256},{64,320},{128,384},{192,448},{256,0},{320,64},{384,128},{4... | collective-permute-start | bytes 393224 | tf_op jit(solution)/shard_map/ppermute | solution.py:292
  105.0 3.1 %collective-permute-start.3 = (bf16[512,128]{1,0:T(8,128)(2,1)S(1)}, bf16[512,128]{1,0:T(8,128)(2,1)S(1)}, u32[]{:S(2)}, u32[]{:S(2)}) collective-permute-start(bf16[512,128]{1,0:T(8,128)(2,1)S(1)} %get-tuple-element.38), channel_id=1, source_target_pairs={{0,128},{64,192},{128,256},{192,320},{256,384},{320,448},{384,0},{... | collective-permute-start | bytes 393224 | tf_op jit(solution)/shard_map/ppermute | solution.py:292
  108.1 4.3 %collective-permute-start.4 = (bf16[512,128]{1,0:T(8,128)(2,1)S(1)}, bf16[512,128]{1,0:T(8,128)(2,1)S(1)}, u32[]{:S(2)}, u32[]{:S(2)}) collective-permute-start(bf16[512,128]{1,0:T(8,128)(2,1)S(1)} %get-tuple-element.39), channel_id=1, source_target_pairs={{0,384},{64,448},{128,0},{192,64},{256,128},{320,192},{384,256},{4... | collective-permute-start | bytes 393224 | tf_op jit(solution)/shard_map/ppermute | solution.py:292
  112.4 1.6 %collective-permute-done.2.refs_1_ = bf16[512,128]{1,0:T(8,128)(2,1)S(1)} collective-permute-done((bf16[512,128]{1,0:T(8,128)(2,1)S(1)}, bf16[512,128]{1,0:T(8,128)(2,1)S(1)}, u32[]{:S(2)}, u32[]{:S(2)}) %collective-permute-start.2) | collective-permute-done | bytes 131104 | tf_op jit(solution)/shard_map/ppermute | solution.py:292
  114.0 4.9 %collective-permute-done.4.refs_3_ = bf16[512,128]{1,0:T(8,128)(2,1)S(1)} collective-permute-done((bf16[512,128]{1,0:T(8,128)(2,1)S(1)}, bf16[512,128]{1,0:T(8,128)(2,1)S(1)}, u32[]{:S(2)}, u32[]{:S(2)}) %collective-permute-start.4) | collective-permute-done | bytes 131104 | tf_op jit(solution)/shard_map/ppermute | solution.py:292
  118.9 0.7 shard_map.99
  119.6 0.7 shard_map.97
  (11 shorter events, 0.1 us)
Async XLA Ops:
  29.9 21.7 %copy-start = (bf16[32,128,128]{2,1,0:T(8,128)(2,1)S(1)}, bf16[32,128,128]{2,1,0:T(8,128)(2,1)}, u32[]{:S(2)}) copy-start(bf16[32,128,128]{2,1,0:T(8,128)(2,1)} %w_in.1) | copy-start | bytes 3145732
  29.9 21.7 %copy-start.1 = (bf16[32,128,128]{2,1,0:T(8,128)(2,1)S(1)}, bf16[32,128,128]{2,1,0:T(8,128)(2,1)}, u32[]{:S(2)}) copy-start(bf16[32,128,128]{2,1,0:T(8,128)(2,1)} %w_out.1) | copy-start | bytes 3145732
  29.9 21.7 %copy-start.2 = (s32[32,2]{0,1:T(2,128)S(1)}, s32[32,2]{0,1:T(2,128)}, u32[]{:S(2)}) copy-start(s32[32,2]{0,1:T(2,128)} %param.9) | copy-start | bytes 772
  29.9 21.7 %copy-start.3 = (s32[32,2]{0,1:T(2,128)S(1)}, s32[32,2]{0,1:T(2,128)}, u32[]{:S(2)}) copy-start(s32[32,2]{0,1:T(2,128)} %param.11) | copy-start | bytes 772
  57.6 32.6 %all-to-all-start.2 = ((bf16[4,8,80,512]{3,2,1,0:T(8,128)(2,1)}), bf16[4,8,80,512]{3,2,1,0:T(8,128)(2,1)}, u32[]{:S(2)}, u32[]{:S(2)}) async-start(bf16[4,8,80,512]{3,2,1,0:T(8,128)(2,1)} %get-tuple-element.25), calls=%async_computation.2 | async-start | bytes 5242880 | tf_op jit(solution)/shard_map/all_to_all | solution.py:261
  68.1 4.6 %collective-permute-start = (bf16[8,512,128]{2,1,0:T(8,128)(2,1)S(1)}, bf16[8,512,128]{2,1,0:T(8,128)(2,1)S(1)}, u32[]{:S(2)}, u32[]{:S(2)}) collective-permute-start(bf16[8,512,128]{2,1,0:T(8,128)(2,1)S(1)} %get-tuple-element.29), channel_id=1, source_target_pairs={{0,32},{32,0},{1,33},{33,1},{2,34},{34,2},{3,35},{35,3},{4,36},{36... | collective-permute-start | bytes 3145736 | tf_op jit(solution)/shard_map/ppermute | solution.py:283
  72.9 17.2 %collective-permute-start.1 = (bf16[4,512,128]{2,1,0:T(8,128)(2,1)S(1)}, bf16[4,512,128]{2,1,0:T(8,128)(2,1)S(1)}, u32[]{:S(2)}, u32[]{:S(2)}) collective-permute-start(bf16[4,512,128]{2,1,0:T(8,128)(2,1)S(1)} %get-tuple-element.30), channel_id=1, source_target_pairs={{0,64},{32,480},{64,0},{96,160},{128,192},{160,96},{192,128},{224,... | collective-permute-start | bytes 1572872 | tf_op jit(solution)/shard_map/ppermute | solution.py:288
  92.7 26.9 %all-to-all-start.3 = ((bf16[8,80,512]{2,1,0:T(8,128)(2,1)}), bf16[8,80,512]{2,1,0:T(8,128)(2,1)S(1)}, u32[]{:S(2)}, u32[]{:S(2)}) async-start(bf16[8,80,512]{2,1,0:T(8,128)(2,1)} %shard_map.96), calls=%async_computation.3 | async-start | bytes 1310720 | tf_op jit(solution)/shard_map/all_to_all | solution.py:261
  100.5 13.5 %collective-permute-start.2 = (bf16[512,128]{1,0:T(8,128)(2,1)S(1)}, bf16[512,128]{1,0:T(8,128)(2,1)S(1)}, u32[]{:S(2)}, u32[]{:S(2)}) collective-permute-start(bf16[512,128]{1,0:T(8,128)(2,1)S(1)} %get-tuple-element.37), channel_id=1, source_target_pairs={{0,256},{64,320},{128,384},{192,448},{256,0},{320,64},{384,128},{4... | collective-permute-start | bytes 393224 | tf_op jit(solution)/shard_map/ppermute | solution.py:292
  105.0 9.0 %collective-permute-start.3 = (bf16[512,128]{1,0:T(8,128)(2,1)S(1)}, bf16[512,128]{1,0:T(8,128)(2,1)S(1)}, u32[]{:S(2)}, u32[]{:S(2)}) collective-permute-start(bf16[512,128]{1,0:T(8,128)(2,1)S(1)} %get-tuple-element.38), channel_id=1, source_target_pairs={{0,128},{64,192},{128,256},{192,320},{256,384},{320,448},{384,0},{... | collective-permute-start | bytes 393224 | tf_op jit(solution)/shard_map/ppermute | solution.py:292
  108.1 10.7 %collective-permute-start.4 = (bf16[512,128]{1,0:T(8,128)(2,1)S(1)}, bf16[512,128]{1,0:T(8,128)(2,1)S(1)}, u32[]{:S(2)}, u32[]{:S(2)}) collective-permute-start(bf16[512,128]{1,0:T(8,128)(2,1)S(1)} %get-tuple-element.39), channel_id=1, source_target_pairs={{0,384},{64,448},{128,0},{192,64},{256,128},{320,192},{384,256},{4... | collective-permute-start | bytes 393224 | tf_op jit(solution)/shard_map/ppermute | solution.py:292

commit v10 on v9

--- a/solution.py
+++ b/solution.py
@@ -162,14 +162,6 @@
         out[...] = both.astype(out.dtype)
 
 
-def last_kernel(*refs):
-    *moved, out_grad, in_grad = refs
-    rows = CAP * SUB
-    for i, grad in enumerate((out_grad, in_grad)):
-        part = slice(i * rows, (i + 1) * rows)
-        grad[...] = sum(m[part, :].astype(jnp.float32) for m in moved).astype(grad.dtype)
-
-
 def near_sum_kernel(parts, out, held, total, in_sems, out_sems):
     reads = [
         pltpu.make_async_copy(parts.at[:, far], held.at[:, far], in_sems.at[far])
@@ -189,10 +181,15 @@
         write.wait()
 
 
-def far_sum_kernel(parts, y, dx):
+def last_kernel(parts, *refs):
+    *moved, y, dx, out_grad, in_grad = refs
     total = sum(parts[far].astype(jnp.float32) for far in range(FAR)).astype(y.dtype)
     y[...] = total[:, :T]
     dx[...] = total[:, T:]
+    rows = CAP * SUB
+    for i, grad in enumerate((out_grad, in_grad)):
+        part = slice(i * rows, (i + 1) * rows)
+        grad[...] = sum(m[part, :].astype(jnp.float32) for m in moved).astype(grad.dtype)
 
 
 SMEM = pl.BlockSpec(memory_space=pltpu.SMEM)
@@ -293,8 +290,8 @@
         for k in (2, 1, 3)
     ]
     parts = exchange(near_sum_call(parts), FAR_GROUPS)
-    y, dx = call(far_sum_kernel, (), (parts,), ((OWN, T),) * 2)
-    grads = call(last_kernel, (), (own, *moved), ((CAP * SUB, BLK),) * 2)
+    outs = ((OWN, T),) * 2 + ((CAP * SUB, BLK),) * 2
+    y, dx, *grads = call(last_kernel, (), (parts, own, *moved), outs)
     out_grad, in_grad = (grad.reshape(CAP, SUB, BLK) for grad in grads)
     return y.T, dx.T, in_grad, out_grad
 

time: 121 us -> 120 us (level)
    pallas_call x5 -> x4, Pallas kernels: 3.82 us -> 3.2 us  [call(): pl.pallas_call(kernel, out_shape=tuple((jax.ShapeDtypeStruct(dims, bf) fo...]
  transfers between devices with their start and end apart: 7 -> 7, of which waited for: 4 -> 4; matrix products, arithmetic and copies ran while one was open for 0% -> 0% of each run, Pallas kernels for 3% -> 2%
where the time goes in v10:
time: 120 us
  blocking collectives  49.7 us (41%)
  starting transfers between devices  40.9 us (34%)
  waiting for transfers between devices  15.4 us (13%)
  Pallas kernels  11.6 us (10%)
    all_to_all x2, blocking collectives, exchange(): lax.all_to_all(x, ('c', 'x', 'y'), split_axis=0, concat_axis=0, axis_inde...  49.7 us
    all_to_all x2, starting transfers between devices, exchange(): lax.all_to_all(x, ('c', 'x', 'y'), split_axis=0, concat_axis=0, axis_inde...  16.2 us
    ppermute x3, starting transfers between devices, body(): lax.ppermute(steps[k - 1], 'z', [(z, (z + 2 * k) % Z) for z in range(Z)])  11.9 us
    ppermute x1, starting transfers between devices, body(): got = lax.ppermute(far, ('z', 'c'), pairs)  10.7 us
    ppermute x1, waiting for transfers between devices, body(): got = lax.ppermute(far, ('z', 'c'), pairs)  6.56 us
    ppermute x3, waiting for transfers between devices, body(): lax.ppermute(steps[k - 1], 'z', [(z, (z + 2 * k) % Z) for z in range(Z)])  6.42 us
    pallas_call x1, Pallas kernels, partials_call(): pl.pallas_call(partials_kernel, out_shape=(*[jax.ShapeDtypeStruct(UNITS,...  5.94 us
    pallas_call x4, Pallas kernels, call(): pl.pallas_call(kernel, out_shape=tuple((jax.ShapeDtypeStruct(dims, bf) fo...  3.2 us
  transfers between devices with their start and end apart: 7, of which 4 were waited for; matrix products, arithmetic and copies ran while one was open for 0% of the time, Pallas kernels for 2%

profile of v10, /device:TPU:1, one launch (start us, length us, event | category | flops | bytes accessed | tf_op | source)
XLA Modules:
  0.0 119.6 jit_solution(8326994601076188933)
XLA Ops:
  0.6 0.1 pad_add_fusion.where
  0.7 0.8 pad_maximum_fusion
  1.6 28.0 %all_to_all.20 = bf16[8,80,512]{2,1,0:T(8,128)(2,1)S(1)} all-to-all(bf16[8,80,512]{2,1,0:T(8,128)(2,1)S(1)} %broadcast_in_dim.4), channel_id=1, replica_groups={{0,2,4,6,16,18,20,22},{1,3,5,7,17,19,21,23},{8,10,12,14,24,26,28,30},{9..., dimensions={0} | all-to-all | bytes 1310720 | tf_op jit(solution)/shard_map/all_to_all | solution.py:258
  29.6 0.3 broadcast_in_dim.5
  29.9 0.0 copy-start.1
  29.9 0.0 copy-start.2
  29.9 21.7 %all_to_all.21.xg_parts = bf16[4,8,80,512]{3,2,1,0:T(8,128)(2,1)S(1)} all-to-all(bf16[4,8,80,512]{3,2,1,0:T(8,128)(2,1)S(1)} %broadcast_in_dim.5), channel_id=1, replica_groups={{0,1,8,9},{2,3,10,11},{4,5,12,13},{6,7,14,15},{16,17,24,25},{18,19,26,2..., dimensions={0} | all-to-all | bytes 5242880 | tf_op jit(solution)/shard_map/all_to_all | solution.py:258
  51.6 5.9 %shard_map.93 = (bf16[5,128,256]{2,1,0:T(8,128)(2,1)S(1)}, bf16[5,128,256]{2,1,0:T(8,128)(2,1)S(1)}, bf16[4,8,80,512]{3,2,1,0:T(8,128)(2,1)}) custom-call(s32[2]{0:T(128)S(1)} %pad_add_fusion.where, s32[2,32]{1,0:T(2,128)S(1)} %bitcast.10, s32[2,32]{1,0:T(2,128)S(1)} %bitcast.12, bf16[4,8,80,512]{3,2,1,0:T(8,128)(2,1)S(1)} %all_to_all.21.xg_parts, ...), custom_call_target="tpu_custom_call" | custom-call | tf_op jit(solution)/shard_map/pallas_call | solution.py:217
  57.5 8.5 %all-to-all-start.2 = ((bf16[4,8,80,512]{3,2,1,0:T(8,128)(2,1)}), bf16[4,8,80,512]{3,2,1,0:T(8,128)(2,1)}, u32[]{:S(2)}, u32[]{:S(2)}) async-start(bf16[4,8,80,512]{3,2,1,0:T(8,128)(2,1)} %get-tuple-element.25), calls=%async_computation.2 | async-start | bytes 5242880 | tf_op jit(solution)/shard_map/all_to_all | solution.py:258
  66.1 2.1 %shard_map.94 = (bf16[8,512,128]{2,1,0:T(8,128)(2,1)S(1)}, bf16[8,512,128]{2,1,0:T(8,128)(2,1)S(1)}) custom-call(s32[2]{0:T(128)S(1)} %pad_add_fusion.where, s32[2,32]{1,0:T(2,128)S(1)} %bitcast.11, s32[2,32]{1,0:T(2,128)S(1)} %bitcast.13, bf16[4,8,80,512]{3,2,1,0:T(8,128)(2,1)S(1)} %all_to_all.21.xg_parts, bf16[5,128,256]{2,1,0:T(8,128)(2,1)S(1)} %get-tuple-element.26.act, ...), custom_call_target="tpu_custom_call" | custom-call | tf_op jit(solution)/shard_map/pallas_call | solution.py:203
  68.1 2.1 %collective-permute-start = (bf16[8,512,128]{2,1,0:T(8,128)(2,1)S(1)}, bf16[8,512,128]{2,1,0:T(8,128)(2,1)S(1)}, u32[]{:S(2)}, u32[]{:S(2)}) collective-permute-start(bf16[8,512,128]{2,1,0:T(8,128)(2,1)S(1)} %get-tuple-element.29), channel_id=1, source_target_pairs={{0,32},{32,0},{1,33},{33,1},{2,34},{34,2},{3,35},{35,3},{4,36},{36... | collective-permute-start | bytes 3145736 | tf_op jit(solution)/shard_map/ppermute | solution.py:280
  70.3 2.4 %collective-permute-done.got = bf16[8,512,128]{2,1,0:T(8,128)(2,1)S(1)} collective-permute-done((bf16[8,512,128]{2,1,0:T(8,128)(2,1)S(1)}, bf16[8,512,128]{2,1,0:T(8,128)(2,1)S(1)}, u32[]{:S(2)}, u32[]{:S(2)}) %collective-permute-start) | collective-permute-done | bytes 1048608 | tf_op jit(solution)/shard_map/ppermute | solution.py:280
  72.7 0.2 shard_map.95
  72.9 10.7 %collective-permute-start.1 = (bf16[4,512,128]{2,1,0:T(8,128)(2,1)S(1)}, bf16[4,512,128]{2,1,0:T(8,128)(2,1)S(1)}, u32[]{:S(2)}, u32[]{:S(2)}) collective-permute-start(bf16[4,512,128]{2,1,0:T(8,128)(2,1)S(1)} %get-tuple-element.30), channel_id=1, source_target_pairs={{0,64},{32,480},{64,0},{96,160},{128,192},{160,96},{192,128},{224,... | collective-permute-start | bytes 1572872 | tf_op jit(solution)/shard_map/ppermute | solution.py:285
  83.6 6.6 %collective-permute-done.1.got = bf16[4,512,128]{2,1,0:T(8,128)(2,1)S(1)} collective-permute-done((bf16[4,512,128]{2,1,0:T(8,128)(2,1)S(1)}, bf16[4,512,128]{2,1,0:T(8,128)(2,1)S(1)}, u32[]{:S(2)}, u32[]{:S(2)}) %collective-permute-start.1) | collective-permute-done | bytes 524320 | tf_op jit(solution)/shard_map/ppermute | solution.py:285
  90.2 2.5 %shard_map.96 = bf16[8,80,512]{2,1,0:T(8,128)(2,1)} custom-call(bf16[4,8,80,512]{3,2,1,0:T(8,128)(2,1)} %all-to-all-done.2.parts), custom_call_target="tpu_custom_call" | custom-call | tf_op jit(solution)/shard_map/pallas_call | solution.py:242
  92.7 7.7 %all-to-all-start.3 = ((bf16[8,80,512]{2,1,0:T(8,128)(2,1)}), bf16[8,80,512]{2,1,0:T(8,128)(2,1)S(1)}, u32[]{:S(2)}, u32[]{:S(2)}) async-start(bf16[8,80,512]{2,1,0:T(8,128)(2,1)} %shard_map.96), calls=%async_computation.3 | async-start | bytes 1310720 | tf_op jit(solution)/shard_map/all_to_all | solution.py:258
  100.4 0.1 shard_map.97
  100.5 4.5 %collective-permute-start.2 = (bf16[512,128]{1,0:T(8,128)(2,1)S(1)}, bf16[512,128]{1,0:T(8,128)(2,1)S(1)}, u32[]{:S(2)}, u32[]{:S(2)}) collective-permute-start(bf16[512,128]{1,0:T(8,128)(2,1)S(1)} %get-tuple-element.35), channel_id=1, source_target_pairs={{0,256},{64,320},{128,384},{192,448},{256,0},{320,64},{384,128},{4... | collective-permute-start | bytes 393224 | tf_op jit(solution)/shard_map/ppermute | solution.py:289
  105.0 3.1 %collective-permute-start.3 = (bf16[512,128]{1,0:T(8,128)(2,1)S(1)}, bf16[512,128]{1,0:T(8,128)(2,1)S(1)}, u32[]{:S(2)}, u32[]{:S(2)}) collective-permute-start(bf16[512,128]{1,0:T(8,128)(2,1)S(1)} %get-tuple-element.36), channel_id=1, source_target_pairs={{0,128},{64,192},{128,256},{192,320},{256,384},{320,448},{384,0},{... | collective-permute-start | bytes 393224 | tf_op jit(solution)/shard_map/ppermute | solution.py:289
  108.1 4.3 %collective-permute-start.4 = (bf16[512,128]{1,0:T(8,128)(2,1)S(1)}, bf16[512,128]{1,0:T(8,128)(2,1)S(1)}, u32[]{:S(2)}, u32[]{:S(2)}) collective-permute-start(bf16[512,128]{1,0:T(8,128)(2,1)S(1)} %get-tuple-element.37), channel_id=1, source_target_pairs={{0,384},{64,448},{128,0},{192,64},{256,128},{320,192},{384,256},{4... | collective-permute-start | bytes 393224 | tf_op jit(solution)/shard_map/ppermute | solution.py:289
  112.4 1.6 %collective-permute-done.2.refs_1_ = bf16[512,128]{1,0:T(8,128)(2,1)S(1)} collective-permute-done((bf16[512,128]{1,0:T(8,128)(2,1)S(1)}, bf16[512,128]{1,0:T(8,128)(2,1)S(1)}, u32[]{:S(2)}, u32[]{:S(2)}) %collective-permute-start.2) | collective-permute-done | bytes 131104 | tf_op jit(solution)/shard_map/ppermute | solution.py:289
  114.0 4.9 %collective-permute-done.4.refs_3_ = bf16[512,128]{1,0:T(8,128)(2,1)S(1)} collective-permute-done((bf16[512,128]{1,0:T(8,128)(2,1)S(1)}, bf16[512,128]{1,0:T(8,128)(2,1)S(1)}, u32[]{:S(2)}, u32[]{:S(2)}) %collective-permute-start.4) | collective-permute-done | bytes 131104 | tf_op jit(solution)/shard_map/ppermute | solution.py:289
  118.9 0.8 shard_map.98
  (10 shorter events, 0.1 us)
Async XLA Ops:
  29.9 21.7 %copy-start = (bf16[32,128,128]{2,1,0:T(8,128)(2,1)S(1)}, bf16[32,128,128]{2,1,0:T(8,128)(2,1)}, u32[]{:S(2)}) copy-start(bf16[32,128,128]{2,1,0:T(8,128)(2,1)} %w_in.1) | copy-start | bytes 3145732
  29.9 21.7 %copy-start.1 = (bf16[32,128,128]{2,1,0:T(8,128)(2,1)S(1)}, bf16[32,128,128]{2,1,0:T(8,128)(2,1)}, u32[]{:S(2)}) copy-start(bf16[32,128,128]{2,1,0:T(8,128)(2,1)} %w_out.1) | copy-start | bytes 3145732
  29.9 21.7 %copy-start.2 = (s32[32,2]{0,1:T(2,128)S(1)}, s32[32,2]{0,1:T(2,128)}, u32[]{:S(2)}) copy-start(s32[32,2]{0,1:T(2,128)} %param.9) | copy-start | bytes 772
  29.9 21.7 %copy-start.3 = (s32[32,2]{0,1:T(2,128)S(1)}, s32[32,2]{0,1:T(2,128)}, u32[]{:S(2)}) copy-start(s32[32,2]{0,1:T(2,128)} %param.11) | copy-start | bytes 772
  57.5 32.6 %all-to-all-start.2 = ((bf16[4,8,80,512]{3,2,1,0:T(8,128)(2,1)}), bf16[4,8,80,512]{3,2,1,0:T(8,128)(2,1)}, u32[]{:S(2)}, u32[]{:S(2)}) async-start(bf16[4,8,80,512]{3,2,1,0:T(8,128)(2,1)} %get-tuple-element.25), calls=%async_computation.2 | async-start | bytes 5242880 | tf_op jit(solution)/shard_map/all_to_all | solution.py:258
  68.1 4.6 %collective-permute-start = (bf16[8,512,128]{2,1,0:T(8,128)(2,1)S(1)}, bf16[8,512,128]{2,1,0:T(8,128)(2,1)S(1)}, u32[]{:S(2)}, u32[]{:S(2)}) collective-permute-start(bf16[8,512,128]{2,1,0:T(8,128)(2,1)S(1)} %get-tuple-element.29), channel_id=1, source_target_pairs={{0,32},{32,0},{1,33},{33,1},{2,34},{34,2},{3,35},{35,3},{4,36},{36... | collective-permute-start | bytes 3145736 | tf_op jit(solution)/shard_map/ppermute | solution.py:280
  72.9 17.2 %collective-permute-start.1 = (bf16[4,512,128]{2,1,0:T(8,128)(2,1)S(1)}, bf16[4,512,128]{2,1,0:T(8,128)(2,1)S(1)}, u32[]{:S(2)}, u32[]{:S(2)}) collective-permute-start(bf16[4,512,128]{2,1,0:T(8,128)(2,1)S(1)} %get-tuple-element.30), channel_id=1, source_target_pairs={{0,64},{32,480},{64,0},{96,160},{128,192},{160,96},{192,128},{224,... | collective-permute-start | bytes 1572872 | tf_op jit(solution)/shard_map/ppermute | solution.py:285
  92.7 26.2 %all-to-all-start.3 = ((bf16[8,80,512]{2,1,0:T(8,128)(2,1)}), bf16[8,80,512]{2,1,0:T(8,128)(2,1)S(1)}, u32[]{:S(2)}, u32[]{:S(2)}) async-start(bf16[8,80,512]{2,1,0:T(8,128)(2,1)} %shard_map.96), calls=%async_computation.3 | async-start | bytes 1310720 | tf_op jit(solution)/shard_map/all_to_all | solution.py:258
  100.5 13.5 %collective-permute-start.2 = (bf16[512,128]{1,0:T(8,128)(2,1)S(1)}, bf16[512,128]{1,0:T(8,128)(2,1)S(1)}, u32[]{:S(2)}, u32[]{:S(2)}) collective-permute-start(bf16[512,128]{1,0:T(8,128)(2,1)S(1)} %get-tuple-element.35), channel_id=1, source_target_pairs={{0,256},{64,320},{128,384},{192,448},{256,0},{320,64},{384,128},{4... | collective-permute-start | bytes 393224 | tf_op jit(solution)/shard_map/ppermute | solution.py:289
  105.0 9.0 %collective-permute-start.3 = (bf16[512,128]{1,0:T(8,128)(2,1)S(1)}, bf16[512,128]{1,0:T(8,128)(2,1)S(1)}, u32[]{:S(2)}, u32[]{:S(2)}) collective-permute-start(bf16[512,128]{1,0:T(8,128)(2,1)S(1)} %get-tuple-element.36), channel_id=1, source_target_pairs={{0,128},{64,192},{128,256},{192,320},{256,384},{320,448},{384,0},{... | collective-permute-start | bytes 393224 | tf_op jit(solution)/shard_map/ppermute | solution.py:289
  108.1 10.7 %collective-permute-start.4 = (bf16[512,128]{1,0:T(8,128)(2,1)S(1)}, bf16[512,128]{1,0:T(8,128)(2,1)S(1)}, u32[]{:S(2)}, u32[]{:S(2)}) collective-permute-start(bf16[512,128]{1,0:T(8,128)(2,1)S(1)} %get-tuple-element.37), channel_id=1, source_target_pairs={{0,384},{64,448},{128,0},{192,64},{256,128},{320,192},{384,256},{4... | collective-permute-start | bytes 393224 | tf_op jit(solution)/shard_map/ppermute | solution.py:289

commit v11 on v10

--- a/solution.py
+++ b/solution.py
@@ -287,7 +287,7 @@
     own, *steps = call(pairs_kernel, (), (near, got), (STEP,) * HALF)
     moved = [
         lax.ppermute(steps[k - 1], "z", [(z, (z + 2 * k) % Z) for z in range(Z)])
-        for k in (2, 1, 3)
+        for k in (1, 3, 2)
     ]
     parts = exchange(near_sum_call(parts), FAR_GROUPS)
     outs = ((OWN, T),) * 2 + ((CAP * SUB, BLK),) * 2

time: 120 us -> 122 us (1.017)
  waiting for transfers between devices: 15.4 us -> 16.7 us
    ppermute x3, waiting for transfers between devices: 6.42 us -> 7.71 us  [body(): lax.ppermute(steps[k - 1], 'z', [(z, (z + 2 * k) % Z) for z in range(Z)])]
  transfers between devices with their start and end apart: 7 -> 7, of which waited for: 4 -> 3; matrix products, arithmetic and copies ran while one was open for 0% -> 0% of each run, Pallas kernels for 2% -> 2%
where the time goes in v11:
time: 122 us; the launch traced here: 121 us
  blocking collectives  49.7 us (41%)
  starting transfers between devices  40.9 us (34%)
  waiting for transfers between devices  16.7 us (14%)
  Pallas kernels  11.6 us (10%)
    all_to_all x2, blocking collectives, exchange(): lax.all_to_all(x, ('c', 'x', 'y'), split_axis=0, concat_axis=0, axis_inde...  49.7 us
    all_to_all x2, starting transfers between devices, exchange(): lax.all_to_all(x, ('c', 'x', 'y'), split_axis=0, concat_axis=0, axis_inde...  16.2 us
    ppermute x3, starting transfers between devices, body(): lax.ppermute(steps[k - 1], 'z', [(z, (z + 2 * k) % Z) for z in range(Z)])  11.9 us
    ppermute x1, starting transfers between devices, body(): got = lax.ppermute(far, ('z', 'c'), pairs)  10.7 us
    ppermute x3, waiting for transfers between devices, body(): lax.ppermute(steps[k - 1], 'z', [(z, (z + 2 * k) % Z) for z in range(Z)])  7.71 us
    ppermute x1, waiting for transfers between devices, body(): got = lax.ppermute(far, ('z', 'c'), pairs)  6.56 us
    pallas_call x1, Pallas kernels, partials_call(): pl.pallas_call(partials_kernel, out_shape=(*[jax.ShapeDtypeStruct(UNITS,...  5.94 us
    pallas_call x4, Pallas kernels, call(): pl.pallas_call(kernel, out_shape=tuple((jax.ShapeDtypeStruct(dims, bf) fo...  3.2 us
  transfers between devices with their start and end apart: 7, of which 3 were waited for; matrix products, arithmetic and copies ran while one was open for 0% of the time, Pallas kernels for 2%

profile of v11, /device:TPU:1, one launch (start us, length us, event | category | flops | bytes accessed | tf_op | source)
XLA Modules:
  0.0 120.9 jit_solution(6048106076272157467)
XLA Ops:
  0.6 0.1 pad_add_fusion.where
  0.7 0.8 pad_maximum_fusion
  1.6 28.0 %all_to_all.20 = bf16[8,80,512]{2,1,0:T(8,128)(2,1)S(1)} all-to-all(bf16[8,80,512]{2,1,0:T(8,128)(2,1)S(1)} %broadcast_in_dim.4), channel_id=1, replica_groups={{0,2,4,6,16,18,20,22},{1,3,5,7,17,19,21,23},{8,10,12,14,24,26,28,30},{9..., dimensions={0} | all-to-all | bytes 1310720 | tf_op jit(solution)/shard_map/all_to_all | solution.py:258
  29.6 0.3 broadcast_in_dim.5
  29.9 0.0 copy-start
  29.9 0.0 copy-start.1
  29.9 0.0 copy-start.3
  29.9 21.7 %all_to_all.21.xg_parts = bf16[4,8,80,512]{3,2,1,0:T(8,128)(2,1)S(1)} all-to-all(bf16[4,8,80,512]{3,2,1,0:T(8,128)(2,1)S(1)} %broadcast_in_dim.5), channel_id=1, replica_groups={{0,1,8,9},{2,3,10,11},{4,5,12,13},{6,7,14,15},{16,17,24,25},{18,19,26,2..., dimensions={0} | all-to-all | bytes 5242880 | tf_op jit(solution)/shard_map/all_to_all | solution.py:258
  51.6 5.9 %shard_map.93 = (bf16[5,128,256]{2,1,0:T(8,128)(2,1)S(1)}, bf16[5,128,256]{2,1,0:T(8,128)(2,1)S(1)}, bf16[4,8,80,512]{3,2,1,0:T(8,128)(2,1)}) custom-call(s32[2]{0:T(128)S(1)} %pad_add_fusion.where, s32[2,32]{1,0:T(2,128)S(1)} %bitcast.10, s32[2,32]{1,0:T(2,128)S(1)} %bitcast.12, bf16[4,8,80,512]{3,2,1,0:T(8,128)(2,1)S(1)} %all_to_all.21.xg_parts, ...), custom_call_target="tpu_custom_call" | custom-call | tf_op jit(solution)/shard_map/pallas_call | solution.py:217
  57.5 8.5 %all-to-all-start.2 = ((bf16[4,8,80,512]{3,2,1,0:T(8,128)(2,1)}), bf16[4,8,80,512]{3,2,1,0:T(8,128)(2,1)}, u32[]{:S(2)}, u32[]{:S(2)}) async-start(bf16[4,8,80,512]{3,2,1,0:T(8,128)(2,1)} %get-tuple-element.25), calls=%async_computation.2 | async-start | bytes 5242880 | tf_op jit(solution)/shard_map/all_to_all | solution.py:258
  66.1 2.1 %shard_map.94 = (bf16[8,512,128]{2,1,0:T(8,128)(2,1)S(1)}, bf16[8,512,128]{2,1,0:T(8,128)(2,1)S(1)}) custom-call(s32[2]{0:T(128)S(1)} %pad_add_fusion.where, s32[2,32]{1,0:T(2,128)S(1)} %bitcast.11, s32[2,32]{1,0:T(2,128)S(1)} %bitcast.13, bf16[4,8,80,512]{3,2,1,0:T(8,128)(2,1)S(1)} %all_to_all.21.xg_parts, bf16[5,128,256]{2,1,0:T(8,128)(2,1)S(1)} %get-tuple-element.26.act, ...), custom_call_target="tpu_custom_call" | custom-call | tf_op jit(solution)/shard_map/pallas_call | solution.py:203
  68.1 2.1 %collective-permute-start = (bf16[8,512,128]{2,1,0:T(8,128)(2,1)S(1)}, bf16[8,512,128]{2,1,0:T(8,128)(2,1)S(1)}, u32[]{:S(2)}, u32[]{:S(2)}) collective-permute-start(bf16[8,512,128]{2,1,0:T(8,128)(2,1)S(1)} %get-tuple-element.29), channel_id=1, source_target_pairs={{0,32},{32,0},{1,33},{33,1},{2,34},{34,2},{3,35},{35,3},{4,36},{36... | collective-permute-start | bytes 3145736 | tf_op jit(solution)/shard_map/ppermute | solution.py:280
  70.3 2.4 %collective-permute-done.got = bf16[8,512,128]{2,1,0:T(8,128)(2,1)S(1)} collective-permute-done((bf16[8,512,128]{2,1,0:T(8,128)(2,1)S(1)}, bf16[8,512,128]{2,1,0:T(8,128)(2,1)S(1)}, u32[]{:S(2)}, u32[]{:S(2)}) %collective-permute-start) | collective-permute-done | bytes 1048608 | tf_op jit(solution)/shard_map/ppermute | solution.py:280
  72.7 0.2 shard_map.95
  72.9 10.7 %collective-permute-start.1 = (bf16[4,512,128]{2,1,0:T(8,128)(2,1)S(1)}, bf16[4,512,128]{2,1,0:T(8,128)(2,1)S(1)}, u32[]{:S(2)}, u32[]{:S(2)}) collective-permute-start(bf16[4,512,128]{2,1,0:T(8,128)(2,1)S(1)} %get-tuple-element.30), channel_id=1, source_target_pairs={{0,64},{32,480},{64,0},{96,160},{128,192},{160,96},{192,128},{224,... | collective-permute-start | bytes 1572872 | tf_op jit(solution)/shard_map/ppermute | solution.py:285
  83.6 6.6 %collective-permute-done.1.got = bf16[4,512,128]{2,1,0:T(8,128)(2,1)S(1)} collective-permute-done((bf16[4,512,128]{2,1,0:T(8,128)(2,1)S(1)}, bf16[4,512,128]{2,1,0:T(8,128)(2,1)S(1)}, u32[]{:S(2)}, u32[]{:S(2)}) %collective-permute-start.1) | collective-permute-done | bytes 524320 | tf_op jit(solution)/shard_map/ppermute | solution.py:285
  90.2 2.5 %shard_map.96 = bf16[8,80,512]{2,1,0:T(8,128)(2,1)} custom-call(bf16[4,8,80,512]{3,2,1,0:T(8,128)(2,1)} %all-to-all-done.2.parts), custom_call_target="tpu_custom_call" | custom-call | tf_op jit(solution)/shard_map/pallas_call | solution.py:242
  92.7 7.7 %all-to-all-start.3 = ((bf16[8,80,512]{2,1,0:T(8,128)(2,1)}), bf16[8,80,512]{2,1,0:T(8,128)(2,1)S(1)}, u32[]{:S(2)}, u32[]{:S(2)}) async-start(bf16[8,80,512]{2,1,0:T(8,128)(2,1)} %shard_map.96), calls=%async_computation.3 | async-start | bytes 1310720 | tf_op jit(solution)/shard_map/all_to_all | solution.py:258
  100.3 0.1 shard_map.97
  100.5 1.9 %collective-permute-start.2 = (bf16[512,128]{1,0:T(8,128)(2,1)S(1)}, bf16[512,128]{1,0:T(8,128)(2,1)S(1)}, u32[]{:S(2)}, u32[]{:S(2)}) collective-permute-start(bf16[512,128]{1,0:T(8,128)(2,1)S(1)} %get-tuple-element.35), channel_id=1, source_target_pairs={{0,128},{64,192},{128,256},{192,320},{256,384},{320,448},{384,0},{... | collective-permute-start | bytes 393224 | tf_op jit(solution)/shard_map/ppermute | solution.py:289
  102.4 5.5 %collective-permute-start.3 = (bf16[512,128]{1,0:T(8,128)(2,1)S(1)}, bf16[512,128]{1,0:T(8,128)(2,1)S(1)}, u32[]{:S(2)}, u32[]{:S(2)}) collective-permute-start(bf16[512,128]{1,0:T(8,128)(2,1)S(1)} %get-tuple-element.36), channel_id=1, source_target_pairs={{0,384},{64,448},{128,0},{192,64},{256,128},{320,192},{384,256},{4... | collective-permute-start | bytes 393224 | tf_op jit(solution)/shard_map/ppermute | solution.py:289
  107.9 4.5 %collective-permute-start.4 = (bf16[512,128]{1,0:T(8,128)(2,1)S(1)}, bf16[512,128]{1,0:T(8,128)(2,1)S(1)}, u32[]{:S(2)}, u32[]{:S(2)}) collective-permute-start(bf16[512,128]{1,0:T(8,128)(2,1)S(1)} %get-tuple-element.37), channel_id=1, source_target_pairs={{0,256},{64,320},{128,384},{192,448},{256,0},{320,64},{384,128},{4... | collective-permute-start | bytes 393224 | tf_op jit(solution)/shard_map/ppermute | solution.py:289
  112.5 7.7 %collective-permute-done.4.refs_3_ = bf16[512,128]{1,0:T(8,128)(2,1)S(1)} collective-permute-done((bf16[512,128]{1,0:T(8,128)(2,1)S(1)}, bf16[512,128]{1,0:T(8,128)(2,1)S(1)}, u32[]{:S(2)}, u32[]{:S(2)}) %collective-permute-start.4) | collective-permute-done | bytes 131104 | tf_op jit(solution)/shard_map/ppermute | solution.py:289
  120.2 0.8 shard_map.98
  (10 shorter events, 0.1 us)
Async XLA Ops:
  29.9 21.7 %copy-start = (bf16[32,128,128]{2,1,0:T(8,128)(2,1)S(1)}, bf16[32,128,128]{2,1,0:T(8,128)(2,1)}, u32[]{:S(2)}) copy-start(bf16[32,128,128]{2,1,0:T(8,128)(2,1)} %w_in.1) | copy-start | bytes 3145732
  29.9 21.7 %copy-start.1 = (bf16[32,128,128]{2,1,0:T(8,128)(2,1)S(1)}, bf16[32,128,128]{2,1,0:T(8,128)(2,1)}, u32[]{:S(2)}) copy-start(bf16[32,128,128]{2,1,0:T(8,128)(2,1)} %w_out.1) | copy-start | bytes 3145732
  29.9 21.7 %copy-start.2 = (s32[32,2]{0,1:T(2,128)S(1)}, s32[32,2]{0,1:T(2,128)}, u32[]{:S(2)}) copy-start(s32[32,2]{0,1:T(2,128)} %param.9) | copy-start | bytes 772
  29.9 21.7 %copy-start.3 = (s32[32,2]{0,1:T(2,128)S(1)}, s32[32,2]{0,1:T(2,128)}, u32[]{:S(2)}) copy-start(s32[32,2]{0,1:T(2,128)} %param.11) | copy-start | bytes 772
  57.5 32.6 %all-to-all-start.2 = ((bf16[4,8,80,512]{3,2,1,0:T(8,128)(2,1)}), bf16[4,8,80,512]{3,2,1,0:T(8,128)(2,1)}, u32[]{:S(2)}, u32[]{:S(2)}) async-start(bf16[4,8,80,512]{3,2,1,0:T(8,128)(2,1)} %get-tuple-element.25), calls=%async_computation.2 | async-start | bytes 5242880 | tf_op jit(solution)/shard_map/all_to_all | solution.py:258
  68.1 4.6 %collective-permute-start = (bf16[8,512,128]{2,1,0:T(8,128)(2,1)S(1)}, bf16[8,512,128]{2,1,0:T(8,128)(2,1)S(1)}, u32[]{:S(2)}, u32[]{:S(2)}) collective-permute-start(bf16[8,512,128]{2,1,0:T(8,128)(2,1)S(1)} %get-tuple-element.29), channel_id=1, source_target_pairs={{0,32},{32,0},{1,33},{33,1},{2,34},{34,2},{3,35},{35,3},{4,36},{36... | collective-permute-start | bytes 3145736 | tf_op jit(solution)/shard_map/ppermute | solution.py:280
  72.9 17.2 %collective-permute-start.1 = (bf16[4,512,128]{2,1,0:T(8,128)(2,1)S(1)}, bf16[4,512,128]{2,1,0:T(8,128)(2,1)S(1)}, u32[]{:S(2)}, u32[]{:S(2)}) collective-permute-start(bf16[4,512,128]{2,1,0:T(8,128)(2,1)S(1)} %get-tuple-element.30), channel_id=1, source_target_pairs={{0,64},{32,480},{64,0},{96,160},{128,192},{160,96},{192,128},{224,... | collective-permute-start | bytes 1572872 | tf_op jit(solution)/shard_map/ppermute | solution.py:285
  92.7 27.5 %all-to-all-start.3 = ((bf16[8,80,512]{2,1,0:T(8,128)(2,1)}), bf16[8,80,512]{2,1,0:T(8,128)(2,1)S(1)}, u32[]{:S(2)}, u32[]{:S(2)}) async-start(bf16[8,80,512]{2,1,0:T(8,128)(2,1)} %shard_map.96), calls=%async_computation.3 | async-start | bytes 1310720 | tf_op jit(solution)/shard_map/all_to_all | solution.py:258
  100.5 12.0 %collective-permute-start.2 = (bf16[512,128]{1,0:T(8,128)(2,1)S(1)}, bf16[512,128]{1,0:T(8,128)(2,1)S(1)}, u32[]{:S(2)}, u32[]{:S(2)}) collective-permute-start(bf16[512,128]{1,0:T(8,128)(2,1)S(1)} %get-tuple-element.35), channel_id=1, source_target_pairs={{0,128},{64,192},{128,256},{192,320},{256,384},{320,448},{384,0},{... | collective-permute-start | bytes 393224 | tf_op jit(solution)/shard_map/ppermute | solution.py:289
  102.4 10.0 %collective-permute-start.3 = (bf16[512,128]{1,0:T(8,128)(2,1)S(1)}, bf16[512,128]{1,0:T(8,128)(2,1)S(1)}, u32[]{:S(2)}, u32[]{:S(2)}) collective-permute-start(bf16[512,128]{1,0:T(8,128)(2,1)S(1)} %get-tuple-element.36), channel_id=1, source_target_pairs={{0,384},{64,448},{128,0},{192,64},{256,128},{320,192},{384,256},{4... | collective-permute-start | bytes 393224 | tf_op jit(solution)/shard_map/ppermute | solution.py:289
  107.9 12.3 %collective-permute-start.4 = (bf16[512,128]{1,0:T(8,128)(2,1)S(1)}, bf16[512,128]{1,0:T(8,128)(2,1)S(1)}, u32[]{:S(2)}, u32[]{:S(2)}) collective-permute-start(bf16[512,128]{1,0:T(8,128)(2,1)S(1)} %get-tuple-element.37), channel_id=1, source_target_pairs={{0,256},{64,320},{128,384},{192,448},{256,0},{320,64},{384,128},{4... | collective-permute-start | bytes 393224 | tf_op jit(solution)/shard_map/ppermute | solution.py:289

commit v12 on v10

--- a/solution.py
+++ b/solution.py
@@ -94,28 +94,33 @@
         d_act[row] += dot(w_out[s], xg[pl.ds(col, BLK), T:], ((1,), (0,))) * live
         return carry
 
-    def down(s, carry):
-        row, col, live = place(out_l, s)
-        y[pl.ds(col, BLK), :] += dot(w_out[s], act[row], ((0,), (0,))) * live
-        row, col, live = place(in_l, s)
-        dx[pl.ds(col, BLK), :] += dot(w_in[s], dh[row], ((0,), (0,))) * live
-        return carry
+    def down(lists, weights, units, total):
+        def product(s, carry):
+            row, col, live = place(lists, s)
+            total[pl.ds(col, BLK), :] += dot(weights[s], units[row], ((0,), (0,))) * live
+            return carry
+
+        lax.fori_loop(0, CAP, product, 0, unroll=CAP)
 
     lax.fori_loop(0, CAP, up, 0, unroll=CAP)
     for row in range(ROWS):
         values, slopes = gelu_pair(hidden[row])
         act[row] = values.astype(act.dtype)
         dh[row] = (d_act[row] * slopes).astype(dh.dtype)
-    lax.fori_loop(0, CAP, down, 0, unroll=CAP)
     stage = xg.reshape(NEAR, FAR, OWN, 2 * T)
     copies = []
-    for near in range(NEAR):
-        for far in range(FAR):
-            rows = features(core, near, far)
-            stage[near, far, :, :T] = y[rows, :].astype(stage.dtype)
-            stage[near, far, :, T:] = dx[rows, :].astype(stage.dtype)
-        copies.append(pltpu.make_async_copy(stage.at[near], parts.at[near], sems.at[near]))
-        copies[-1].start()
+    for half, (lists, weights, units, total) in enumerate(
+        ((out_l, w_out, act, y), (in_l, w_in, dh, dx))
+    ):
+        down(lists, weights, units, total)
+        cols = pl.ds(half * T, T)
+        for near in range(NEAR):
+            for far in range(FAR):
+                rows = features(core, near, far)
+                stage[near, far, :, cols] = total[rows, :].astype(stage.dtype)
+            source, target = stage.at[near, :, :, cols], parts.at[near, :, :, cols]
+            copies.append(pltpu.make_async_copy(source, target, sems.at[half, near]))
+            copies[-1].start()
     for copy in copies:
         copy.wait()
 
@@ -223,7 +228,7 @@
             pltpu.VMEM((FEAT, 2 * T), bf),
             *[pltpu.VMEM(UNITS, f32)] * 2,
             *[pltpu.VMEM((FEAT, T), f32)] * 2,
-            pltpu.SemaphoreType.DMA((NEAR,)),
+            pltpu.SemaphoreType.DMA((2, NEAR)),
         ],
         compiler_params=LIMIT,
         interpret=INTERPRET,

time: 120 us -> 120 us (level)
  no operation moved by 1% of the time
where the time goes in v12:
time: 120 us
  blocking collectives  49.7 us (41%)
  starting transfers between devices  40.9 us (34%)
  waiting for transfers between devices  15.4 us (13%)
  Pallas kernels  11.7 us (10%)
    all_to_all x2, blocking collectives, exchange(): lax.all_to_all(x, ('c', 'x', 'y'), split_axis=0, concat_axis=0, axis_inde...  49.7 us
    all_to_all x2, starting transfers between devices, exchange(): lax.all_to_all(x, ('c', 'x', 'y'), split_axis=0, concat_axis=0, axis_inde...  16.2 us
    ppermute x3, starting transfers between devices, body(): lax.ppermute(steps[k - 1], 'z', [(z, (z + 2 * k) % Z) for z in range(Z)])  11.9 us
    ppermute x1, starting transfers between devices, body(): got = lax.ppermute(far, ('z', 'c'), pairs)  10.7 us
    ppermute x1, waiting for transfers between devices, body(): got = lax.ppermute(far, ('z', 'c'), pairs)  6.56 us
    ppermute x3, waiting for transfers between devices, body(): lax.ppermute(steps[k - 1], 'z', [(z, (z + 2 * k) % Z) for z in range(Z)])  6.43 us
    pallas_call x1, Pallas kernels, partials_call(): pl.pallas_call(partials_kernel, out_shape=(*[jax.ShapeDtypeStruct(UNITS,...  5.99 us
    pallas_call x4, Pallas kernels, call(): pl.pallas_call(kernel, out_shape=tuple((jax.ShapeDtypeStruct(dims, bf) fo...  3.2 us
  transfers between devices with their start and end apart: 7, of which 4 were waited for; matrix products, arithmetic and copies ran while one was open for 0% of the time, Pallas kernels for 2%

profile of v12, /device:TPU:1, one launch (start us, length us, event | category | flops | bytes accessed | tf_op | source)
XLA Modules:
  0.0 119.7 jit_solution(11029455781985036603)
XLA Ops:
  0.6 0.1 pad_add_fusion.where
  0.7 0.8 pad_maximum_fusion
  1.6 28.0 %all_to_all.20 = bf16[8,80,512]{2,1,0:T(8,128)(2,1)S(1)} all-to-all(bf16[8,80,512]{2,1,0:T(8,128)(2,1)S(1)} %broadcast_in_dim.4), channel_id=1, replica_groups={{0,2,4,6,16,18,20,22},{1,3,5,7,17,19,21,23},{8,10,12,14,24,26,28,30},{9..., dimensions={0} | all-to-all | bytes 1310720 | tf_op jit(solution)/shard_map/all_to_all | solution.py:263
  29.6 0.3 broadcast_in_dim.5
  29.9 0.0 copy-start
  29.9 0.0 copy-start.1
  29.9 21.7 %all_to_all.21.xg_parts = bf16[4,8,80,512]{3,2,1,0:T(8,128)(2,1)S(1)} all-to-all(bf16[4,8,80,512]{3,2,1,0:T(8,128)(2,1)S(1)} %broadcast_in_dim.5), channel_id=1, replica_groups={{0,1,8,9},{2,3,10,11},{4,5,12,13},{6,7,14,15},{16,17,24,25},{18,19,26,2..., dimensions={0} | all-to-all | bytes 5242880 | tf_op jit(solution)/shard_map/all_to_all | solution.py:263
  51.6 6.0 %shard_map.93 = (bf16[5,128,256]{2,1,0:T(8,128)(2,1)S(1)}, bf16[5,128,256]{2,1,0:T(8,128)(2,1)S(1)}, bf16[4,8,80,512]{3,2,1,0:T(8,128)(2,1)}) custom-call(s32[2]{0:T(128)S(1)} %pad_add_fusion.where, s32[2,32]{1,0:T(2,128)S(1)} %bitcast.10, s32[2,32]{1,0:T(2,128)S(1)} %bitcast.12, bf16[4,8,80,512]{3,2,1,0:T(8,128)(2,1)S(1)} %all_to_all.21.xg_parts, ...), custom_call_target="tpu_custom_call" | custom-call | tf_op jit(solution)/shard_map/pallas_call | solution.py:222
  57.6 8.5 %all-to-all-start.2 = ((bf16[4,8,80,512]{3,2,1,0:T(8,128)(2,1)}), bf16[4,8,80,512]{3,2,1,0:T(8,128)(2,1)}, u32[]{:S(2)}, u32[]{:S(2)}) async-start(bf16[4,8,80,512]{3,2,1,0:T(8,128)(2,1)} %get-tuple-element.25), calls=%async_computation.2 | async-start | bytes 5242880 | tf_op jit(solution)/shard_map/all_to_all | solution.py:263
  66.1 2.1 %shard_map.94 = (bf16[8,512,128]{2,1,0:T(8,128)(2,1)S(1)}, bf16[8,512,128]{2,1,0:T(8,128)(2,1)S(1)}) custom-call(s32[2]{0:T(128)S(1)} %pad_add_fusion.where, s32[2,32]{1,0:T(2,128)S(1)} %bitcast.11, s32[2,32]{1,0:T(2,128)S(1)} %bitcast.13, bf16[4,8,80,512]{3,2,1,0:T(8,128)(2,1)S(1)} %all_to_all.21.xg_parts, bf16[5,128,256]{2,1,0:T(8,128)(2,1)S(1)} %get-tuple-element.26.act, ...), custom_call_target="tpu_custom_call" | custom-call | tf_op jit(solution)/shard_map/pallas_call | solution.py:208
  68.2 2.1 %collective-permute-start = (bf16[8,512,128]{2,1,0:T(8,128)(2,1)S(1)}, bf16[8,512,128]{2,1,0:T(8,128)(2,1)S(1)}, u32[]{:S(2)}, u32[]{:S(2)}) collective-permute-start(bf16[8,512,128]{2,1,0:T(8,128)(2,1)S(1)} %get-tuple-element.29), channel_id=1, source_target_pairs={{0,32},{32,0},{1,33},{33,1},{2,34},{34,2},{3,35},{35,3},{4,36},{36... | collective-permute-start | bytes 3145736 | tf_op jit(solution)/shard_map/ppermute | solution.py:285
  70.3 2.4 %collective-permute-done.got = bf16[8,512,128]{2,1,0:T(8,128)(2,1)S(1)} collective-permute-done((bf16[8,512,128]{2,1,0:T(8,128)(2,1)S(1)}, bf16[8,512,128]{2,1,0:T(8,128)(2,1)S(1)}, u32[]{:S(2)}, u32[]{:S(2)}) %collective-permute-start) | collective-permute-done | bytes 1048608 | tf_op jit(solution)/shard_map/ppermute | solution.py:285
  72.8 0.2 shard_map.95
  73.0 10.7 %collective-permute-start.1 = (bf16[4,512,128]{2,1,0:T(8,128)(2,1)S(1)}, bf16[4,512,128]{2,1,0:T(8,128)(2,1)S(1)}, u32[]{:S(2)}, u32[]{:S(2)}) collective-permute-start(bf16[4,512,128]{2,1,0:T(8,128)(2,1)S(1)} %get-tuple-element.30), channel_id=1, source_target_pairs={{0,64},{32,480},{64,0},{96,160},{128,192},{160,96},{192,128},{224,... | collective-permute-start | bytes 1572872 | tf_op jit(solution)/shard_map/ppermute | solution.py:290
  83.7 6.6 %collective-permute-done.1.got = bf16[4,512,128]{2,1,0:T(8,128)(2,1)S(1)} collective-permute-done((bf16[4,512,128]{2,1,0:T(8,128)(2,1)S(1)}, bf16[4,512,128]{2,1,0:T(8,128)(2,1)S(1)}, u32[]{:S(2)}, u32[]{:S(2)}) %collective-permute-start.1) | collective-permute-done | bytes 524320 | tf_op jit(solution)/shard_map/ppermute | solution.py:290
  90.2 2.5 %shard_map.96 = bf16[8,80,512]{2,1,0:T(8,128)(2,1)} custom-call(bf16[4,8,80,512]{3,2,1,0:T(8,128)(2,1)} %all-to-all-done.2.parts), custom_call_target="tpu_custom_call" | custom-call | tf_op jit(solution)/shard_map/pallas_call | solution.py:247
  92.7 7.7 %all-to-all-start.3 = ((bf16[8,80,512]{2,1,0:T(8,128)(2,1)}), bf16[8,80,512]{2,1,0:T(8,128)(2,1)S(1)}, u32[]{:S(2)}, u32[]{:S(2)}) async-start(bf16[8,80,512]{2,1,0:T(8,128)(2,1)} %shard_map.96), calls=%async_computation.3 | async-start | bytes 1310720 | tf_op jit(solution)/shard_map/all_to_all | solution.py:263
  100.4 0.1 shard_map.97
  100.5 4.5 %collective-permute-start.2 = (bf16[512,128]{1,0:T(8,128)(2,1)S(1)}, bf16[512,128]{1,0:T(8,128)(2,1)S(1)}, u32[]{:S(2)}, u32[]{:S(2)}) collective-permute-start(bf16[512,128]{1,0:T(8,128)(2,1)S(1)} %get-tuple-element.35), channel_id=1, source_target_pairs={{0,256},{64,320},{128,384},{192,448},{256,0},{320,64},{384,128},{4... | collective-permute-start | bytes 393224 | tf_op jit(solution)/shard_map/ppermute | solution.py:294
  105.1 3.1 %collective-permute-start.3 = (bf16[512,128]{1,0:T(8,128)(2,1)S(1)}, bf16[512,128]{1,0:T(8,128)(2,1)S(1)}, u32[]{:S(2)}, u32[]{:S(2)}) collective-permute-start(bf16[512,128]{1,0:T(8,128)(2,1)S(1)} %get-tuple-element.36), channel_id=1, source_target_pairs={{0,128},{64,192},{128,256},{192,320},{256,384},{320,448},{384,0},{... | collective-permute-start | bytes 393224 | tf_op jit(solution)/shard_map/ppermute | solution.py:294
  108.2 4.3 %collective-permute-start.4 = (bf16[512,128]{1,0:T(8,128)(2,1)S(1)}, bf16[512,128]{1,0:T(8,128)(2,1)S(1)}, u32[]{:S(2)}, u32[]{:S(2)}) collective-permute-start(bf16[512,128]{1,0:T(8,128)(2,1)S(1)} %get-tuple-element.37), channel_id=1, source_target_pairs={{0,384},{64,448},{128,0},{192,64},{256,128},{320,192},{384,256},{4... | collective-permute-start | bytes 393224 | tf_op jit(solution)/shard_map/ppermute | solution.py:294
  112.5 1.6 %collective-permute-done.2.refs_1_ = bf16[512,128]{1,0:T(8,128)(2,1)S(1)} collective-permute-done((bf16[512,128]{1,0:T(8,128)(2,1)S(1)}, bf16[512,128]{1,0:T(8,128)(2,1)S(1)}, u32[]{:S(2)}, u32[]{:S(2)}) %collective-permute-start.2) | collective-permute-done | bytes 131104 | tf_op jit(solution)/shard_map/ppermute | solution.py:294
  114.1 4.9 %collective-permute-done.4.refs_3_ = bf16[512,128]{1,0:T(8,128)(2,1)S(1)} collective-permute-done((bf16[512,128]{1,0:T(8,128)(2,1)S(1)}, bf16[512,128]{1,0:T(8,128)(2,1)S(1)}, u32[]{:S(2)}, u32[]{:S(2)}) %collective-permute-start.4) | collective-permute-done | bytes 131104 | tf_op jit(solution)/shard_map/ppermute | solution.py:294
  118.9 0.8 shard_map.98
  (10 shorter events, 0.1 us)
Async XLA Ops:
  29.9 21.7 %copy-start = (bf16[32,128,128]{2,1,0:T(8,128)(2,1)S(1)}, bf16[32,128,128]{2,1,0:T(8,128)(2,1)}, u32[]{:S(2)}) copy-start(bf16[32,128,128]{2,1,0:T(8,128)(2,1)} %w_in.1) | copy-start | bytes 3145732
  29.9 21.7 %copy-start.1 = (bf16[32,128,128]{2,1,0:T(8,128)(2,1)S(1)}, bf16[32,128,128]{2,1,0:T(8,128)(2,1)}, u32[]{:S(2)}) copy-start(bf16[32,128,128]{2,1,0:T(8,128)(2,1)} %w_out.1) | copy-start | bytes 3145732
  29.9 21.7 %copy-start.2 = (s32[32,2]{0,1:T(2,128)S(1)}, s32[32,2]{0,1:T(2,128)}, u32[]{:S(2)}) copy-start(s32[32,2]{0,1:T(2,128)} %param.9) | copy-start | bytes 772
  29.9 21.7 %copy-start.3 = (s32[32,2]{0,1:T(2,128)S(1)}, s32[32,2]{0,1:T(2,128)}, u32[]{:S(2)}) copy-start(s32[32,2]{0,1:T(2,128)} %param.11) | copy-start | bytes 772
  57.6 32.6 %all-to-all-start.2 = ((bf16[4,8,80,512]{3,2,1,0:T(8,128)(2,1)}), bf16[4,8,80,512]{3,2,1,0:T(8,128)(2,1)}, u32[]{:S(2)}, u32[]{:S(2)}) async-start(bf16[4,8,80,512]{3,2,1,0:T(8,128)(2,1)} %get-tuple-element.25), calls=%async_computation.2 | async-start | bytes 5242880 | tf_op jit(solution)/shard_map/all_to_all | solution.py:263
  68.2 4.6 %collective-permute-start = (bf16[8,512,128]{2,1,0:T(8,128)(2,1)S(1)}, bf16[8,512,128]{2,1,0:T(8,128)(2,1)S(1)}, u32[]{:S(2)}, u32[]{:S(2)}) collective-permute-start(bf16[8,512,128]{2,1,0:T(8,128)(2,1)S(1)} %get-tuple-element.29), channel_id=1, source_target_pairs={{0,32},{32,0},{1,33},{33,1},{2,34},{34,2},{3,35},{35,3},{4,36},{36... | collective-permute-start | bytes 3145736 | tf_op jit(solution)/shard_map/ppermute | solution.py:285
  73.0 17.2 %collective-permute-start.1 = (bf16[4,512,128]{2,1,0:T(8,128)(2,1)S(1)}, bf16[4,512,128]{2,1,0:T(8,128)(2,1)S(1)}, u32[]{:S(2)}, u32[]{:S(2)}) collective-permute-start(bf16[4,512,128]{2,1,0:T(8,128)(2,1)S(1)} %get-tuple-element.30), channel_id=1, source_target_pairs={{0,64},{32,480},{64,0},{96,160},{128,192},{160,96},{192,128},{224,... | collective-permute-start | bytes 1572872 | tf_op jit(solution)/shard_map/ppermute | solution.py:290
  92.7 26.2 %all-to-all-start.3 = ((bf16[8,80,512]{2,1,0:T(8,128)(2,1)}), bf16[8,80,512]{2,1,0:T(8,128)(2,1)S(1)}, u32[]{:S(2)}, u32[]{:S(2)}) async-start(bf16[8,80,512]{2,1,0:T(8,128)(2,1)} %shard_map.96), calls=%async_computation.3 | async-start | bytes 1310720 | tf_op jit(solution)/shard_map/all_to_all | solution.py:263
  100.5 13.5 %collective-permute-start.2 = (bf16[512,128]{1,0:T(8,128)(2,1)S(1)}, bf16[512,128]{1,0:T(8,128)(2,1)S(1)}, u32[]{:S(2)}, u32[]{:S(2)}) collective-permute-start(bf16[512,128]{1,0:T(8,128)(2,1)S(1)} %get-tuple-element.35), channel_id=1, source_target_pairs={{0,256},{64,320},{128,384},{192,448},{256,0},{320,64},{384,128},{4... | collective-permute-start | bytes 393224 | tf_op jit(solution)/shard_map/ppermute | solution.py:294
  105.1 9.0 %collective-permute-start.3 = (bf16[512,128]{1,0:T(8,128)(2,1)S(1)}, bf16[512,128]{1,0:T(8,128)(2,1)S(1)}, u32[]{:S(2)}, u32[]{:S(2)}) collective-permute-start(bf16[512,128]{1,0:T(8,128)(2,1)S(1)} %get-tuple-element.36), channel_id=1, source_target_pairs={{0,128},{64,192},{128,256},{192,320},{256,384},{320,448},{384,0},{... | collective-permute-start | bytes 393224 | tf_op jit(solution)/shard_map/ppermute | solution.py:294
  108.2 10.7 %collective-permute-start.4 = (bf16[512,128]{1,0:T(8,128)(2,1)S(1)}, bf16[512,128]{1,0:T(8,128)(2,1)S(1)}, u32[]{:S(2)}, u32[]{:S(2)}) collective-permute-start(bf16[512,128]{1,0:T(8,128)(2,1)S(1)} %get-tuple-element.37), channel_id=1, source_target_pairs={{0,384},{64,448},{128,0},{192,64},{256,128},{320,192},{384,256},{4... | collective-permute-start | bytes 393224 | tf_op jit(solution)/shard_map/ppermute | solution.py:294
